TPU v7x, 128 devices: a whole 4x4x4 slice. The times are simulated.
128 devices in a mesh: blk: 64 (over x, z, y), rep: 2 (over core).
Axes of the slice: x: 4, y: 4, z: 4, core: 2. Of those that a mesh axis runs over, the one named last changes fastest.
Arguments:
- sky_map: float32 [2048, 32768], P('blk', 'rep'), may hold values from -6 to 6
- noise_weight: float32 [2048, 32768], P('blk', 'rep'), may hold values from 0.25 to 4
- prior_weight: float32 [512, 4, 2, 128], P('blk', 'rep'), may hold values from 0.5 to 4
- seeds: float32 [512, 4, 2, 2048], P('blk', 'rep'), may hold values from -5 to 5
- loop_cos: float32 [2048], replicated, may hold values from -0.3 to 0.3
- pair_m: int32 [512, 2], replicated, may hold values from 1 to 14939
- block_count: int32 [512], P('blk'), may hold values from 1 to 3, as said below
Outputs:
- solution: float32 [512, 4, 2, 128], P('blk', 'rep')
- residual: float32 [512, 4, 2, 128], P('blk', 'rep')
Inputs may be any that keep to these rules, and one draw needn't show every extreme that they name: `pair_m`: each pair holds two m-columns; values may repeat between pairs. Pair p's first block_count[p] l-blocks belong to its first column, the other 4 - block_count[p] to its second.
All inputs are finite; a program needn't handle non-finite values.
Results may differ from a plain program's by a relative error of at most 0.00045.
Values sent between devices are 32-bit elements; how exact they have to be, the bound alone decides.
No kernel may reach another device: no remote copies, remote signals or barrier semaphores. Data moves between devices by JAX's collectives and lax.ppermute only.
A program may use at most 128 MiB of HBM per device.

v0:
```python
import math

import jax
import jax.numpy as jnp
from jax import lax
from jax.sharding import PartitionSpec as P

ITERS = 2


EXACT = lax.Precision.HIGHEST


def block_layout(pair_m, block_count, block_ids):
    block_side = (block_ids[None, :] >= block_count[:, None]).astype(jnp.int32)
    offset = jnp.where(
        block_side == 0, block_ids[None, :], block_ids[None, :] - block_count[:, None]
    )
    column_m = jnp.where(block_side == 0, pair_m[:, 0:1], pair_m[:, 1:2])
    block_start = 128 * (17 * column_m // 2048 + 1) + 128 * offset
    return (block_side, column_m, block_start)


def ladder(degree, column_m):
    degree_f = degree.astype(jnp.float32)
    m_over_l = column_m.astype(jnp.float32) / degree_f
    return jnp.sqrt((4.0 - 1.0 / (degree_f * degree_f)) / ((1.0 - m_over_l) * (1.0 + m_over_l)))


def legendre_rows(column_m, block_start, seeds, loop_cos, visit, initial):
    carried, first_out = visit(initial, seeds[:, 0], 0)
    carried, second_out = visit(carried, seeds[:, 1], 1)

    def advance(packed, step_id):
        earlier, latest, totals = packed
        degree = block_start + step_id
        coef_now = ladder(degree, column_m)[:, None]
        coef_prev = ladder(degree - 1, column_m)[:, None]
        current = coef_now * (loop_cos[None, :] * latest - earlier / coef_prev)
        totals, emitted = visit(totals, current, step_id)
        return ((latest, current, totals), emitted)

    (_, _, carried), others = lax.scan(
        advance, (seeds[:, 0], seeds[:, 1], carried), jnp.arange(2, 128, dtype=jnp.int32), unroll=8
    )
    return (carried, first_out, second_out, others)


def sum_columns(coef, block_side, column_m, block_start, seeds, loop_cos):
    pair_total, block_total = block_side.shape
    count_all = pair_total * block_total
    loop_total = loop_cos.shape[0]
    flat_coef = coef.reshape(count_all, 2, 128)

    def visit(totals, current, step_id):
        weight = lax.dynamic_index_in_dim(flat_coef, step_id, 2, keepdims=False)
        return (totals + weight[:, :, None] * current[:, None, :], None)

    totals, _, _, _ = legendre_rows(
        column_m.reshape(count_all),
        block_start.reshape(count_all),
        seeds.reshape(count_all, 2, loop_total),
        loop_cos,
        visit,
        jnp.zeros((count_all, 2, loop_total), jnp.float32),
    )
    member = (block_side[:, :, None] == jnp.arange(2, dtype=jnp.int32)[None, None, :]).astype(
        jnp.float32
    )
    summed = jnp.einsum(
        "pbs,pbtr->tpsr",
        member,
        totals.reshape(pair_total, block_total, 2, loop_total),
        precision=EXACT,
    )
    return summed.reshape(2, 2 * pair_total, loop_total)


def spread_columns(spectra, block_side, column_m, block_start, seeds, loop_cos):
    pair_total, block_total = block_side.shape
    count_all = pair_total * block_total
    loop_total = loop_cos.shape[0]
    by_side = spectra.reshape(2, pair_total, 2, loop_total)
    side_zero = jnp.transpose(by_side[:, :, 0], (1, 0, 2))[:, None]
    side_one = jnp.transpose(by_side[:, :, 1], (1, 0, 2))[:, None]
    chosen = jnp.where(block_side[:, :, None, None] == 0, side_zero, side_one)
    flat_spec = chosen.reshape(count_all, 2, loop_total)

    def visit(carried, current, step_id):
        return (carried, jnp.sum(current[:, None, :] * flat_spec, axis=2))

    _, first_out, second_out, others = legendre_rows(
        column_m.reshape(count_all),
        block_start.reshape(count_all),
        seeds.reshape(count_all, 2, loop_total),
        loop_cos,
        visit,
        jnp.zeros((), jnp.float32),
    )
    stacked = jnp.concatenate([first_out[None], second_out[None], others], axis=0)
    return jnp.transpose(stacked, (1, 2, 0)).reshape(pair_total, block_total, 2, 128)


def phase_table(every_m, positions, period):
    cycles = positions[:, None] * every_m[None, :] % period
    angles = cycles.astype(jnp.float32) * (2.0 * math.pi / period)
    return (jnp.cos(angles), jnp.sin(angles))


def shards(sky_map, noise_weight, prior_weight, seeds, loop_cos, pair_m, block_count):
    pairs_dev = block_count.shape[0]
    half_blocks = seeds.shape[1]
    loop_total = loop_cos.shape[0]
    columns = 2 * pair_m.shape[0]
    period = sky_map.shape[1] * lax.axis_size("rep")
    map_scale = 1.0 / math.sqrt(loop_total * period)
    rep_index = lax.axis_index("rep")
    local_m = lax.dynamic_slice_in_dim(pair_m, lax.axis_index("blk") * pairs_dev, pairs_dev, 0)
    block_ids = rep_index * half_blocks + jnp.arange(half_blocks, dtype=jnp.int32)
    block_side, column_m, block_start = block_layout(local_m, block_count, block_ids)
    every_m = pair_m.reshape(columns)
    sky_here, noise_here = (sky_map, noise_weight)
    phase_base = rep_index * sky_map.shape[1]
    loop_here, pixel_width = sky_here.shape
    inner_len = min(1024, pixel_width)
    outer_len = pixel_width // inner_len
    cos_inner, sin_inner = phase_table(every_m, jnp.arange(inner_len, dtype=jnp.int32), period)
    basis = jnp.concatenate([cos_inner, sin_inner], axis=1)
    cos_outer, sin_outer = phase_table(
        every_m, phase_base + inner_len * jnp.arange(outer_len, dtype=jnp.int32), period
    )

    def forward(pixels):
        sectioned = jnp.dot(
            pixels.reshape(loop_here * outer_len, inner_len), basis, precision=EXACT
        )
        sectioned = sectioned.reshape(loop_here, outer_len, 2, columns)
        cos_sums, sin_sums = (sectioned[:, :, 0], sectioned[:, :, 1])
        real_part = jnp.einsum("rjm,jm->mr", cos_sums, cos_outer, precision=EXACT) - jnp.einsum(
            "rjm,jm->mr", sin_sums, sin_outer, precision=EXACT
        )
        imag_part = -(
            jnp.einsum("rjm,jm->mr", sin_sums, cos_outer, precision=EXACT)
            + jnp.einsum("rjm,jm->mr", cos_sums, sin_outer, precision=EXACT)
        )
        return map_scale * jnp.stack([real_part, imag_part])

    def analyze(pixels):
        partial_spec = forward(pixels)
        ready = lax.psum(partial_spec, "rep")
        by_column = lax.all_to_all(ready, "blk", split_axis=1, concat_axis=2, tiled=True)
        return spread_columns(by_column, block_side, column_m, block_start, seeds, loop_cos)

    def squares(vector):
        return lax.psum(jnp.sum(vector * vector), ("blk", "rep"))

    rhs_coef = analyze(noise_here * sky_here)
    solution = jnp.zeros_like(rhs_coef)
    residual = rhs_coef
    direction = rhs_coef
    norm_now = squares(residual)
    for turn_id in range(ITERS):
        column_spec = sum_columns(direction, block_side, column_m, block_start, seeds, loop_cos)
        column_spec = lax.psum(column_spec, "rep")
        by_loop = lax.all_to_all(column_spec, "blk", split_axis=2, concat_axis=1, tiled=True)
        spec_re = jnp.transpose(by_loop[0])[:, None, :]
        spec_im = jnp.transpose(by_loop[1])[:, None, :]
        mixed_one = spec_re * cos_outer[None] - spec_im * sin_outer[None]
        mixed_two = spec_re * sin_outer[None] + spec_im * cos_outer[None]
        stacked = jnp.concatenate([mixed_one, -mixed_two], axis=2).reshape(
            loop_here * outer_len, 2 * columns
        )
        inverse_pixels = jnp.einsum("km,jm->kj", stacked, basis, precision=EXACT)
        applied = prior_weight * direction + analyze(
            noise_here * (map_scale * inverse_pixels.reshape(loop_here, pixel_width))
        )
        step_len = norm_now / lax.psum(jnp.sum(direction * applied), ("blk", "rep"))
        solution = solution + step_len * direction
        residual = residual - step_len * applied
        norm_next = squares(residual)
        direction = residual + norm_next / norm_now * direction
        norm_now = norm_next
    return (solution, residual)


def solution(mesh):
    placed = (
        P("blk", "rep"),
        P("blk", "rep"),
        P("blk", "rep", None, None),
        P("blk", "rep", None, None),
        P(),
        P(),
        P("blk"),
    )
    return jax.shard_map(
        shards,
        mesh=mesh,
        in_specs=placed,
        out_specs=(P("blk", "rep", None, None), P("blk", "rep", None, None)),
        check_vma=False,
    )
```

profile of v0, /device:TPU:1, one launch (start us, length us, event | category | flops | bytes accessed | tf_op | source)
XLA Modules:
  0.0 2224.2 jit_solution(317752087883285091)
XLA Ops:
  8.2 18.8 fusion.158
  35.4 14.0 fusion.155
  62.4 17.4 all-reduce.7.cloned.1.call-done
  82.9 10.1 all-to-all-start
  93.1 10.4 all-reduce.9.cloned.1.call-start
  120.2 5.1 fusion.210
  135.6 244.1 %while.95 = (s32[]{:T(128)}, f32[16,2048]{1,0:T(8,128)S(1)}, f32[16,2048]{1,0:T(8,128)}, f32[15,8,16,2]{2,3,1,0:T(2,128)}, s32[15,8]{0,1:T(8,128)S(1)}, /*index=...) while((s32[]{:T(128)}, f32[16,2048]{1,0:T(8,128)S(1)}, ...), condition=%wide.region_12.13_spmd.clone.clone, body=%wide.region_3.12_spmd.clone.clone.sunk | while | flops 2165490 | bytes 4757069 | solution.py:43
  140.1 5.1 fusion.266
  156.4 5.1 fusion.266
  189.0 5.1 fusion.266
  205.2 5.1 fusion.266
  221.5 5.1 fusion.266
  237.8 5.1 fusion.266
  254.1 5.1 fusion.266
  404.4 431.2 %while.96 = (s32[]{:T(128)}, f32[16,2048]{1,0:T(8,128)S(1)}, f32[16,2048]{1,0:T(8,128)S(1)}, f32[16,2,2048]{2,1,0:T(2,128)}, s32[15,8]{0,1:T(8,128)S(1)}, /*inde...) while((s32[]{:T(128)}, f32[16,2048]{1,0:T(8,128)S(1)}, ...), condition=%wide.region_22.23_spmd.clone.clone, body=%wide.region_21.22_spmd.clone.clone.sunk | while | flops 2100234 | bytes 2901229 | solution.py:43
  408.9 5.1 fusion.269
  437.7 5.1 fusion.269
  466.4 5.1 fusion.269
  495.1 5.1 fusion.269
  523.9 5.1 fusion.269
  552.6 5.1 fusion.269
  581.4 5.1 fusion.269
  610.1 5.1 fusion.269
  638.9 5.1 fusion.269
  667.6 5.1 fusion.269
  696.4 5.1 fusion.269
  725.1 5.1 fusion.269
  753.8 5.1 fusion.269
  782.6 5.1 fusion.269
  811.3 5.1 fusion.269
  840.9 25.5 %all-reduce.9.cloned.1.call-done = f32[2,16,2048]{2,0,1:T(2,128)} async-done(((f32[2,16,2048]{2,0,1:T(2,128)}), f32[2,16,2048]{2,0,1:T(2,128)}) %all-reduce.9.cloned.1.call-update) | async-done | bytes 262160 | tf_op jit(solution)/shard_map/psum | solution.py:164
  874.6 20.1 all_to_all.75
  907.9 16.3 fusion.162
  930.0 16.5 fusion.153
  949.2 21.3 all-reduce.11.cloned.1.call-done
  973.6 10.1 all-to-all-start.2
  984.7 8.9 all-to-all-done.2
  1003.3 228.7 %while.97 = (s32[]{:T(128)}, f32[16,2048]{1,0:T(8,128)S(1)}, f32[16,2048]{1,0:T(8,128)S(1)}, f32[15,8,16,2]{2,3,1,0:T(2,128)}, s32[15,8]{0,1:T(8,128)S(1)}, /*in...) while((s32[]{:T(128)}, f32[16,2048]{1,0:T(8,128)S(1)}, ...), condition=%wide.region_36.37_spmd.clone.clone, body=%wide.region_27.36_spmd.clone.clone.sunk | while | flops 2165490 | bytes 4757069 | solution.py:43
  1248.4 63.3 %all-reduce = (f32[]{:T(128)}, f32[]{:T(128)}) all-reduce(f32[]{:T(128)} %multiply_reduce_fusion.39, f32[]{:T(128)} %multiply_reduce_fusion.38), channel_id=1, replica_groups=mesh['blk'=64,'rep'=2] {'blk','rep'}, use_global_device_ids=true, to_apply=%region_20.21 | all-reduce | flops 2 | bytes 16 | tf_op jit(solution)/shard_map/psum | solution.py:155
  1313.7 62.9 %psum.68 = f32[]{:T(128)} all-reduce(f32[]{:T(128)} %multiply_reduce_fusion.37), channel_id=1, replica_groups=mesh['blk'=64,'rep'=2] {'blk','rep'}, use_global_device_ids=true, to_apply=%region_46.47 | all-reduce | flops 1 | bytes 8 | tf_op jit(solution)/shard_map/psum | solution.py:155
  1381.1 440.8 %while.98 = (s32[]{:T(128)}, f32[16,2048]{1,0:T(8,128)S(1)}, f32[16,2048]{1,0:T(8,128)S(1)}, f32[16,2,2048]{2,1,0:T(2,128)}, s32[15,8]{0,1:T(8,128)S(1)}, /*inde...) while((s32[]{:T(128)}, f32[16,2048]{1,0:T(8,128)S(1)}, ...), condition=%wide.region_48.49_spmd.clone.clone, body=%wide.region_47.48_spmd.clone.clone.sunk | while | flops 2100234 | bytes 2901229 | solution.py:43
  1830.5 21.4 all-reduce.13.cloned.1.call-done
  1860.0 19.9 all_to_all.76
  1893.2 16.3 fusion.159
  1915.3 16.5 fusion.151
  1934.5 21.3 all-reduce.15.cloned.1.call-done
  1958.2 20.0 all_to_all.77
  1981.8 165.4 %while.99 = (s32[]{:T(128)}, f32[16,2048]{1,0:T(8,128)S(1)}, f32[16,2048]{1,0:T(8,128)S(1)}, f32[15,8,16,2]{2,3,1,0:T(2,128)S(1)}, s32[15,8]{0,1:T(8,128)S(1)}, ...) while((s32[]{:T(128)}, f32[16,2048]{1,0:T(8,128)S(1)}, ...), condition=%wide.region_62.63_spmd.clone.clone, body=%wide.region_53.62_spmd.clone.clone.sunk | while | flops 2165490 | bytes 4763729 | solution.py:43
  1986.4 5.1 fusion.280
  1997.4 5.1 fusion.280
  2008.5 5.1 fusion.280
  2019.5 5.1 fusion.280
  2030.5 5.1 fusion.280
  2041.5 5.1 fusion.280
  2052.6 5.1 fusion.280
  2063.6 5.1 fusion.280
  2074.6 5.1 fusion.280
  2085.6 5.1 fusion.280
  2096.7 5.1 fusion.280
  2107.7 5.1 fusion.280
  2118.7 5.1 fusion.280
  2129.7 5.1 fusion.280
  2140.8 5.1 fusion.280
  2152.0 63.3 %psum.71 = f32[]{:T(128)} all-reduce(f32[]{:T(128)} %multiply_reduce_fusion.36), channel_id=1, replica_groups=mesh['blk'=64,'rep'=2] {'blk','rep'}, use_global_device_ids=true, to_apply=%region_70.71 | all-reduce | flops 1 | bytes 8 | tf_op jit(solution)/shard_map/psum | solution.py:177
  (2377 shorter events, 1052.7 us)
Async XLA Ops:
  7.2 72.6 %all-reduce.7.cloned.1.call-start = ((), (), s32[]{:S(2)}) async-start(), calls=%async_computation.5 | async-start | bytes 524288 | tf_op jit(solution)/shard_map/psum | solution.py:150
  8.2 18.8 copy-start
  8.2 18.8 copy-start.9
  30.9 18.5 copy-start.17
  30.9 18.5 copy-start.20
  30.9 4.5 copy-start.16
  35.3 14.1 copy-start.3
  49.4 7.5 copy-start.30
  61.0 42.5 %copy-start.49 = (s32[16]{0:T(128)S(1)}, s32[16]{0:T(128)}, u32[]{:S(2)}) copy-start(s32[16]{0:T(128)} %ge.98) | copy-start | bytes 196
  82.9 42.3 %all-to-all-start = ((f32[64,1,1024]{2,1,0:T(1,128)}), f32[64,1,1024]{2,1,0:T(1,128)S(1)}, u32[]{:S(2)}, u32[]{:S(2)}) async-start(f32[64,1,1024]{2,1,0:T(1,128)} %reshape.2928), calls=%async_computation | async-start | bytes 524288 | tf_op jit(solution)/shard_map/all_to_all | solution.py:151
  93.1 773.4 %all-reduce.9.cloned.1.call-start = ((), (), s32[]{:S(2)}) async-start(), calls=%async_computation.6 | async-start | bytes 524288 | tf_op jit(solution)/shard_map/psum | solution.py:164
  130.2 5.4 copy-start.4
  379.7 11.8 copy-start.5
  379.7 11.9 copy-start.10
  379.7 11.9 copy-start.13
  402.7 581.4 %copy-start.7 = (f32[128,16,2]{0,1,2:T(8,128)}, f32[128,16,2]{0,1,2:T(8,128)S(1)}, u32[]{:S(2)}) copy-start(f32[128,16,2]{0,1,2:T(8,128)S(1)} %concatenate.42) | copy-start | bytes 49156
  404.4 432.5 %copy-start.34 = (f32[16]{0:T(128)S(1)}, f32[16]{0:T(128)}, u32[]{:S(2)}) copy-start(f32[16]{0:T(128)} %get-tuple-element.2192) | copy-start | bytes 196
  835.5 3.7 copy-start.32
  840.9 129.6 %all-reduce.11.cloned.1.call-start = ((), (), s32[]{:S(2)}) async-start(), calls=%async_computation.7 | async-start | bytes 524288 | tf_op jit(solution)/shard_map/psum | solution.py:150
  903.7 2.0 copy-start.23
  903.7 2.0 copy-start.25
  905.8 2.2 copy-start.1
  930.0 16.5 copy-start.18
  930.0 16.5 copy-start.21
  973.6 19.9 all-to-all-start.2
  983.7 868.2 %all-reduce.13.cloned.1.call-start = ((), (), s32[]{:S(2)}) async-start(), calls=%async_computation.8 | async-start | bytes 524288 | tf_op jit(solution)/shard_map/psum | solution.py:164
  1232.1 11.6 copy-start.6
  1232.1 11.6 copy-start.11
  1232.1 11.6 copy-start.14
  1232.1 11.6 copy-start.47
  1234.0 13.7 copy-start.8
  1234.0 13.7 copy-start.29
  1821.9 6.9 copy-start.33
  1830.4 125.3 %all-reduce.15.cloned.1.call-start = ((), (), s32[]{:S(2)}) async-start(), calls=%async_computation.9 | async-start | bytes 524288 | tf_op jit(solution)/shard_map/psum | solution.py:150
  1889.0 2.0 copy-start.24
  1889.0 2.0 copy-start.26
  1891.0 2.2 copy-start.2
  1915.3 16.5 copy-start.19
  1915.3 16.5 copy-start.22
  1980.4 1.3 copy-start.31
  1981.7 166.2 %copy-start.35 = (f32[16]{0:T(128)S(1)}, f32[16]{0:T(128)}, u32[]{:S(2)}) copy-start(f32[16]{0:T(128)} %get-tuple-element.2192) | copy-start | bytes 196
  1981.7 166.2 %copy-start.36 = (f32[16]{0:T(128)S(1)}, f32[16]{0:T(128)}, u32[]{:S(2)}) copy-start(f32[16]{0:T(128)} %get-tuple-element.2193) | copy-start | bytes 196
  1981.7 166.1 %copy-start.37 = (f32[16]{0:T(128)S(1)}, f32[16]{0:T(128)}, u32[]{:S(2)}) copy-start(f32[16]{0:T(128)} %get-tuple-element.2194) | copy-start | bytes 196
  1981.7 166.1 %copy-start.38 = (f32[16]{0:T(128)S(1)}, f32[16]{0:T(128)}, u32[]{:S(2)}) copy-start(f32[16]{0:T(128)} %get-tuple-element.2195) | copy-start | bytes 196
  1981.7 166.1 %copy-start.39 = (f32[16]{0:T(128)S(1)}, f32[16]{0:T(128)}, u32[]{:S(2)}) copy-start(f32[16]{0:T(128)} %get-tuple-element.2196) | copy-start | bytes 196
  1981.8 166.1 %copy-start.40 = (f32[16]{0:T(128)S(1)}, f32[16]{0:T(128)}, u32[]{:S(2)}) copy-start(f32[16]{0:T(128)} %get-tuple-element.2197) | copy-start | bytes 196
  1981.8 166.1 %copy-start.41 = (f32[16]{0:T(128)S(1)}, f32[16]{0:T(128)}, u32[]{:S(2)}) copy-start(f32[16]{0:T(128)} %get-tuple-element.2198) | copy-start | bytes 196
  1981.8 166.1 %copy-start.42 = (f32[16]{0:T(128)S(1)}, f32[16]{0:T(128)}, u32[]{:S(2)}) copy-start(f32[16]{0:T(128)} %get-tuple-element.2199) | copy-start | bytes 196
  1981.8 166.1 %copy-start.43 = (f32[16]{0:T(128)S(1)}, f32[16]{0:T(128)}, u32[]{:S(2)}) copy-start(f32[16]{0:T(128)} %get-tuple-element.2200) | copy-start | bytes 196
  1981.8 166.1 %copy-start.44 = (f32[16]{0:T(128)S(1)}, f32[16]{0:T(128)}, u32[]{:S(2)}) copy-start(f32[16]{0:T(128)} %get-tuple-element.2201) | copy-start | bytes 196
  1981.8 166.1 %copy-start.45 = (f32[16]{0:T(128)S(1)}, f32[16]{0:T(128)}, u32[]{:S(2)}) copy-start(f32[16]{0:T(128)} %get-tuple-element.2202) | copy-start | bytes 196
  1981.8 166.1 %copy-start.46 = (f32[16]{0:T(128)S(1)}, f32[16]{0:T(128)}, u32[]{:S(2)}) copy-start(f32[16]{0:T(128)} %get-tuple-element.2018) | copy-start | bytes 196
  2147.2 0.6 copy-start.27
  2148.0 1.3 copy-start.12
  2148.0 1.3 copy-start.15
  2148.0 1.3 copy-start.48
  2148.4 2.7 copy-start.28
Sparse Core Ops, SparseCore 0:
  52.2 27.4 all-reduce.6
  841.0 25.3 all-reduce.8
  949.3 21.1 all-reduce.10
  1830.5 21.3 all-reduce.12
  1934.6 21.1 all-reduce.14
where the time goes:
time: 2260 us; the launch traced here: 2220 us
  other arithmetic  728 us (32%)
  local copies, waits for them, and re-layouts  536 us (24%)
  loops' own time  452 us (20%)
  blocking collectives  250 us (11%)
  waiting for transfers between devices  116 us (5%)
  matrix products  81 us (4%)
  starting transfers between devices  31 us (1%)
  between operations  30.8 us (1%)
    another operation x5, loops' own time, legendre_rows(): lax.scan(advance, (seeds[:, 0], seeds[:, 1], carried), jnp.arange(2, 128,...  452 us
    sqrt x152, other arithmetic, ladder(): jnp.sqrt((4.0 - 1.0 / (degree_f * degree_f)) / ((1.0 - m_over_l) * (1.0 +...  434 us
    psum x2, blocking collectives, squares(): return lax.psum(jnp.sum(vector * vector), ('blk', 'rep'))  126 us
    broadcast_in_dim x305, local copies, waits for them, and re-layouts, block_layout(): column_m = jnp.where(block_side == 0, pair_m[:, 0:1], pair_m[:, 1:2])  113 us
    broadcast_in_dim x180, local copies, waits for them, and re-layouts, spread_columns(): chosen = jnp.where(block_side[:, :, None, None] == 0, side_zero, side_one)  81.7 us
    add x34, other arithmetic, visit(): return (totals + weight[:, :, None] * current[:, None, :], None)  74.5 us
    mul x287, local copies, waits for them, and re-layouts, visit(): return (totals + weight[:, :, None] * current[:, None, :], None)  69 us
    ge x306, local copies, waits for them, and re-layouts, block_layout(): block_side = (block_ids[None, :] >= block_count[:, None]).astype(jnp.int32)  68.6 us
  transfers between devices with their start and end apart: 7, of which 6 were waited for; matrix products, arithmetic and copies ran while one was open for 1% of the time, Pallas kernels for 0%

commit v1 on v0

v1 whole, which is shorter than its diff:
```python
import functools
import math

import jax
import jax.numpy as jnp
from jax import lax
from jax.experimental import pallas as pl
from jax.experimental.pallas import tpu as pltpu
from jax.sharding import PartitionSpec as P

NPHI = 32768
NCOL = 1024
NPAIRS = 512
NBP = 4
RH = 16
CHIPS = 64
SECTION = 1024
HALF = SECTION // 2
OUTER = NPHI // SECTION
LOOPS = CHIPS * RH
GROUPS = LOOPS // 128
COARSE = 16
FINE = HALF // COARSE
SCALE = 2.0**-13
PERIOD = 2 * NPHI
F32 = jnp.float32
BF16 = jnp.bfloat16


def chip_at(group, place):
    return 8 * group + 4 * (place % 2) + place // 2


def split(value):
    high = value.astype(BF16)
    return high, (value - high.astype(F32)).astype(BF16)


def lanes(rows=8, width=128):
    return lax.broadcasted_iota(jnp.int32, (rows, width), 1)


def prepare_kernel(rep_ref, seeds_ref, cos_ref, m_ref, start_ref, keep_ref, send_ref, x_ref, step_ref, norm_ref):
    first = rep_ref[0] == 0
    low = (lanes() % 32) < 16

    def halves(near, far):
        zero = jnp.where(low, near, pltpu.roll(far, 16, 1))
        one = jnp.where(low, pltpu.roll(near, 112, 1), far)
        return jnp.where(first, zero, one), jnp.where(first, one, zero)

    for group in range(GROUPS):
        at = 256 * group
        spot = slice(128 * group, 128 * group + 128)
        near = jnp.broadcast_to(cos_ref[:, at : at + 128], (8, 128))
        far = jnp.broadcast_to(cos_ref[:, at + 128 : at + 256], (8, 128))
        x_ref[:, spot] = halves(near, far)[0]
        for block in range(2):
            for which in range(2):
                near = seeds_ref[block, which, :, at : at + 128]
                far = seeds_ref[block, which, :, at + 128 : at + 256]
                keep, send = halves(near, far)
                keep_ref[block, which, :, spot] = keep
                send_ref[block, which, :, spot] = send

    lane = lanes()

    def ladder(degree, column_m):
        ratio = column_m / degree
        return jnp.sqrt((4.0 - 1.0 / (degree * degree)) / ((1.0 - ratio) * (1.0 + ratio)))

    for block in range(NBP):
        column_m = m_ref[block].astype(F32)
        degree = start_ref[block] + lane
        now = ladder(degree.astype(F32), column_m)
        before = ladder((degree - 1).astype(F32), column_m)
        norm = jnp.where(lane < 2, 1.0, now / before)
        for shift in (2, 4, 8, 16, 32, 64):
            norm = norm * jnp.where(lane >= shift, pltpu.roll(norm, shift, 1), 1.0)
        step_ref[block] = now * pltpu.roll(norm, 1, 1) / norm
        norm_ref[block] = norm


def prepare(rep, seeds, loop_cos, column_m, block_start):
    sds = jax.ShapeDtypeStruct
    return pl.pallas_call(
        prepare_kernel,
        in_specs=[pl.BlockSpec(memory_space=pltpu.SMEM)] + [pl.BlockSpec(memory_space=pltpu.VMEM)] * 4,
        out_shape=(
            sds((2, 2, 8, LOOPS), F32),
            sds((2, 2, 8, LOOPS), F32),
            sds((8, LOOPS), F32),
            sds((NBP, 8, 128), F32),
            sds((NBP, 8, 128), F32),
        ),
        name="prepare",
    )(rep, seeds, loop_cos, column_m, block_start)


def analysis_kernel(recv_ref, seeds_ref, x_ref, step_ref, norm_ref, count_ref, out_ref, spec_ref):
    place = lanes() // 16
    tail = jnp.zeros((8, 128), F32)
    for group in range(GROUPS):
        made = [None] * 4
        for spot in range(8):
            tile = recv_ref[chip_at(group, spot)]
            tail = tail + tile
            for kind in range(4):
                turned = pltpu.roll(tile, ((spot - kind) * 16) % 128, 1) if spot != kind else tile
                made[kind] = turned if spot == 0 else jnp.where(place == spot, turned, made[kind])
        for kind in range(4):
            spec_ref[kind, group] = made[kind]
    out_ref[2 * NBP] = tail
    lane = lanes()
    even = {shift: (lane & shift) == 0 for shift in (1, 2, 4, 8, 16, 32, 64)}

    def push(stack, value, index):
        shift = 1
        while index & shift:
            first = stack.pop()
            near = jnp.where(even[shift], first, value)
            far = jnp.where(even[shift], value, first)
            value = near + pltpu.roll(far, 128 - shift, 1)
            shift *= 2
        stack.append(value)

    span = [slice(128 * g, 128 * g + 128) for g in range(GROUPS)]

    @pl.loop(0, NBP)
    def _(block):
        x = [x_ref[:, s] for s in span]
        older = [seeds_ref[block, 0, :, s] for s in span]
        newer = [seeds_ref[block, 1, :, s] for s in span]
        side = block >= count_ref[...]
        real = [jnp.where(side, spec_ref[1, g], spec_ref[0, g]) for g in range(GROUPS)]
        imag = [jnp.where(side, spec_ref[3, g], spec_ref[2, g]) for g in range(GROUPS)]
        steps = step_ref[block]

        def emit(rows, index):
            for stack, part in zip(stacks, (real, imag)):
                terms = [row * value for row, value in zip(rows, part)]
                while len(terms) > 1:
                    terms = [a + b for a, b in zip(terms[::2], terms[1::2])]
                push(stack, terms[0], index)

        stacks = ([], [])
        emit(older, 0)
        emit(newer, 1)
        for index in range(2, 128):
            factor = jnp.broadcast_to(steps[:, index : index + 1], (8, 128))
            fresh = [(factor * a) * b - c for a, b, c in zip(x, newer, older)]
            older, newer = newer, fresh
            emit(newer, index)
        outs = [stack[0] for stack in stacks]
        norm = norm_ref[block]
        out_ref[2 * block] = outs[0] * norm
        out_ref[2 * block + 1] = outs[1] * norm


def vmem(count):
    return [pl.BlockSpec(memory_space=pltpu.VMEM)] * count


def analysis(recv, seeds, x, step, norm, count):
    return pl.pallas_call(
        analysis_kernel,
        in_specs=vmem(6),
        out_shape=jax.ShapeDtypeStruct((2 * NBP + 1, 8, 128), F32),
        scratch_shapes=[pltpu.VMEM((4, GROUPS, 8, 128), F32)],
        name="analysis",
    )(recv, seeds, x, step, norm, count)


def total_of(tile):
    return jnp.sum(jnp.sum(tile, axis=1, keepdims=True), axis=0, keepdims=True)


def lane_total(tile, lane):
    return total_of(jnp.where(lanes() == lane, tile, 0.0))


def synthesis(coef_ref, seeds_ref, x_ref, step_ref, norm_ref, count_ref, spec_ref, extra, out_ref):
    span = [slice(128 * g, 128 * g + 128) for g in range(GROUPS)]
    spec_ref[...] = jnp.zeros_like(spec_ref)

    @pl.loop(0, NBP)
    def _(block):
        x = [x_ref[:, s] for s in span]
        older = [seeds_ref[block, 0, :, s] for s in span]
        newer = [seeds_ref[block, 1, :, s] for s in span]
        steps = step_ref[block]
        norm = norm_ref[block]
        real = coef_ref[2 * block] * norm
        imag = coef_ref[2 * block + 1] * norm

        def spread(values, index):
            return jnp.broadcast_to(values[:, index : index + 1], (8, 128))

        sums_re = [spread(real, 0) * a + spread(real, 1) * b for a, b in zip(older, newer)]
        sums_im = [spread(imag, 0) * a + spread(imag, 1) * b for a, b in zip(older, newer)]
        for index in range(2, 128):
            factor = spread(steps, index)
            fresh = [(factor * a) * b - c for a, b, c in zip(x, newer, older)]
            older, newer = newer, fresh
            weight_re = spread(real, index)
            weight_im = spread(imag, index)
            sums_re = [s + weight_re * p for s, p in zip(sums_re, newer)]
            sums_im = [s + weight_im * p for s, p in zip(sums_im, newer)]
        side = block >= count_ref[...]
        for g in range(GROUPS):
            spec_ref[0, g] += jnp.where(side, 0.0, sums_re[g])
            spec_ref[1, g] += jnp.where(side, sums_re[g], 0.0)
            spec_ref[2, g] += jnp.where(side, 0.0, sums_im[g])
            spec_ref[3, g] += jnp.where(side, sums_im[g], 0.0)

    place = lanes() // 16
    for group in range(GROUPS):
        values = [spec_ref[kind, group] for kind in range(4)]
        for spot in range(8):
            tile = extra
            for kind in range(4):
                turned = pltpu.roll(values[kind], ((kind - spot) * 16) % 128, 1) if spot != kind else values[kind]
                tile = jnp.where(place == kind, turned, tile)
            out_ref[chip_at(group, spot)] = tile


def first_kernel(mine_ref, other_ref, prior_ref, seeds_ref, x_ref, step_ref, norm_ref, count_ref, out_ref, rhs_ref, spec_ref):
    squares = jnp.zeros((8, 128), F32)
    energy = jnp.zeros((8, 128), F32)
    for row in range(2 * NBP):
        value = mine_ref[row] + other_ref[row]
        rhs_ref[row] = value
        squares = squares + value * value
        energy = energy + prior_ref[row] * value * value
    lane = lanes()
    extra = jnp.where(lane == 64, jnp.sum(squares, axis=1, keepdims=True), 0.0)
    extra = jnp.where(lane == 65, jnp.sum(energy, axis=1, keepdims=True), extra)
    synthesis(rhs_ref, seeds_ref, x_ref, step_ref, norm_ref, count_ref, spec_ref, extra, out_ref)


def second_kernel(
    mine_ref, other_ref, prior_ref, rhs_ref, told_ref, seeds_ref, x_ref, step_ref, norm_ref, count_ref,
    out_ref, res_ref, alpha_ref, spec_ref,
):
    told = told_ref[...]
    norm_now = lane_total(told, 0) * 0.125
    energy = lane_total(told, 1) * 0.125
    pixels = lane_total(mine_ref[2 * NBP] + other_ref[2 * NBP], 64)
    alpha = norm_now / (energy + pixels)
    alpha_ref[...] = jnp.broadcast_to(alpha, (8, 128))
    squares = jnp.zeros((8, 128), F32)
    for row in range(2 * NBP):
        image = prior_ref[row] * rhs_ref[row] + (mine_ref[row] + other_ref[row])
        value = rhs_ref[row] - alpha * image
        res_ref[row] = value
        squares = squares + value * value
    extra = jnp.where(lanes() == 64, jnp.sum(squares, axis=1, keepdims=True), 0.0)
    synthesis(res_ref, seeds_ref, x_ref, step_ref, norm_ref, count_ref, spec_ref, extra, out_ref)


def last_kernel(mine_ref, other_ref, prior_ref, rhs_ref, res_ref, dir_ref, told_ref, alpha_ref, sol_ref, out_ref):
    norm_now = lane_total(told_ref[...], 0) * 0.125
    energy = lane_total(mine_ref[2 * NBP], 65)
    pixels = lane_total(mine_ref[2 * NBP] + other_ref[2 * NBP], 64)
    alpha = norm_now / (energy + pixels)
    for row in range(2 * NBP):
        image = prior_ref[row] * dir_ref[row] + (mine_ref[row] + other_ref[row])
        sol_ref[row] = alpha_ref[...] * rhs_ref[row] + alpha * dir_ref[row]
        out_ref[row] = res_ref[row] - alpha * image


COEF = jax.ShapeDtypeStruct((2 * NBP, 8, 128), F32)
PAYLOAD = jax.ShapeDtypeStruct((CHIPS, 8, 128), F32)
TILE = jax.ShapeDtypeStruct((8, 128), F32)


def first_step(*arrays):
    return pl.pallas_call(
        first_kernel,
        in_specs=vmem(8),
        out_shape=(PAYLOAD, COEF),
        scratch_shapes=[pltpu.VMEM((4, GROUPS, 8, 128), F32)],
        name="first",
    )(*arrays)


def second_step(*arrays):
    return pl.pallas_call(
        second_kernel,
        in_specs=vmem(10),
        out_shape=(PAYLOAD, COEF, TILE),
        scratch_shapes=[pltpu.VMEM((4, GROUPS, 8, 128), F32)],
        name="second",
    )(*arrays)


def last_step(*arrays):
    return pl.pallas_call(last_kernel, in_specs=vmem(8), out_shape=(COEF, COEF), name="last")(*arrays)


ROWS = OUTER * RH
CHUNK = 256


def dot3(left, right_ref, spot):
    high, low = left
    return (
        jnp.dot(high, right_ref[0, :, spot], preferred_element_type=F32)
        + jnp.dot(low, right_ref[0, :, spot], preferred_element_type=F32)
        + jnp.dot(high, right_ref[1, :, spot], preferred_element_type=F32)
    )


def dot3_turned(left, right_ref, spot):
    high, low = left
    dims = (((1,), (1,)), ((), ()))
    return (
        lax.dot_general(high, right_ref[0, spot, :], dims, preferred_element_type=F32)
        + lax.dot_general(low, right_ref[0, spot, :], dims, preferred_element_type=F32)
        + lax.dot_general(high, right_ref[1, spot, :], dims, preferred_element_type=F32)
    )


def to_columns(even, odd, cos_ref, sin_ref, phase_ref, extra, out_ref):
    parts = [[], []]
    for at in range(0, NCOL, CHUNK):
        spot = slice(at, at + CHUNK)
        along = dot3(even, cos_ref, spot).reshape(OUTER, RH, CHUNK)
        across = dot3(odd, sin_ref, spot).reshape(OUTER, RH, CHUNK)
        real = jnp.zeros((RH, CHUNK), F32)
        imag = jnp.zeros((RH, CHUNK), F32)
        for section in range(OUTER):
            cos = phase_ref[0, section : section + 1, spot]
            sin = phase_ref[1, section : section + 1, spot]
            real = real + (cos * along[section] - sin * across[section])
            imag = imag - (cos * across[section] + sin * along[section])
        parts[0].append(real)
        parts[1].append(imag)
    rows = []
    for part in parts:
        whole = jnp.concatenate(part, axis=1)
        rows += [whole[:, :NPAIRS], whole[:, NPAIRS:]]
    whole = jnp.concatenate(rows + [extra, jnp.zeros((56, NPAIRS), F32)], axis=0)
    for at in range(0, NPAIRS, 128):
        turned = jnp.transpose(whole[:, at : at + 128])
        out_ref[at // 8 : at // 8 + 16] = turned.reshape(16, 8, 128)


def sky_kernel(
    rep_ref, noise_ref, noise_other_ref, sky_ref, sky_other_ref, angle_ref, phase_ref,
    out_ref, plus_ref, minus_ref, cos_ref, sin_ref, even_ref, odd_ref,
):
    for coarse in range(COARSE):
        c_one = angle_ref[0, coarse : coarse + 1, :]
        s_one = angle_ref[1, coarse : coarse + 1, :]
        c_two = angle_ref[0, COARSE:, :]
        s_two = angle_ref[1, COARSE:, :]
        spot = slice(FINE * coarse, FINE * coarse + FINE)
        high, low = split(c_one * c_two - s_one * s_two)
        cos_ref[0, spot, :] = high
        cos_ref[1, spot, :] = low
        high, low = split(s_one * c_two + c_one * s_two)
        sin_ref[0, spot, :] = high
        sin_ref[1, spot, :] = low
    flip = jnp.where(
        lax.broadcasted_iota(jnp.int32, (256, 256), 0) + lax.broadcasted_iota(jnp.int32, (256, 256), 1) == 255, 1.0, 0.0
    ).astype(BF16)

    def turned(rows):
        pieces = []
        for at in (256, 0):
            high, low = split(rows[:, at : at + 256])
            pieces.append(jnp.dot(high, flip, preferred_element_type=F32) + jnp.dot(low, flip, preferred_element_type=F32))
        return jnp.concatenate(pieces, axis=1)

    for half, (noise, sky) in enumerate(((noise_ref, sky_ref), (noise_other_ref, sky_other_ref))):
        count = OUTER // 2

        def rows_of(ref, offset):
            return jnp.concatenate([ref[:, SECTION * b + offset : SECTION * b + offset + HALF] for b in range(count)], axis=0)

        plus = rows_of(noise, HALF) * (SCALE * SCALE)
        minus = turned(rows_of(noise, 0)) * (SCALE * SCALE)
        spot = slice(half * count * RH, (half + 1) * count * RH)
        plus_ref[spot, :] = plus
        minus_ref[spot, :] = minus
        ahead = plus * rows_of(sky, HALF) * (1.0 / SCALE)
        back = minus * turned(rows_of(sky, 0)) * (1.0 / SCALE)
        high, low = split(ahead + back)
        even_ref[0, spot, :] = high
        even_ref[1, spot, :] = low
        high, low = split(ahead - back)
        odd_ref[0, spot, :] = high
        odd_ref[1, spot, :] = low
    to_columns(
        (even_ref[0], even_ref[1]), (odd_ref[0], odd_ref[1]), cos_ref, sin_ref, phase_ref,
        jnp.zeros((8, NPAIRS), F32), out_ref,
    )


def sky_step(rep, noise, noise_other, sky, sky_other, angles, phases):
    sds = jax.ShapeDtypeStruct
    own = pl.BlockSpec((RH, NPHI // 2), lambda i, rep: (rep[0], 0))

    def full(*shape):
        return pl.BlockSpec(shape, lambda i, rep: (0,) * len(shape))

    return pl.pallas_call(
        sky_kernel,
        grid_spec=pltpu.PrefetchScalarGridSpec(
            num_scalar_prefetch=1,
            grid=(1,),
            in_specs=[
                own, full(RH, NPHI // 2), own, full(RH, NPHI // 2),
                full(2, COARSE + FINE, NCOL), full(2, OUTER, NCOL),
            ],
            out_specs=(
                full(CHIPS, 8, 128), full(ROWS, HALF), full(ROWS, HALF),
                full(2, HALF, NCOL), full(2, HALF, NCOL),
            ),
            scratch_shapes=[pltpu.VMEM((2, ROWS, HALF), BF16), pltpu.VMEM((2, ROWS, HALF), BF16)],
        ),
        out_shape=(
            PAYLOAD, sds((ROWS, HALF), F32), sds((ROWS, HALF), F32),
            sds((2, HALF, NCOL), BF16), sds((2, HALF, NCOL), BF16),
        ),
        compiler_params=pltpu.CompilerParams(vmem_limit_bytes=60 * 2**20),
        name="sky",
    )(rep, noise, noise_other, sky, sky_other, angles, phases)


def by_rows(recv_ref):
    flat = recv_ref[...].reshape(NPAIRS, 128)
    return jnp.concatenate([jnp.transpose(flat[at : at + 128]) for at in range(0, NPAIRS, 128)], axis=1)


def through_map(rows, energy, plus_ref, minus_ref, cos_ref, sin_ref, phase_ref, out_ref, mixed_ref, even_ref, odd_ref):
    real = jnp.concatenate([rows[0:RH], rows[RH : 2 * RH]], axis=1)
    imag = jnp.concatenate([rows[2 * RH : 3 * RH], rows[3 * RH : 4 * RH]], axis=1)
    for section in range(OUTER):
        cos = phase_ref[0, section : section + 1, :]
        sin = phase_ref[1, section : section + 1, :]
        spot = slice(section * RH, section * RH + RH)
        high, low = split(real * cos - imag * sin)
        mixed_ref[0, spot, :] = high
        mixed_ref[1, spot, :] = low
        high, low = split(real * sin + imag * cos)
        mixed_ref[2, spot, :] = high
        mixed_ref[3, spot, :] = low
    power = jnp.zeros((ROWS, 128), F32)
    for at in range(0, HALF, CHUNK):
        spot = slice(at, at + CHUNK)
        even = dot3_turned((mixed_ref[0], mixed_ref[1]), cos_ref, spot)
        odd = dot3_turned((mixed_ref[2], mixed_ref[3]), sin_ref, spot)
        ahead = even - odd
        back = even + odd
        heavy_ahead = plus_ref[:, spot] * ahead
        heavy_back = minus_ref[:, spot] * back
        terms = heavy_ahead * ahead + heavy_back * back
        for piece in range(0, CHUNK, 128):
            power = power + terms[:, piece : piece + 128]
        high, low = split(heavy_ahead + heavy_back)
        even_ref[0, :, spot] = high
        even_ref[1, :, spot] = low
        high, low = split(heavy_ahead - heavy_back)
        odd_ref[0, :, spot] = high
        odd_ref[1, :, spot] = low
    pixels = total_of(power)
    lane = lanes(8, NPAIRS)
    row = lax.broadcasted_iota(jnp.int32, (8, NPAIRS), 0)
    extra = jnp.where((lane % 8 == 0) & (row == 0), pixels, 0.0)
    extra = jnp.where((lane % 8 == 0) & (row == 1), energy, extra)
    to_columns((even_ref[0], even_ref[1]), (odd_ref[0], odd_ref[1]), cos_ref, sin_ref, phase_ref, extra, out_ref)


def row_total(rows, index):
    return jnp.sum(rows[index : index + 1], axis=1, keepdims=True)


def map_one_kernel(recv_ref, plus_ref, minus_ref, cos_ref, sin_ref, phase_ref, out_ref, told_ref, mixed_ref, even_ref, odd_ref):
    rows = by_rows(recv_ref)
    lane = lanes()
    told = jnp.where(lane == 0, row_total(rows, 64), 0.0)
    told_ref[...] = jnp.where(lane == 1, row_total(rows, 65), told)
    through_map(
        rows, jnp.zeros((1, 1), F32), plus_ref, minus_ref, cos_ref, sin_ref, phase_ref, out_ref, mixed_ref, even_ref, odd_ref
    )


def map_two_kernel(
    recv_ref, before_ref, told_ref, prior_ref, rhs_ref, res_ref, plus_ref, minus_ref, cos_ref, sin_ref, phase_ref,
    out_ref, dir_ref, told_out_ref, mixed_ref, even_ref, odd_ref,
):
    rows = by_rows(recv_ref)
    norm_next = row_total(rows, 64)
    beta = norm_next / (lane_total(told_ref[...], 0) * 0.125)
    told_out_ref[...] = jnp.where(lanes() == 0, norm_next, 0.0)
    energy = jnp.zeros((8, 128), F32)
    for row in range(2 * NBP):
        value = res_ref[row] + beta * rhs_ref[row]
        dir_ref[row] = value
        energy = energy + prior_ref[row] * value * value
    rows = rows + beta * by_rows(before_ref)
    through_map(
        rows, total_of(energy), plus_ref, minus_ref, cos_ref, sin_ref, phase_ref, out_ref, mixed_ref, even_ref, odd_ref
    )


MAP_SCRATCH = [pltpu.VMEM((4, ROWS, NCOL), BF16), pltpu.VMEM((2, ROWS, HALF), BF16), pltpu.VMEM((2, ROWS, HALF), BF16)]


def map_one(*arrays):
    return pl.pallas_call(
        map_one_kernel,
        in_specs=vmem(6),
        out_shape=(PAYLOAD, TILE),
        scratch_shapes=MAP_SCRATCH,
        compiler_params=pltpu.CompilerParams(vmem_limit_bytes=60 * 2**20),
        name="map_one",
    )(*arrays)


def map_two(*arrays):
    return pl.pallas_call(
        map_two_kernel,
        in_specs=vmem(11),
        out_shape=(PAYLOAD, COEF, TILE),
        scratch_shapes=MAP_SCRATCH,
        compiler_params=pltpu.CompilerParams(vmem_limit_bytes=60 * 2**20),
        name="map_two",
    )(*arrays)


def shards(sky_map, noise_weight, prior_weight, seeds, loop_cos, pair_m, block_count):
    rep = lax.axis_index("rep")
    rep_array = jnp.reshape(rep, (1,)).astype(jnp.int32)

    def swap(value):
        return lax.ppermute(value, "rep", [(0, 1), (1, 0)])

    def both(mine, other):
        first = rep == 0
        return jnp.concatenate([jnp.where(first, mine, other), jnp.where(first, other, mine)], axis=0)

    def transpose(payload):
        return lax.all_to_all(payload, "blk", split_axis=0, concat_axis=0, tiled=True)

    away = RH * (1 - rep)
    noise_other = swap(lax.dynamic_slice_in_dim(noise_weight, away, RH, 0))
    sky_other = swap(lax.dynamic_slice_in_dim(sky_map, away, RH, 0))

    every_m = jnp.transpose(pair_m).reshape(1, NCOL)
    coarse = 2 * FINE * jnp.arange(COARSE, dtype=jnp.int32)
    fine = 2 * jnp.arange(FINE, dtype=jnp.int32) + 1
    section = jnp.arange(OUTER, dtype=jnp.int32)
    section = (section + OUTER // 2 * rep) % OUTER
    centre = 2 * SECTION * section + SECTION - 1
    factors = jnp.concatenate([coarse, fine, centre])
    cycles = factors[:, None] * every_m % PERIOD
    angles = cycles.astype(F32) * (2.0 * math.pi / PERIOD)
    table = jnp.stack([jnp.cos(angles), jnp.sin(angles)])
    inner, phases = table[:, : COARSE + FINE], table[:, COARSE + FINE :]

    local_m = lax.dynamic_slice_in_dim(pair_m, lax.axis_index("blk") * 8, 8, 0)
    blocks = jnp.arange(NBP, dtype=jnp.int32)[:, None]
    side = blocks >= block_count[None, :]
    offset = jnp.where(side, blocks - block_count[None, :], blocks)
    column_m = jnp.where(side, local_m[None, :, 1], local_m[None, :, 0])
    block_start = 128 * (17 * column_m // 2048 + 1) + 128 * offset
    wide = (NBP, 8, 128)
    count = jnp.broadcast_to(block_count[:, None], (8, 128))
    keep, send, x, step, norm = prepare(
        rep_array,
        jnp.transpose(seeds, (1, 2, 0, 3)),
        loop_cos[None, :],
        jnp.broadcast_to(column_m[:, :, None], wide),
        jnp.broadcast_to(block_start[:, :, None], wide),
    )
    seeds_all = both(keep, swap(send))
    prior_here = jnp.transpose(prior_weight, (1, 2, 0, 3))
    prior = both(prior_here, swap(prior_here)).reshape(2 * NBP, 8, 128)
    legendre = (seeds_all, x, step, norm, count)

    payload, plus, minus, cos, sin = sky_step(rep_array, noise_weight, noise_other, sky_map, sky_other, inner, phases)
    here = analysis(transpose(payload), *legendre)
    payload, rhs = first_step(here, swap(here), prior, *legendre)
    before = transpose(payload)
    payload, told = map_one(before, plus, minus, cos, sin, phases)
    here = analysis(transpose(payload), *legendre)
    payload, residual, alpha = second_step(here, swap(here), prior, rhs, told, *legendre)
    payload, direction, told = map_two(
        transpose(payload), before, told, prior, rhs, residual, plus, minus, cos, sin, phases
    )
    here = analysis(transpose(payload), *legendre)
    results = last_step(here, swap(here), prior, rhs, residual, direction, told, alpha)

    def own(value):
        part = lax.dynamic_slice_in_dim(value.reshape(NBP, 2, 8, 128), 2 * rep, 2, 0)
        return jnp.transpose(part, (2, 0, 1, 3))

    return (own(results[0]), own(results[1]))


def solution(mesh):
    placed = (
        P("blk", "rep"),
        P("blk", "rep"),
        P("blk", "rep", None, None),
        P("blk", "rep", None, None),
        P(),
        P(),
        P("blk"),
    )
    return jax.shard_map(
        shards,
        mesh=mesh,
        in_specs=placed,
        out_specs=(P("blk", "rep", None, None), P("blk", "rep", None, None)),
        check_vma=False,
    )
```

time: 2260 us -> 180 us (0.08); the launches traced: 2220 us -> 179 us
  other arithmetic: 728 us -> 3.84 us
  local copies, waits for them, and re-layouts: 536 us -> 11 us
  loops' own time: 452 us -> 0 us
  blocking collectives: 250 us -> 60.2 us
  waiting for transfers between devices: 116 us -> 11.6 us
  matrix products: 81 us -> 0 us
  Pallas kernels: 0 us -> 71.8 us
  between operations: 30.8 us -> 0.79 us
    another operation x5 -> x0, loops' own time: 452 us -> none  [legendre_rows(): lax.scan(advance, (seeds[:, 0], seeds[:, 1], carried), jnp.arange(2, 128,...]
    sqrt x152 -> x0, other arithmetic: 434 us -> none  [ladder(): jnp.sqrt((4.0 - 1.0 / (degree_f * degree_f)) / ((1.0 - m_over_l) * (1.0 +...]
    broadcast_in_dim x525 -> x4, local copies, waits for them, and re-layouts: 198 us -> 2.03 us  [the longest x1 0.68 us: shards(): jnp.broadcast_to(column_m[:, :, None], wide)]
    psum x3 -> x0, blocking collectives: 190 us -> none  [the longest x2 126 us: squares(): return lax.psum(jnp.sum(vector * vector), ('blk', 'rep'))]
    psum x5 -> x0, waiting for transfers between devices: 107 us -> none  [the longest x3 60 us: analyze(): ready = lax.psum(partial_spec, 'rep')]
    mul x330 -> x0, local copies, waits for them, and re-layouts: 97.8 us -> none  [the longest x287 69 us: visit(): return (totals + weight[:, :, None] * current[:, None, :], None)]
    dot_general x7 -> x0, matrix products: 81 us -> none  [the longest x3 47 us: forward(): jnp.dot(pixels.reshape(loop_here * outer_len, inner_len), basis, precisio...]
    add x38 -> x2, other arithmetic: 74.5 us -> 0.02 us  [the longest x1 0.02 us: shards(): block_start = 128 * (17 * column_m // 2048 + 1) + 128 * offset]
  transfers between devices with their start and end apart: 7 -> 8, of which waited for: 6 -> 4; matrix products, arithmetic and copies ran while one was open for 1% -> 4% of each run, Pallas kernels for 0% -> 6%
where the time goes in v1:
time: 180 us; the launch traced here: 179 us
  Pallas kernels  71.8 us (40%)
  blocking collectives  60.2 us (33%)
  starting transfers between devices  20 us (11%)
  waiting for transfers between devices  11.6 us (6%)
  local copies, waits for them, and re-layouts  11 us (6%)
  other arithmetic  3.84 us (2%)
    all_to_all x4, blocking collectives, transpose(): lax.all_to_all(payload, 'blk', split_axis=0, concat_axis=0, tiled=True)  60.2 us
    pallas_call x3, Pallas kernels, analysis(): pl.pallas_call(analysis_kernel, in_specs=vmem(6), out_shape=jax.ShapeDtyp...  24.8 us
    pallas_call x1, Pallas kernels, map_two(): pl.pallas_call(map_two_kernel, in_specs=vmem(11), out_shape=(PAYLOAD, COE...  11.3 us
    all_to_all x1, starting transfers between devices, transpose(): lax.all_to_all(payload, 'blk', split_axis=0, concat_axis=0, tiled=True)  11.2 us
    pallas_call x1, Pallas kernels, map_one(): pl.pallas_call(map_one_kernel, in_specs=vmem(6), out_shape=(PAYLOAD, TILE...  11 us
    all_to_all x1, waiting for transfers between devices, transpose(): lax.all_to_all(payload, 'blk', split_axis=0, concat_axis=0, tiled=True)  9.03 us
    ppermute x7, starting transfers between devices, swap(): return lax.ppermute(value, 'rep', [(0, 1), (1, 0)])  8.83 us
    pallas_call x1, Pallas kernels, sky_step(): pl.pallas_call(sky_kernel, grid_spec=pltpu.PrefetchScalarGridSpec(num_sca...  8.44 us
  transfers between devices with their start and end apart: 8, of which 4 were waited for; matrix products, arithmetic and copies ran while one was open for 4% of the time, Pallas kernels for 6%

profile of v1, /device:TPU:1, one launch (start us, length us, event | category | flops | bytes accessed | tf_op | source)
XLA Modules:
  0.0 179.3 jit_solution(1467008050448151784)
XLA Ops:
  0.6 0.0 copy-start
  0.7 0.0 copy-start.3
  0.7 0.0 copy-start.9
  0.7 0.0 copy-start.10
  0.7 0.0 copy-start.8
  0.7 1.4 constant_dynamic-slice_fusion.4
  2.1 1.5 collective-permute-start
  3.6 0.0 copy-done
  3.6 1.0 constant_dynamic-slice_fusion.3
  4.7 0.3 collective-permute-start.1
  5.0 0.0 copy-done.3
  5.0 0.9 copy.19
  5.9 0.0 copy-done.9
  5.9 0.1 constant_dynamic-slice_fusion.2
  6.0 0.0 copy-done.10
  6.0 0.7 broadcast_in_dim.56.m_ref
  6.7 0.7 broadcast_in_dim.57.start_ref
  7.3 2.2 %prepare.1 = (f32[2,2,8,1024]{3,2,1,0:T(8,128)}, f32[2,2,8,1024]{3,2,1,0:T(8,128)}, f32[8,1024]{1,0:T(8,128)}, f32[4,8,128]{2,1,0:T(8,128)}, f32[4,8,128]{2,1,0:T(8,128)}) custom-call(s32[1]{0:T(128)} %bitcast.rep_ref, f32[2,2,8,2048]{3,2,1,0:T(8,128)} %bitcast.24, f32[1,2048]{1,0:T(1,128)} %bitcast.33, s32[4,8,128]{2,1,0:T(8,128)} %broadcast_in_dim.56.m_ref, ...), custom_call_target="tpu_custom_call" | custom-call | tf_op jit(solution)/shard_map/prepare/pallas_call | solution.py:86
  9.5 0.2 collective-permute-start.2
  9.7 0.0 copy-done.8
  9.7 0.3 collective-permute-start.4
  10.1 0.1 pad_add_fusion
  10.1 1.4 fusion.4
  11.5 0.8 fusion.angle_ref
  12.3 0.7 pad_maximum_fusion.phase_ref
  13.1 0.0 collective-permute-done.4
  13.1 0.0 copy-start.4
  13.1 0.0 collective-permute-done.noise_other_ref
  13.1 0.0 collective-permute-done.1.sky_other_ref
  13.1 0.0 copy-start.2
  13.1 1.1 copy-done.2
  14.2 8.4 %sky.1 = (f32[64,8,128]{2,1,0:T(8,128)}, f32[512,512]{1,0:T(8,128)}, f32[512,512]{1,0:T(8,128)}, bf16[2,512,1024]{2,1,0:T(8,128)(2,1)}, bf16[2,512,1024]{2,1,0:T(8,128)(2,1)}) custom-call(s32[1]{0:T(128)} %bitcast.rep_ref, f32[32,16384]{1,0:T(8,128)} %noise_ref.1, f32[16,16384]{1,0:T(8,128)} %collective-permute-done.noise_other_ref, f32[32,16384]{1,0:T(8,128)} %sky_ref.1, ...), custom_call_target="tpu_custom_call" | custom-call | tf_op jit(solution)/shard_map/sky/pallas_call | solution.py:408
  22.6 11.2 %all-to-all-start = ((f32[64,8,128]{2,1,0:T(8,128)}), f32[64,8,128]{2,1,0:T(8,128)S(1)}, u32[]{:S(2)}, u32[]{:S(2)}) async-start(f32[64,8,128]{2,1,0:T(8,128)} %get-tuple-element.24), calls=%async_computation | async-start | bytes 524288 | tf_op jit(solution)/shard_map/all_to_all | solution.py:546
  33.9 0.0 collective-permute-done.2
  33.9 0.0 copy-done.4
  33.9 0.7 pad_maximum_fusion.1.seeds_ref
  34.7 9.0 %all-to-all-done.recv_ref = f32[64,8,128]{2,1,0:T(8,128)S(1)} async-done(((f32[64,8,128]{2,1,0:T(8,128)}), f32[64,8,128]{2,1,0:T(8,128)S(1)}, u32[]{:S(2)}, u32[]{:S(2)}) %all-to-all-start) | async-done | bytes 262176 | tf_op jit(solution)/shard_map/all_to_all | solution.py:546
  43.7 0.7 broadcast_in_dim.58.count_ref
  44.4 0.0 copy-done.1
  44.4 8.3 %analysis.3.mine_ref = f32[9,8,128]{2,1,0:T(8,128)} custom-call(f32[64,8,128]{2,1,0:T(8,128)} %copy-done.1, f32[4,2,8,1024]{3,2,1,0:T(8,128)} %pad_maximum_fusion.1.seeds_ref, f32[8,1024]{1,0:T(8,128)} %get-tuple-element.27.x_ref, f32[4,8,128]{2,1,0:T(8,128)} %get-tuple-element.28.step_ref, f32[4,8,128]{2,1,0:T(8,128)} %get-tuple-element.29.norm_ref, ...), custom_call_target="tpu_custom_call" | custom-call | tf_op jit(solution)/shard_map/analysis/pallas_call | solution.py:165
  52.7 1.5 collective-permute-start.3
  54.2 0.6 copy.10
  54.9 0.4 collective-permute-done.3.other_ref
  55.3 0.6 copy-done.6
  55.9 6.2 %first.1 = (f32[64,8,128]{2,1,0:T(8,128)}, f32[8,8,128]{2,1,0:T(8,128)}) custom-call(f32[9,8,128]{2,1,0:T(8,128)} %analysis.3.mine_ref, f32[9,8,128]{2,1,0:T(8,128)} %copy-done.6, f32[8,8,128]{2,1,0:T(8,128)} %bitcast.25, f32[4,2,8,1024]{3,2,1,0:T(8,128)} %pad_maximum_fusion.1.seeds_ref, f32[8,1024]{1,0:T(8,128)} %get-tuple-element.27.x_ref, ...), custom_call_target="tpu_custom_call" | custom-call | tf_op jit(solution)/shard_map/first/pallas_call | solution.py:278
  62.1 15.5 %all_to_all.25.recv_ref.before_ref = f32[64,8,128]{2,1,0:T(8,128)} all-to-all(f32[64,8,128]{2,1,0:T(8,128)} %get-tuple-element.30), channel_id=1, replica_groups=mesh['blk'=64,'rep'=2] {'blk'}, dimensions={0} | all-to-all | bytes 524288 | tf_op jit(solution)/shard_map/all_to_all | solution.py:546
  77.7 11.0 %map_one.1 = (f32[64,8,128]{2,1,0:T(8,128)}, f32[8,128]{1,0:T(8,128)}) custom-call(f32[64,8,128]{2,1,0:T(8,128)} %all_to_all.25.recv_ref.before_ref, f32[512,512]{1,0:T(8,128)} %get-tuple-element.31.plus_ref, f32[512,512]{1,0:T(8,128)} %get-tuple-element.32.minus_ref, bf16[2,512,1024]{2,1,0:T(8,128)(2,1)} %get-tuple-element.33.cos_ref, ...), custom_call_target="tpu_custom_call" | custom-call | tf_op jit(solution)/shard_map/map_one/pallas_call | solution.py:513
  88.6 14.7 %all_to_all.26.recv_ref = f32[64,8,128]{2,1,0:T(8,128)} all-to-all(f32[64,8,128]{2,1,0:T(8,128)} %get-tuple-element.35), channel_id=1, replica_groups=mesh['blk'=64,'rep'=2] {'blk'}, dimensions={0} | all-to-all | bytes 524288 | tf_op jit(solution)/shard_map/all_to_all | solution.py:546
  103.3 8.3 %analysis.4.mine_ref = f32[9,8,128]{2,1,0:T(8,128)} custom-call(f32[64,8,128]{2,1,0:T(8,128)} %all_to_all.26.recv_ref, f32[4,2,8,1024]{3,2,1,0:T(8,128)} %pad_maximum_fusion.1.seeds_ref, f32[8,1024]{1,0:T(8,128)} %get-tuple-element.27.x_ref, f32[4,8,128]{2,1,0:T(8,128)} %get-tuple-element.28.step_ref, f32[4,8,128]{2,1,0:T(8,128)} %get-tuple-element.29.norm_ref, ...), custom_call_target="tpu_custom_call" | custom-call | tf_op jit(solution)/shard_map/analysis/pallas_call | solution.py:165
  111.6 2.5 %collective-permute-start.5 = (f32[9,8,128]{2,1,0:T(8,128)}, f32[9,8,128]{2,1,0:T(8,128)S(1)}, u32[]{:S(2)}, u32[]{:S(2)}) collective-permute-start(f32[9,8,128]{2,1,0:T(8,128)} %analysis.4.mine_ref), channel_id=1, source_target_pairs={{0,1},{1,0},{2,3},{3,2},{4,5},{5,4},{6,7},{7,6},{8,9},{9,8},{10,11... | collective-permute-start | bytes 110600 | tf_op jit(solution)/shard_map/ppermute | solution.py:539
  114.1 1.1 collective-permute-done.5.other_ref
  115.1 0.6 copy-done.7
  115.8 6.3 %second.1 = (f32[64,8,128]{2,1,0:T(8,128)}, f32[8,8,128]{2,1,0:T(8,128)}, f32[8,128]{1,0:T(8,128)}) custom-call(f32[9,8,128]{2,1,0:T(8,128)} %analysis.4.mine_ref, f32[9,8,128]{2,1,0:T(8,128)} %copy-done.7, f32[8,8,128]{2,1,0:T(8,128)} %bitcast.26, f32[8,8,128]{2,1,0:T(8,128)} %get-tuple-element.36.rhs_ref, f32[8,128]{1,0:T(8,128)} %get-tuple-element.37.told_ref, ...), custom_call_target="tpu_custom_call" | custom-call | tf_op jit(solution)/shard_map/second/pallas_call | solution.py:288
  122.1 15.3 %all_to_all.27.recv_ref = f32[64,8,128]{2,1,0:T(8,128)} all-to-all(f32[64,8,128]{2,1,0:T(8,128)} %get-tuple-element.38), channel_id=1, replica_groups=mesh['blk'=64,'rep'=2] {'blk'}, dimensions={0} | all-to-all | bytes 524288 | tf_op jit(solution)/shard_map/all_to_all | solution.py:546
  137.4 11.3 %map_two.1 = (f32[64,8,128]{2,1,0:T(8,128)}, f32[8,8,128]{2,1,0:T(8,128)}, f32[8,128]{1,0:T(8,128)}) custom-call(f32[64,8,128]{2,1,0:T(8,128)} %all_to_all.27.recv_ref, f32[64,8,128]{2,1,0:T(8,128)} %all_to_all.25.recv_ref.before_ref, f32[8,128]{1,0:T(8,128)} %get-tuple-element.37.told_ref, f32[8,8,128]{2,1,0:T(8,128)} %bitcast.27, ...), custom_call_target="tpu_custom_call" | custom-call | tf_op jit(solution)/shard_map/map_two/pallas_call | solution.py:524
  148.7 14.7 %all_to_all.28.recv_ref = f32[64,8,128]{2,1,0:T(8,128)} all-to-all(f32[64,8,128]{2,1,0:T(8,128)} %get-tuple-element.40), channel_id=1, replica_groups=mesh['blk'=64,'rep'=2] {'blk'}, dimensions={0} | all-to-all | bytes 524288 | tf_op jit(solution)/shard_map/all_to_all | solution.py:546
  163.4 8.3 %analysis.5.mine_ref = f32[9,8,128]{2,1,0:T(8,128)} custom-call(f32[64,8,128]{2,1,0:T(8,128)} %all_to_all.28.recv_ref, f32[4,2,8,1024]{3,2,1,0:T(8,128)} %pad_maximum_fusion.1.seeds_ref, f32[8,1024]{1,0:T(8,128)} %get-tuple-element.27.x_ref, f32[4,8,128]{2,1,0:T(8,128)} %get-tuple-element.28.step_ref, f32[4,8,128]{2,1,0:T(8,128)} %get-tuple-element.29.norm_ref, ...), custom_call_target="tpu_custom_call" | custom-call | tf_op jit(solution)/shard_map/analysis/pallas_call | solution.py:165
  171.6 2.5 %collective-permute-start.6 = (f32[9,8,128]{2,1,0:T(8,128)}, f32[9,8,128]{2,1,0:T(8,128)S(1)}, u32[]{:S(2)}, u32[]{:S(2)}) collective-permute-start(f32[9,8,128]{2,1,0:T(8,128)} %analysis.5.mine_ref), channel_id=1, source_target_pairs={{0,1},{1,0},{2,3},{3,2},{4,5},{5,4},{6,7},{7,6},{8,9},{9,8},{10,11... | collective-permute-start | bytes 110600 | tf_op jit(solution)/shard_map/ppermute | solution.py:539
  174.1 1.1 collective-permute-done.6.other_ref
  175.2 0.6 copy-done.5
  175.8 1.6 last.1
  177.4 0.7 constant_dynamic-slice_fusion
  178.1 0.6 copy.21
  178.7 0.6 copy.20
  (13 shorter events, 0.1 us)
Async XLA Ops:
  0.6 3.0 %copy-start = (f32[32,16384]{1,0:T(8,128)S(1)}, f32[32,16384]{1,0:T(8,128)}, u32[]{:S(2)}) copy-start(f32[32,16384]{1,0:T(8,128)} %sky_ref.1) | copy-start | bytes 6291460
  0.7 4.4 %copy-start.3 = (f32[8,2,2,2048]{3,2,1,0:T(2,128)S(1)}, f32[8,2,2,2048]{3,2,1,0:T(2,128)}, u32[]{:S(2)}) copy-start(f32[8,2,2,2048]{3,2,1,0:T(2,128)} %param.10) | copy-start | bytes 786436
  0.7 5.2 %copy-start.9 = (s32[512,2]{0,1:T(2,128)S(1)}, s32[512,2]{0,1:T(2,128)}, u32[]{:S(2)}) copy-start(s32[512,2]{0,1:T(2,128)} %param.12) | copy-start | bytes 12292
  0.7 5.3 %copy-start.10 = (s32[8]{0:T(128)S(1)}, s32[8]{0:T(128)}, u32[]{:S(2)}) copy-start(s32[8]{0:T(128)} %param.13) | copy-start | bytes 100
  0.7 9.0 %copy-start.8 = (f32[8,2,2,128]{3,2,1,0:T(2,128)S(1)}, f32[8,2,2,128]{3,2,1,0:T(2,128)}, u32[]{:S(2)}) copy-start(f32[8,2,2,128]{3,2,1,0:T(2,128)} %param.9) | copy-start | bytes 49156
  2.1 11.0 %collective-permute-start = (f32[16,16384]{1,0:T(8,128)S(1)}, f32[16,16384]{1,0:T(8,128)}, u32[]{:S(2)}, u32[]{:S(2)}) collective-permute-start(f32[16,16384]{1,0:T(8,128)S(1)} %constant_dynamic-slice_fusion.4), channel_id=1, source_target_pairs={{0,1},{1,0},{2,3},{3,2},{4,5},{5,4},{6,7},{7,6},{8,9},{9,8},{10,11... | collective-permute-start | bytes 3145736 | tf_op jit(solution)/shard_map/ppermute | solution.py:539
  4.7 8.4 %collective-permute-start.1 = (f32[16,16384]{1,0:T(8,128)}, f32[16,16384]{1,0:T(8,128)S(1)}, u32[]{:S(2)}, u32[]{:S(2)}) collective-permute-start(f32[16,16384]{1,0:T(8,128)} %constant_dynamic-slice_fusion.3), channel_id=1, source_target_pairs={{0,1},{1,0},{2,3},{3,2},{4,5},{5,4},{6,7},{7,6},{8,9},{9,8},{10,11... | collective-permute-start | bytes 3145736 | tf_op jit(solution)/shard_map/ppermute | solution.py:539
  9.5 24.3 %collective-permute-start.2 = (f32[2,2,8,1024]{3,2,1,0:T(8,128)}, f32[2,2,8,1024]{3,2,1,0:T(8,128)S(1)}, u32[]{:S(2)}, u32[]{:S(2)}) collective-permute-start(f32[2,2,8,1024]{3,2,1,0:T(8,128)} %get-tuple-element.26), channel_id=1, source_target_pairs={{0,1},{1,0},{2,3},{3,2},{4,5},{5,4},{6,7},{7,6},{8,9},{9,8},{10,11... | collective-permute-start | bytes 393224 | tf_op jit(solution)/shard_map/ppermute | solution.py:539
  9.7 3.3 %collective-permute-start.4 = (f32[2,2,8,128]{3,1,0,2:T(2,128)S(1)}, f32[2,2,8,128]{3,1,0,2:T(2,128)S(1)}, u32[]{:S(2)}, u32[]{:S(2)}) collective-permute-start(f32[2,2,8,128]{3,1,0,2:T(2,128)S(1)} %bitcast.32), channel_id=1, source_target_pairs={{0,1},{1,0},{2,3},{3,2},{4,5},{5,4},{6,7},{7,6},{8,9},{9,8},{10,11... | collective-permute-start | bytes 49160 | tf_op jit(solution)/shard_map/ppermute | solution.py:539
  13.1 20.8 %copy-start.4 = (f32[2,2,8,1024]{3,2,1,0:T(8,128)S(1)}, f32[2,2,8,1024]{3,2,1,0:T(8,128)}, u32[]{:S(2)}) copy-start(f32[2,2,8,1024]{3,2,1,0:T(8,128)} %get-tuple-element.25) | copy-start | bytes 393220
  13.1 1.1 copy-start.2
  22.6 21.1 %all-to-all-start = ((f32[64,8,128]{2,1,0:T(8,128)}), f32[64,8,128]{2,1,0:T(8,128)S(1)}, u32[]{:S(2)}, u32[]{:S(2)}) async-start(f32[64,8,128]{2,1,0:T(8,128)} %get-tuple-element.24), calls=%async_computation | async-start | bytes 524288 | tf_op jit(solution)/shard_map/all_to_all | solution.py:546
  43.7 0.7 copy-start.1
  52.7 2.6 %collective-permute-start.3 = (f32[9,8,128]{2,1,0:T(8,128)}, f32[9,8,128]{2,1,0:T(8,128)S(1)}, u32[]{:S(2)}, u32[]{:S(2)}) collective-permute-start(f32[9,8,128]{2,1,0:T(8,128)} %analysis.3.mine_ref), channel_id=1, source_target_pairs={{0,1},{1,0},{2,3},{3,2},{4,5},{5,4},{6,7},{7,6},{8,9},{9,8},{10,11... | collective-permute-start | bytes 110600 | tf_op jit(solution)/shard_map/ppermute | solution.py:539
  55.3 0.6 copy-start.6
  111.6 3.6 %collective-permute-start.5 = (f32[9,8,128]{2,1,0:T(8,128)}, f32[9,8,128]{2,1,0:T(8,128)S(1)}, u32[]{:S(2)}, u32[]{:S(2)}) collective-permute-start(f32[9,8,128]{2,1,0:T(8,128)} %analysis.4.mine_ref), channel_id=1, source_target_pairs={{0,1},{1,0},{2,3},{3,2},{4,5},{5,4},{6,7},{7,6},{8,9},{9,8},{10,11... | collective-permute-start | bytes 110600 | tf_op jit(solution)/shard_map/ppermute | solution.py:539
  115.1 0.6 copy-start.7
  171.6 3.6 %collective-permute-start.6 = (f32[9,8,128]{2,1,0:T(8,128)}, f32[9,8,128]{2,1,0:T(8,128)S(1)}, u32[]{:S(2)}, u32[]{:S(2)}) collective-permute-start(f32[9,8,128]{2,1,0:T(8,128)} %analysis.5.mine_ref), channel_id=1, source_target_pairs={{0,1},{1,0},{2,3},{3,2},{4,5},{5,4},{6,7},{7,6},{8,9},{9,8},{10,11... | collective-permute-start | bytes 110600 | tf_op jit(solution)/shard_map/ppermute | solution.py:539
  175.2 0.6 copy-start.5

commit v2 on v1

v2 whole, which is shorter than its diff:
```python
import functools
import math

import jax
import jax.numpy as jnp
from jax import lax
from jax.experimental import pallas as pl
from jax.experimental.pallas import tpu as pltpu
from jax.sharding import PartitionSpec as P

NPHI = 32768
NCOL = 1024
NPAIRS = 512
NBP = 4
RH = 16
CHIPS = 64
SECTION = 1024
HALF = SECTION // 2
OUTER = NPHI // SECTION
LOOPS = CHIPS * RH
GROUPS = LOOPS // 128
COARSE = 16
FINE = HALF // COARSE
SCALE = 2.0**-13
PERIOD = 2 * NPHI
F32 = jnp.float32
BF16 = jnp.bfloat16


def chip_at(group, place):
    return 8 * group + 4 * (place % 2) + place // 2


def split(value):
    high = value.astype(BF16)
    return high, (value - high.astype(F32)).astype(BF16)


def lanes(rows=8, width=128):
    return lax.broadcasted_iota(jnp.int32, (rows, width), 1)


LIMIT = 36 * 2**20
SMEM = pl.BlockSpec(memory_space=pltpu.SMEM)
VMEM = pl.BlockSpec(memory_space=pltpu.VMEM)
COEF = pltpu.VMEM((2 * NBP, 8, 128), F32)
SPECTRA = pltpu.VMEM((2 * NBP + 1, 8, 128), F32)
PAYLOAD = pltpu.VMEM((CHIPS, 8, 128), F32)
TILE = pltpu.VMEM((8, 128), F32)
ROWS = OUTER * RH
PIXELS = jax.ShapeDtypeStruct((ROWS, HALF), F32)
TABLE = pltpu.VMEM((2, HALF, NCOL), BF16)
PHASES = pltpu.VMEM((2, OUTER, NCOL), F32)


def held(*arrays):
    return [pltpu.with_memory_space_constraint(array, pltpu.VMEM) for array in arrays]


def far(*arrays):
    return [pltpu.with_memory_space_constraint(array, pltpu.HBM) for array in arrays]


def list_of(*arrays):
    return list(arrays)


def call(kernel, outs, scratch, name, arrays, scalars=0, hold=held):
    return pl.pallas_call(
        kernel,
        in_specs=[SMEM] * scalars + [VMEM] * (len(arrays) - scalars),
        out_specs=jax.tree.map(lambda _: VMEM, outs),
        out_shape=outs,
        scratch_shapes=scratch,
        compiler_params=pltpu.CompilerParams(vmem_limit_bytes=LIMIT),
        name=name,
    )(*arrays[:scalars], *hold(*arrays[scalars:]))


WIDE = LOOPS + 128


def prepare_kernel(
    place_ref, count_ref, seeds_ref, prior_ref, cos_ref, m_ref, keep_ref, send_ref, x_ref, step_ref, norm_ref, side_ref
):
    chip, rep = place_ref[0], place_ref[1]
    first = rep == 0
    low = (lanes() % 32) < 16

    def halves(near, far):
        zero = jnp.where(low, near, pltpu.roll(far, 16, 1))
        one = jnp.where(low, pltpu.roll(near, 112, 1), far)
        return jnp.where(first, zero, one), jnp.where(first, one, zero)

    for block in range(2):
        for which in range(2):
            row = prior_ref[:, block, which, :]
            keep_ref[block, which, :, LOOPS:] = row
            send_ref[block, which, :, LOOPS:] = row
            seed = seeds_ref[:, block, which, :]
            for group in range(GROUPS):
                at = 256 * group
                spot = slice(128 * group, 128 * group + 128)
                keep, send = halves(seed[:, at : at + 128], seed[:, at + 128 : at + 256])
                keep_ref[block, which, :, spot] = keep
                send_ref[block, which, :, spot] = send
    for group in range(GROUPS):
        at = 256 * group
        near = jnp.broadcast_to(cos_ref[:, at : at + 128], (8, 128))
        far = jnp.broadcast_to(cos_ref[:, at + 128 : at + 256], (8, 128))
        x_ref[:, 128 * group : 128 * group + 128] = halves(near, far)[0]

    lane = lanes()
    row = lax.broadcasted_iota(jnp.int32, (8, NPAIRS), 0)
    chosen = lax.broadcasted_iota(jnp.int32, (8, NPAIRS), 1) == 8 * chip + row

    def own_m(side):
        every = jnp.broadcast_to(m_ref[side : side + 1, :], (8, NPAIRS)).astype(F32)
        return jnp.broadcast_to(jnp.sum(jnp.where(chosen, every, 0.0), axis=1, keepdims=True), (8, 128))

    m_zero, m_one = own_m(0).astype(jnp.int32), own_m(1).astype(jnp.int32)
    pair = lax.broadcasted_iota(jnp.int32, (8, 128), 0)
    count = jnp.zeros((8, 128), jnp.int32)
    for p in range(8):
        count = jnp.where(pair == p, count_ref[p], count)

    def ladder(degree, column_m):
        ratio = column_m / degree
        return jnp.sqrt((4.0 - 1.0 / (degree * degree)) / ((1.0 - ratio) * (1.0 + ratio)))

    for block in range(NBP):
        real_block = jnp.where(block < 2, 2 * rep + block, 2 * (1 - rep) + block - 2)
        side = real_block >= count
        m_here = jnp.where(side, m_one, m_zero)
        offset = jnp.where(side, real_block - count, real_block)
        degree = 128 * (lax.shift_right_logical(17 * m_here, 11) + 1) + 128 * offset + lane
        column_m = m_here.astype(F32)
        now = ladder(degree.astype(F32), column_m)
        before = ladder((degree - 1).astype(F32), column_m)
        norm = jnp.where(lane < 2, 1.0, now / before)
        for shift in (2, 4, 8, 16, 32, 64):
            norm = norm * jnp.where(lane >= shift, pltpu.roll(norm, shift, 1), 1.0)
        step_ref[block] = now * pltpu.roll(norm, 1, 1) / norm
        norm_ref[block] = norm
        side_ref[block] = side.astype(F32)


def prepare(*arrays):
    small = pltpu.VMEM((NBP, 8, 128), F32)
    wide = pltpu.VMEM((2, 2, 8, WIDE), F32)
    return call(prepare_kernel, (wide, wide, pltpu.VMEM((8, LOOPS), F32), small, small, small), [], "prepare", arrays, 2, list_of)


def load_seeds(keep_ref, other_ref, seeds_ref):
    seeds_ref[0:2] = keep_ref[:, :, :, :LOOPS]
    seeds_ref[2:4] = other_ref[:, :, :, :LOOPS]


def load_prior(keep_ref, other_ref):
    return [ref[j, t, :, LOOPS:] for ref in (keep_ref, other_ref) for j in range(2) for t in range(2)]


def analysis_kernel(recv_ref, keep_ref, other_ref, x_ref, step_ref, norm_ref, side_ref, out_ref, spec_ref, seeds_ref, sums_ref, halves_ref):
    load_seeds(keep_ref, other_ref, seeds_ref)
    place = lanes() // 16
    tail = jnp.zeros((8, 128), F32)
    for group in range(GROUPS):
        made = [None] * 4
        for spot in range(8):
            tile = recv_ref[chip_at(group, spot)]
            tail = tail + tile
            for kind in range(4):
                turned = pltpu.roll(tile, ((spot - kind) * 16) % 128, 1) if spot != kind else tile
                made[kind] = turned if spot == 0 else jnp.where(place == spot, turned, made[kind])
        for kind in range(4):
            spec_ref[kind, group] = made[kind]
    out_ref[2 * NBP] = tail
    lane = lanes()
    even = {shift: (lane & shift) == 0 for shift in (1, 2, 4, 8, 16, 32, 64)}

    span = [slice(128 * g, 128 * g + 128) for g in range(GROUPS)]

    @pl.loop(0, NBP)
    def _(block):
        x = [x_ref[:, s] for s in span]
        older = [seeds_ref[block, 0, :, s] for s in span]
        newer = [seeds_ref[block, 1, :, s] for s in span]
        side = side_ref[block] > 0.5
        real = [jnp.where(side, spec_ref[1, g], spec_ref[0, g]) for g in range(GROUPS)]
        imag = [jnp.where(side, spec_ref[3, g], spec_ref[2, g]) for g in range(GROUPS)]
        steps = step_ref[block]

        def emit(rows, index):
            for part, values in enumerate((real, imag)):
                terms = [row * value for row, value in zip(rows, values)]
                while len(terms) > 1:
                    terms = [a + b for a, b in zip(terms[::2], terms[1::2])]
                sums_ref[2 * block + part, index] = terms[0]

        emit(older, 0)
        emit(newer, 1)
        for index in range(2, 128):
            factor = jnp.broadcast_to(steps[:, index : index + 1], (8, 128))
            fresh = [(factor * a) * b - c for a, b, c in zip(x, newer, older)]
            older, newer = newer, fresh
            emit(newer, index)

    source, target, left = sums_ref, halves_ref, 64
    while left:
        shift = 64 // left
        for row in range(2 * NBP):
            for index in range(left):
                first, second = source[row, 2 * index], source[row, 2 * index + 1]
                near = jnp.where(even[shift], first, second)
                far = jnp.where(even[shift], second, first)
                target[row, index] = near + pltpu.roll(far, 128 - shift, 1)
        source, target, left = target, source, left // 2
    for row in range(2 * NBP):
        out_ref[row] = source[row, 0] * norm_ref[row // 2]


LEGENDRE = [pltpu.VMEM((4, GROUPS, 8, 128), F32), pltpu.VMEM((NBP, 2, 8, LOOPS), F32)]


def analysis(*arrays):
    scratch = LEGENDRE + [pltpu.VMEM((2 * NBP, count, 8, 128), F32) for count in (128, 64)]
    return call(analysis_kernel, SPECTRA, scratch, "analysis", arrays)


def total_of(tile):
    return jnp.sum(jnp.sum(tile, axis=1, keepdims=True), axis=0, keepdims=True)


def lane_total(tile, lane):
    return total_of(jnp.where(lanes() == lane, tile, 0.0))


def synthesis(coef_ref, seeds_ref, x_ref, step_ref, norm_ref, side_ref, spec_ref, extra, out_ref):
    span = [slice(128 * g, 128 * g + 128) for g in range(GROUPS)]
    spec_ref[...] = jnp.zeros_like(spec_ref)

    @pl.loop(0, NBP)
    def _(block):
        x = [x_ref[:, s] for s in span]
        older = [seeds_ref[block, 0, :, s] for s in span]
        newer = [seeds_ref[block, 1, :, s] for s in span]
        steps = step_ref[block]
        norm = norm_ref[block]
        real = coef_ref[2 * block] * norm
        imag = coef_ref[2 * block + 1] * norm

        def spread(values, index):
            return jnp.broadcast_to(values[:, index : index + 1], (8, 128))

        sums_re = [spread(real, 0) * a + spread(real, 1) * b for a, b in zip(older, newer)]
        sums_im = [spread(imag, 0) * a + spread(imag, 1) * b for a, b in zip(older, newer)]
        for index in range(2, 128):
            factor = spread(steps, index)
            fresh = [(factor * a) * b - c for a, b, c in zip(x, newer, older)]
            older, newer = newer, fresh
            weight_re = spread(real, index)
            weight_im = spread(imag, index)
            sums_re = [s + weight_re * p for s, p in zip(sums_re, newer)]
            sums_im = [s + weight_im * p for s, p in zip(sums_im, newer)]
        side = side_ref[block] > 0.5
        for g in range(GROUPS):
            spec_ref[0, g] += jnp.where(side, 0.0, sums_re[g])
            spec_ref[1, g] += jnp.where(side, sums_re[g], 0.0)
            spec_ref[2, g] += jnp.where(side, 0.0, sums_im[g])
            spec_ref[3, g] += jnp.where(side, sums_im[g], 0.0)

    place = lanes() // 16
    for group in range(GROUPS):
        values = [spec_ref[kind, group] for kind in range(4)]
        for spot in range(8):
            tile = extra
            for kind in range(4):
                turned = pltpu.roll(values[kind], ((kind - spot) * 16) % 128, 1) if spot != kind else values[kind]
                tile = jnp.where(place == kind, turned, tile)
            out_ref[chip_at(group, spot)] = tile


def swapped(row):
    return (row + NBP) % (2 * NBP)


def sum_rows(terms):
    paired = [terms[row] + terms[swapped(row)] for row in range(NBP)]
    return (paired[0] + paired[1]) + (paired[2] + paired[3])


def first_kernel(
    mine_ref, theirs_ref, keep_ref, other_ref, x_ref, step_ref, norm_ref, side_ref, out_ref, rhs_ref, spec_ref, seeds_ref
):
    load_seeds(keep_ref, other_ref, seeds_ref)
    prior = load_prior(keep_ref, other_ref)
    rhs = [mine_ref[row] + theirs_ref[swapped(row)] for row in range(2 * NBP)]
    for row in range(2 * NBP):
        rhs_ref[row] = rhs[row]
    squares = sum_rows([value * value for value in rhs])
    energy = sum_rows([weight * value * value for weight, value in zip(prior, rhs)])
    lane = lanes()
    extra = jnp.where(lane == 64, jnp.sum(squares, axis=1, keepdims=True), 0.0)
    extra = jnp.where(lane == 65, jnp.sum(energy, axis=1, keepdims=True), extra)
    synthesis(rhs_ref, seeds_ref, x_ref, step_ref, norm_ref, side_ref, spec_ref, extra, out_ref)


def second_kernel(
    mine_ref, theirs_ref, rhs_ref, told_ref, keep_ref, other_ref, x_ref, step_ref, norm_ref, side_ref,
    out_ref, res_ref, alpha_ref, spec_ref, seeds_ref,
):
    load_seeds(keep_ref, other_ref, seeds_ref)
    prior = load_prior(keep_ref, other_ref)
    told = told_ref[...]
    norm_now = lane_total(told, 0) * 0.125
    energy = lane_total(told, 1) * 0.125
    pixels = lane_total(mine_ref[2 * NBP] + theirs_ref[2 * NBP], 64)
    alpha = norm_now / (energy + pixels)
    alpha_ref[...] = jnp.broadcast_to(alpha, (8, 128))
    residual = []
    for row in range(2 * NBP):
        image = prior[row] * rhs_ref[row] + (mine_ref[row] + theirs_ref[swapped(row)])
        residual.append(rhs_ref[row] - alpha * image)
        res_ref[row] = residual[row]
    squares = sum_rows([value * value for value in residual])
    extra = jnp.where(lanes() == 64, jnp.sum(squares, axis=1, keepdims=True), 0.0)
    synthesis(res_ref, seeds_ref, x_ref, step_ref, norm_ref, side_ref, spec_ref, extra, out_ref)


def last_kernel(
    mine_ref, theirs_ref, keep_ref, rhs_ref, res_ref, dir_ref, told_ref, alpha_ref, sol_ref, out_ref
):
    norm_now = lane_total(told_ref[...], 0) * 0.125
    energy = lane_total(mine_ref[2 * NBP], 65)
    pixels = lane_total(mine_ref[2 * NBP] + theirs_ref[2 * NBP], 64)
    alpha = norm_now / (energy + pixels)
    for block in range(2):
        for part in range(2):
            row = 2 * block + part
            image = keep_ref[block, part, :, LOOPS:] * dir_ref[row] + (mine_ref[row] + theirs_ref[swapped(row)])
            sol_ref[:, block, part, :] = alpha_ref[...] * rhs_ref[row] + alpha * dir_ref[row]
            out_ref[:, block, part, :] = res_ref[row] - alpha * image


def first_step(*arrays):
    return call(first_kernel, (PAYLOAD, COEF), LEGENDRE, "first", arrays)


def second_step(*arrays):
    return call(second_kernel, (PAYLOAD, COEF, TILE), LEGENDRE, "second", arrays)


def last_step(*arrays):
    result = jax.ShapeDtypeStruct((8, 2, 2, 128), F32)
    return call(last_kernel, (result, result), [], "last", arrays)


CHUNK = 256


def dot3(left, right_ref, spot):
    high, low = left
    return (
        jnp.dot(high, right_ref[0, :, spot], preferred_element_type=F32)
        + jnp.dot(low, right_ref[0, :, spot], preferred_element_type=F32)
        + jnp.dot(high, right_ref[1, :, spot], preferred_element_type=F32)
    )


def dot3_turned(left, right_ref, spot):
    high, low = left
    dims = (((1,), (1,)), ((), ()))
    return (
        lax.dot_general(high, right_ref[0, spot, :], dims, preferred_element_type=F32)
        + lax.dot_general(low, right_ref[0, spot, :], dims, preferred_element_type=F32)
        + lax.dot_general(high, right_ref[1, spot, :], dims, preferred_element_type=F32)
    )


def to_columns(even, odd, cos_ref, sin_ref, phase_ref, extra, out_ref):
    parts = [[], []]
    for at in range(0, NCOL, CHUNK):
        spot = slice(at, at + CHUNK)
        along = dot3(even, cos_ref, spot).reshape(OUTER, RH, CHUNK)
        across = dot3(odd, sin_ref, spot).reshape(OUTER, RH, CHUNK)
        real = jnp.zeros((RH, CHUNK), F32)
        imag = jnp.zeros((RH, CHUNK), F32)
        for section in range(OUTER):
            cos = phase_ref[0, section : section + 1, spot]
            sin = phase_ref[1, section : section + 1, spot]
            real = real + (cos * along[section] - sin * across[section])
            imag = imag - (cos * across[section] + sin * along[section])
        parts[0].append(real)
        parts[1].append(imag)
    rows = []
    for part in parts:
        whole = jnp.concatenate(part, axis=1)
        rows += [whole[:, :NPAIRS], whole[:, NPAIRS:]]
    whole = jnp.concatenate(rows + [extra, jnp.zeros((56, NPAIRS), F32)], axis=0)
    for at in range(0, NPAIRS, 128):
        turned = jnp.transpose(whole[:, at : at + 128])
        out_ref[at // 8 : at // 8 + 16] = turned.reshape(16, 8, 128)


def circle(cycles):
    quarter = lax.shift_right_logical(cycles + PERIOD // 8, 14)
    angle = (cycles - quarter * (PERIOD // 4)).astype(F32) * (2.0 * math.pi / PERIOD)
    square = angle * angle
    sin = angle * (1.0 + square * (-1 / 6 + square * (1 / 120 + square * (-1 / 5040 + square * (1 / 362880)))))
    cos = 1.0 + square * (-0.5 + square * (1 / 24 + square * (-1 / 720 + square * (1 / 40320))))
    odd = (quarter & 1) == 1
    cos, sin = jnp.where(odd, sin, cos), jnp.where(odd, cos, sin)
    cos = jnp.where((quarter == 1) | (quarter == 2), -cos, cos)
    sin = jnp.where((quarter == 2) | (quarter == 3), -sin, sin)
    return cos, sin


def table_kernel(place_ref, m_ref, cos_ref, sin_ref, phase_ref):
    rep = place_ref[1]
    every_m = jnp.concatenate([m_ref[0:1, :], m_ref[1:2, :]], axis=1)

    def angles(rows, factor):
        return circle((factor(lax.broadcasted_iota(jnp.int32, (rows, NCOL), 0)) * every_m) & (PERIOD - 1))

    c_coarse, s_coarse = angles(COARSE, lambda row: 2 * FINE * row)
    c_fine, s_fine = angles(FINE, lambda row: 2 * row + 1)
    for row in range(COARSE):
        c_one, s_one = c_coarse[row : row + 1], s_coarse[row : row + 1]
        spot = slice(FINE * row, FINE * row + FINE)
        high, low = split(c_one * c_fine - s_one * s_fine)
        cos_ref[0, spot, :] = high
        cos_ref[1, spot, :] = low
        high, low = split(s_one * c_fine + c_one * s_fine)
        sin_ref[0, spot, :] = high
        sin_ref[1, spot, :] = low

    def centre(row):
        section = (row + OUTER // 2 * rep) & (OUTER - 1)
        return 2 * SECTION * section + SECTION - 1

    cos, sin = angles(OUTER, centre)
    phase_ref[0] = cos
    phase_ref[1] = sin


def tables(*arrays):
    return call(table_kernel, (TABLE, TABLE, PHASES), [], "tables", arrays, 1)


def folded(ref, offset):
    count = OUTER // 2
    return jnp.concatenate([ref[:, SECTION * b + offset : SECTION * b + offset + HALF] for b in range(count)], axis=0)


def turned(rows):
    down = lax.broadcasted_iota(jnp.int32, (256, 256), 0)
    along = lax.broadcasted_iota(jnp.int32, (256, 256), 1)
    flip = jnp.where(down + along == 255, 1.0, 0.0).astype(BF16)
    pieces = []
    for at in (256, 0):
        high, low = split(rows[:, at : at + 256])
        pieces.append(jnp.dot(high, flip, preferred_element_type=F32) + jnp.dot(low, flip, preferred_element_type=F32))
    return jnp.concatenate(pieces, axis=1)


def sky_kernel(
    rep_ref, noise_ref, sky_ref, heavy_ref, cos_ref, sin_ref, phase_ref, out_ref, even_ref, odd_ref, mine_ref
):
    mine_ref[...] = noise_ref[...] * sky_ref[...]
    for half, ref in enumerate((mine_ref, heavy_ref)):
        spot = slice(half * ROWS // 2, (half + 1) * ROWS // 2)
        ahead = folded(ref, HALF) * SCALE
        back = turned(folded(ref, 0)) * SCALE
        high, low = split(ahead + back)
        even_ref[0, spot, :] = high
        even_ref[1, spot, :] = low
        high, low = split(ahead - back)
        odd_ref[0, spot, :] = high
        odd_ref[1, spot, :] = low
    to_columns(
        (even_ref[0], even_ref[1]), (odd_ref[0], odd_ref[1]), cos_ref, sin_ref, phase_ref,
        jnp.zeros((8, NPAIRS), F32), out_ref,
    )


def noise_kernel(rep_ref, noise_ref, other_ref, plus_ref, minus_ref):
    for half, ref in enumerate((noise_ref, other_ref)):
        spot = slice(half * ROWS // 2, (half + 1) * ROWS // 2)
        plus_ref[spot, :] = folded(ref, HALF) * (SCALE * SCALE)
        minus_ref[spot, :] = turned(folded(ref, 0)) * (SCALE * SCALE)


OWN = pl.BlockSpec((RH, NPHI // 2), lambda i, rep: (rep[0], 0))


def sky_step(rep, noise, sky, heavy, cos, sin, phases):
    half = pltpu.VMEM((2, ROWS, HALF), BF16)
    return pl.pallas_call(
        sky_kernel,
        grid_spec=pltpu.PrefetchScalarGridSpec(
            num_scalar_prefetch=1,
            grid=(1,),
            in_specs=[OWN, OWN, VMEM, VMEM, VMEM, VMEM],
            out_specs=VMEM,
            scratch_shapes=[half, half, pltpu.VMEM((RH, NPHI // 2), F32)],
        ),
        out_shape=PAYLOAD,
        compiler_params=pltpu.CompilerParams(vmem_limit_bytes=LIMIT),
        name="sky",
    )(rep, *far(noise, sky), *held(heavy, cos, sin, phases))


def noise_step(rep, noise, other):
    return pl.pallas_call(
        noise_kernel,
        grid_spec=pltpu.PrefetchScalarGridSpec(
            num_scalar_prefetch=1, grid=(1,), in_specs=[OWN, VMEM], out_specs=(VMEM, VMEM)
        ),
        out_shape=(PIXELS, PIXELS),
        compiler_params=pltpu.CompilerParams(vmem_limit_bytes=LIMIT),
        name="noise",
    )(rep, *far(noise), *held(other))


def by_rows(recv_ref):
    flat = recv_ref[...].reshape(NPAIRS, 128)
    return jnp.concatenate([jnp.transpose(flat[at : at + 128]) for at in range(0, NPAIRS, 128)], axis=1)


def fetch(places, holders, sems):
    copies = [pltpu.make_async_copy(a, b, sems.at[i]) for i, (a, b) in enumerate(zip(places, holders))]
    for copy in copies:
        copy.start()
    return copies


def through_map(rows, energy, copies, holders, phase_ref, out_ref, mixed_ref, even_ref, odd_ref):
    cos_ref, sin_ref, plus_ref, minus_ref = holders
    real = jnp.concatenate([rows[0:RH], rows[RH : 2 * RH]], axis=1)
    imag = jnp.concatenate([rows[2 * RH : 3 * RH], rows[3 * RH : 4 * RH]], axis=1)
    for section in range(OUTER):
        cos = phase_ref[0, section : section + 1, :]
        sin = phase_ref[1, section : section + 1, :]
        spot = slice(section * RH, section * RH + RH)
        high, low = split(real * cos - imag * sin)
        mixed_ref[0, spot, :] = high
        mixed_ref[1, spot, :] = low
        high, low = split(real * sin + imag * cos)
        mixed_ref[2, spot, :] = high
        mixed_ref[3, spot, :] = low
    spots = [slice(at, at + CHUNK) for at in range(0, HALF, CHUNK)]
    evens = [dot3_turned((mixed_ref[0], mixed_ref[1]), cos_ref, spot) for spot in spots]
    copies[0].wait()
    odds = [dot3_turned((mixed_ref[2], mixed_ref[3]), sin_ref, spot) for spot in spots]
    copies[1].wait()
    copies[2].wait()
    power = jnp.zeros((ROWS, 128), F32)
    for spot, even, odd in zip(spots, evens, odds):
        ahead = even - odd
        back = even + odd
        heavy_ahead = plus_ref[:, spot] * ahead
        heavy_back = minus_ref[:, spot] * back
        terms = heavy_ahead * ahead + heavy_back * back
        for piece in range(0, CHUNK, 128):
            power = power + terms[:, piece : piece + 128]
        high, low = split(heavy_ahead + heavy_back)
        even_ref[0, :, spot] = high
        even_ref[1, :, spot] = low
        high, low = split(heavy_ahead - heavy_back)
        odd_ref[0, :, spot] = high
        odd_ref[1, :, spot] = low
    pixels = total_of(power)
    lane = lanes(8, NPAIRS)
    row = lax.broadcasted_iota(jnp.int32, (8, NPAIRS), 0)
    extra = jnp.where((lane % 8 == 0) & (row == 0), pixels, 0.0)
    extra = jnp.where((lane % 8 == 0) & (row == 1), energy, extra)
    to_columns((even_ref[0], even_ref[1]), (odd_ref[0], odd_ref[1]), cos_ref, sin_ref, phase_ref, extra, out_ref)


def row_total(rows, index):
    return jnp.sum(rows[index : index + 1], axis=1, keepdims=True)


def map_one_kernel(
    recv_ref, phase_ref, cos_ref, sin_hbm, plus_hbm, minus_hbm,
    out_ref, told_ref, mixed_ref, even_ref, odd_ref, sin_ref, plus_ref, minus_ref, sems,
):
    holders = (cos_ref, sin_ref, plus_ref, minus_ref)
    copies = fetch((sin_hbm, plus_hbm, minus_hbm), holders[1:], sems)
    rows = by_rows(recv_ref)
    lane = lanes()
    told = jnp.where(lane == 0, row_total(rows, 64), 0.0)
    told_ref[...] = jnp.where(lane == 1, row_total(rows, 65), told)
    through_map(rows, jnp.zeros((1, 1), F32), copies, holders, phase_ref, out_ref, mixed_ref, even_ref, odd_ref)


def map_two_kernel(
    recv_ref, before_ref, told_ref, keep_ref, other_ref, rhs_ref, res_ref, phase_ref, cos_ref, sin_hbm, plus_hbm, minus_hbm,
    out_ref, dir_ref, told_out_ref, mixed_ref, even_ref, odd_ref, sin_ref, plus_ref, minus_ref, sems,
):
    holders = (cos_ref, sin_ref, plus_ref, minus_ref)
    copies = fetch((sin_hbm, plus_hbm, minus_hbm), holders[1:], sems)
    rows = by_rows(recv_ref)
    norm_next = row_total(rows, 64)
    beta = norm_next / (lane_total(told_ref[...], 0) * 0.125)
    told_out_ref[...] = jnp.where(lanes() == 0, norm_next, 0.0)
    prior = load_prior(keep_ref, other_ref)
    terms = []
    for row in range(2 * NBP):
        value = res_ref[row] + beta * rhs_ref[row]
        dir_ref[row] = value
        terms.append(prior[row] * value * value)
    energy = sum_rows(terms)
    rows = rows + beta * by_rows(before_ref)
    through_map(rows, total_of(energy), copies, holders, phase_ref, out_ref, mixed_ref, even_ref, odd_ref)


def map_call(kernel, outs, name, arrays, tables_and_noise):
    half = pltpu.VMEM((2, ROWS, HALF), BF16)
    return pl.pallas_call(
        kernel,
        in_specs=[VMEM] * len(arrays) + [pl.BlockSpec(memory_space=pl.ANY)] * 3,
        out_specs=jax.tree.map(lambda _: VMEM, outs),
        out_shape=outs,
        scratch_shapes=[
            pltpu.VMEM((4, ROWS, NCOL), BF16), half, half,
            pltpu.VMEM((2, HALF, NCOL), BF16),
            pltpu.VMEM((ROWS, HALF), F32), pltpu.VMEM((ROWS, HALF), F32),
            pltpu.SemaphoreType.DMA((3,)),
        ],
        compiler_params=pltpu.CompilerParams(vmem_limit_bytes=LIMIT),
        name=name,
    )(*held(*arrays), *far(*tables_and_noise))


def map_one(*arrays):
    return map_call(map_one_kernel, (PAYLOAD, TILE), "map_one", arrays[:-3], arrays[-3:])


def map_two(*arrays):
    return map_call(map_two_kernel, (PAYLOAD, COEF, TILE), "map_two", arrays[:-3], arrays[-3:])


def shards(sky_map, noise_weight, prior_weight, seeds, loop_cos, pair_m, block_count):
    rep = lax.axis_index("rep")
    rep_array = jnp.reshape(rep, (1,)).astype(jnp.int32)
    place = jnp.stack([lax.axis_index("blk"), rep]).astype(jnp.int32)

    def swap(value):
        return lax.ppermute(value, "rep", [(0, 1), (1, 0)])

    def transpose(payload):
        return lax.all_to_all(payload, "blk", split_axis=0, concat_axis=0, tiled=True)

    away = RH * (1 - rep)
    noise_away = lax.dynamic_slice_in_dim(noise_weight, away, RH, 0)
    heavy = swap(noise_away * lax.dynamic_slice_in_dim(sky_map, away, RH, 0))
    every_m = jnp.transpose(pair_m)
    cos, sin, phases = tables(place, every_m)
    fourier = (cos, sin, phases)
    payload = sky_step(rep_array, noise_weight, sky_map, heavy, *fourier)
    recv = transpose(payload)

    payload, place, noise_away = lax.optimization_barrier((payload, place, noise_away))
    plus, minus = noise_step(rep_array, noise_weight, swap(noise_away))
    keep, send, x, step, norm, side = prepare(place, block_count, seeds, prior_weight, loop_cos[None, :], every_m)
    other = swap(send)
    legendre = (keep, other, x, step, norm, side)

    recv, plus, minus = lax.optimization_barrier((recv, plus, minus))
    here = analysis(recv, *legendre)
    payload, rhs = first_step(here, swap(here), *legendre)
    before = transpose(payload)
    payload, told = map_one(before, phases, cos, sin, plus, minus)
    here = analysis(transpose(payload), *legendre)
    payload, residual, alpha = second_step(here, swap(here), rhs, told, *legendre)
    payload, direction, told = map_two(
        transpose(payload), before, told, keep, other, rhs, residual, phases, cos, sin, plus, minus
    )
    here = analysis(transpose(payload), *legendre)
    return last_step(here, swap(here), keep, rhs, residual, direction, told, alpha)


def solution(mesh):
    placed = (
        P("blk", "rep"),
        P("blk", "rep"),
        P("blk", "rep", None, None),
        P("blk", "rep", None, None),
        P(),
        P(),
        P("blk"),
    )
    return jax.shard_map(
        shards,
        mesh=mesh,
        in_specs=placed,
        out_specs=(P("blk", "rep", None, None), P("blk", "rep", None, None)),
        check_vma=False,
    )
```

time: 180 us -> 146 us (0.81)
  Pallas kernels: 71.8 us -> 54.6 us
  local copies, waits for them, and re-layouts: 11 us -> 1.99 us
  waiting for transfers between devices: 11.6 us -> 7.36 us
  blocking collectives: 60.2 us -> 56.1 us
    pallas_call x9 -> x11, Pallas kernels: 63.4 us -> 48.1 us  [the longest x8 29.9 us: call(): pl.pallas_call(kernel, in_specs=[SMEM] * scalars + [VMEM] * (len(arrays)...]
    all_to_all x1, waiting for transfers between devices: 9.03 us -> 4.12 us  [transpose(): lax.all_to_all(payload, 'blk', split_axis=0, concat_axis=0, tiled=True)]
    all_to_all x4, blocking collectives: 60.2 us -> 56.1 us  [transpose(): lax.all_to_all(payload, 'blk', split_axis=0, concat_axis=0, tiled=True)]
    dynamic_slice x4 -> x0, local copies, waits for them, and re-layouts: 3.31 us -> none  [the longest x1 1.45 us: shards(): noise_other = swap(lax.dynamic_slice_in_dim(noise_weight, away, RH, 0))]
    unnamed x26 -> x16, local copies, waits for them, and re-layouts: 5.03 us -> 1.99 us
    dynamic_slice x0 -> x1, other arithmetic: none -> 2.98 us  [shards(): noise_away = lax.dynamic_slice_in_dim(noise_weight, away, RH, 0)]
    broadcast_in_dim x4 -> x0, local copies, waits for them, and re-layouts: 2.03 us -> none  [the longest x1 0.68 us: shards(): jnp.broadcast_to(column_m[:, :, None], wide)]
    pallas_call x1, Pallas kernels: 8.44 us -> 6.52 us  [sky_step(): pl.pallas_call(sky_kernel, grid_spec=pltpu.PrefetchScalarGridSpec(num_sca...]
  transfers between devices with their start and end apart: 8 -> 7, of which waited for: 4 -> 5; matrix products, arithmetic and copies ran while one was open for 4% -> 0% of each run, Pallas kernels for 6% -> 4%
where the time goes in v2:
time: 146 us; the launch traced here: 145 us
  blocking collectives  56.1 us (38%)
  Pallas kernels  54.6 us (37%)
  starting transfers between devices  21.4 us (15%)
  waiting for transfers between devices  7.36 us (5%)
  other arithmetic  3.05 us (2%)
  local copies, waits for them, and re-layouts  1.99 us (1%)
    all_to_all x4, blocking collectives, transpose(): lax.all_to_all(payload, 'blk', split_axis=0, concat_axis=0, tiled=True)  56.1 us
    pallas_call x8, Pallas kernels, call(): pl.pallas_call(kernel, in_specs=[SMEM] * scalars + [VMEM] * (len(arrays)...  29.9 us
    pallas_call x2, Pallas kernels, map_call(): pl.pallas_call(kernel, in_specs=[VMEM] * len(arrays) + [pl.BlockSpec(memo...  16.1 us
    all_to_all x1, starting transfers between devices, transpose(): lax.all_to_all(payload, 'blk', split_axis=0, concat_axis=0, tiled=True)  11.2 us
    ppermute x6, starting transfers between devices, swap(): return lax.ppermute(value, 'rep', [(0, 1), (1, 0)])  10.2 us
    pallas_call x1, Pallas kernels, sky_step(): pl.pallas_call(sky_kernel, grid_spec=pltpu.PrefetchScalarGridSpec(num_sca...  6.52 us
    all_to_all x1, waiting for transfers between devices, transpose(): lax.all_to_all(payload, 'blk', split_axis=0, concat_axis=0, tiled=True)  4.12 us
    ppermute x6, waiting for transfers between devices, swap(): return lax.ppermute(value, 'rep', [(0, 1), (1, 0)])  3.24 us
  transfers between devices with their start and end apart: 7, of which 5 were waited for; matrix products, arithmetic and copies ran while one was open for 0% of the time, Pallas kernels for 4%

profile of v2, /device:TPU:1, one launch (start us, length us, event | category | flops | bytes accessed | tf_op | source)
XLA Modules:
  0.0 145.2 jit_solution(3612054615005072191)
XLA Ops:
  0.6 0.0 copy-start.4
  0.6 3.0 %constant_dynamic-slice_fusion = (f32[16,16384]{1,0:T(8,128)}, f32[16,16384]{1,0:T(8,128)}) fusion(f32[32,16384]{1,0:T(8,128)} %noise_ref.3, s32[]{:T(128)S(6)} %select_n.4, f32[32,16384]{1,0:T(8,128)} %sky_ref.1), kind=kLoop, calls=%fused_computation.2 | loop fusion | flops 262144 | bytes 4194308 | tf_op jit(solution)/shard_map/dynamic_slice | solution.py:656
  3.6 1.4 collective-permute-start
  5.0 0.1 pad_add_fusion.place_ref
  5.1 0.0 copy-done.4
  5.1 1.9 %tables.1 = (bf16[2,512,1024]{2,1,0:T(8,128)(2,1)S(1)}, bf16[2,512,1024]{2,1,0:T(8,128)(2,1)S(1)}, f32[2,32,1024]{2,1,0:T(8,128)S(1)}) custom-call(s32[2]{0:T(128)S(1)} %pad_add_fusion.place_ref, s32[2,512]{1,0:T(2,128)S(1)} %bitcast.4), custom_call_target="tpu_custom_call" | custom-call | tf_op jit(solution)/shard_map/tables/pallas_call | solution.py:69
  7.0 0.0 copy-start
  7.0 0.6 collective-permute-done.heavy_ref
  7.7 0.0 copy-start.3
  7.7 0.0 copy-start.5
  7.7 0.0 copy-start.6
  7.7 0.0 copy-start.7
  7.7 6.5 %sky.1 = f32[64,8,128]{2,1,0:T(8,128)} custom-call(s32[1]{0:T(128)} %bitcast.rep_ref, f32[32,16384]{1,0:T(8,128)} %noise_ref.3, f32[32,16384]{1,0:T(8,128)} %sky_ref.1, f32[16,16384]{1,0:T(8,128)} %collective-permute-done.heavy_ref, bf16[2,512,1024]{2,1,0:T(8,128)(2,1)S(1)} %get-tuple-element.28.cos_ref, ...), custom_call_target="tpu_custom_call" | custom-call | tf_op jit(solution)/shard_map/sky/pallas_call | solution.py:498
  14.2 0.0 copy-done
  14.2 0.3 collective-permute-start.1
  14.5 11.2 %all-to-all-start = ((f32[64,8,128]{2,1,0:T(8,128)}), f32[64,8,128]{2,1,0:T(8,128)S(1)}, u32[]{:S(2)}, u32[]{:S(2)}) async-start(f32[64,8,128]{2,1,0:T(8,128)} %sky.1), calls=%async_computation | async-start | bytes 524288 | tf_op jit(solution)/shard_map/all_to_all | solution.py:653
  25.8 0.0 copy-done.3
  25.8 0.0 copy-done.5
  25.8 0.0 copy-done.6
  25.8 0.0 copy-done.7
  25.8 1.2 prepare.1
  27.0 0.5 collective-permute-start.2
  27.5 0.0 collective-permute-done.1.other_ref
  27.5 2.0 %noise.1 = (f32[512,512]{1,0:T(8,128)S(1)}, f32[512,512]{1,0:T(8,128)S(1)}) custom-call(s32[1]{0:T(128)} %bitcast.rep_ref, f32[32,16384]{1,0:T(8,128)} %noise_ref.3, f32[16,16384]{1,0:T(8,128)} %collective-permute-done.1.other_ref), custom_call_target="tpu_custom_call" | custom-call | tf_op jit(solution)/shard_map/noise/pallas_call | solution.py:514
  29.6 0.0 copy-start.1
  29.6 1.0 copy-done.1
  30.5 0.0 copy-start.2
  30.5 1.0 copy-done.2
  31.5 4.1 %all-to-all-done.recv_ref = f32[64,8,128]{2,1,0:T(8,128)S(1)} async-done(((f32[64,8,128]{2,1,0:T(8,128)}), f32[64,8,128]{2,1,0:T(8,128)S(1)}, u32[]{:S(2)}, u32[]{:S(2)}) %all-to-all-start) | async-done | bytes 262176 | tf_op jit(solution)/shard_map/all_to_all | solution.py:653
  35.7 0.0 collective-permute-done.2.other_ref
  35.7 5.6 %analysis.3.mine_ref = f32[9,8,128]{2,1,0:T(8,128)S(1)} custom-call(f32[64,8,128]{2,1,0:T(8,128)S(1)} %all-to-all-done.recv_ref, f32[2,2,8,1152]{3,2,1,0:T(8,128)S(1)} %get-tuple-element.36.keep_ref, f32[2,2,8,1152]{3,2,1,0:T(8,128)S(1)} %collective-permute-done.2.other_ref, f32[8,1024]{1,0:T(8,128)S(1)} %get-tuple-element.38.x_ref, ...), custom_call_target="tpu_custom_call" | custom-call | tf_op jit(solution)/shard_map/analysis/pallas_call | solution.py:69
  41.3 1.6 %collective-permute-start.3 = (f32[9,8,128]{2,1,0:T(8,128)S(1)}, f32[9,8,128]{2,1,0:T(8,128)S(1)}, u32[]{:S(2)}, u32[]{:S(2)}) collective-permute-start(f32[9,8,128]{2,1,0:T(8,128)S(1)} %analysis.3.mine_ref), channel_id=1, source_target_pairs={{0,1},{1,0},{2,3},{3,2},{4,5},{5,4},{6,7},{7,6},{8,9},{9,8},{10,11... | collective-permute-start | bytes 110600 | tf_op jit(solution)/shard_map/ppermute | solution.py:650
  42.9 0.9 collective-permute-done.3.theirs_ref
  43.7 4.5 %first.1 = (f32[64,8,128]{2,1,0:T(8,128)S(1)}, f32[8,8,128]{2,1,0:T(8,128)S(1)}) custom-call(f32[9,8,128]{2,1,0:T(8,128)S(1)} %analysis.3.mine_ref, f32[9,8,128]{2,1,0:T(8,128)S(1)} %collective-permute-done.3.theirs_ref, f32[2,2,8,1152]{3,2,1,0:T(8,128)S(1)} %get-tuple-element.36.keep_ref, f32[2,2,8,1152]{3,2,1,0:T(8,128)S(1)} %collective-permute-done.2.other_ref, ...), custom_call_target="tpu_custom_call" | custom-call | tf_op jit(solution)/shard_map/first/pallas_call | solution.py:69
  48.3 14.3 %all_to_all.25.recv_ref.before_ref = f32[64,8,128]{2,1,0:T(8,128)S(1)} all-to-all(f32[64,8,128]{2,1,0:T(8,128)S(1)} %get-tuple-element.42), channel_id=1, replica_groups=mesh['blk'=64,'rep'=2] {'blk'}, dimensions={0} | all-to-all | bytes 524288 | tf_op jit(solution)/shard_map/all_to_all | solution.py:653
  62.6 8.0 %map_one.1 = (f32[64,8,128]{2,1,0:T(8,128)S(1)}, f32[8,128]{1,0:T(8,128)S(1)}) custom-call(f32[64,8,128]{2,1,0:T(8,128)S(1)} %all_to_all.25.recv_ref.before_ref, f32[2,32,1024]{2,1,0:T(8,128)S(1)} %get-tuple-element.30.phase_ref, bf16[2,512,1024]{2,1,0:T(8,128)(2,1)S(1)} %get-tuple-element.28.cos_ref, bf16[2,512,1024]{2,1,0:T(8,128)(2,1)} %copy-done, ...), custom_call_target="tpu_custom_call" | custom-call | tf_op jit(solution)/shard_map/map_one/pallas_call | solution.py:620
  70.6 13.8 %all_to_all.26.recv_ref = f32[64,8,128]{2,1,0:T(8,128)S(1)} all-to-all(f32[64,8,128]{2,1,0:T(8,128)S(1)} %get-tuple-element.45), channel_id=1, replica_groups=mesh['blk'=64,'rep'=2] {'blk'}, dimensions={0} | all-to-all | bytes 524288 | tf_op jit(solution)/shard_map/all_to_all | solution.py:653
  84.4 5.6 %analysis.4.mine_ref = f32[9,8,128]{2,1,0:T(8,128)S(1)} custom-call(f32[64,8,128]{2,1,0:T(8,128)S(1)} %all_to_all.26.recv_ref, f32[2,2,8,1152]{3,2,1,0:T(8,128)S(1)} %get-tuple-element.36.keep_ref, f32[2,2,8,1152]{3,2,1,0:T(8,128)S(1)} %collective-permute-done.2.other_ref, f32[8,1024]{1,0:T(8,128)S(1)} %get-tuple-element.38.x_ref, ...), custom_call_target="tpu_custom_call" | custom-call | tf_op jit(solution)/shard_map/analysis/pallas_call | solution.py:69
  90.1 3.1 %collective-permute-start.4 = (f32[9,8,128]{2,1,0:T(8,128)S(1)}, f32[9,8,128]{2,1,0:T(8,128)S(1)}, u32[]{:S(2)}, u32[]{:S(2)}) collective-permute-start(f32[9,8,128]{2,1,0:T(8,128)S(1)} %analysis.4.mine_ref), channel_id=1, source_target_pairs={{0,1},{1,0},{2,3},{3,2},{4,5},{5,4},{6,7},{7,6},{8,9},{9,8},{10,11... | collective-permute-start | bytes 110600 | tf_op jit(solution)/shard_map/ppermute | solution.py:650
  93.2 0.9 collective-permute-done.4.theirs_ref
  94.0 4.6 %second.1 = (f32[64,8,128]{2,1,0:T(8,128)S(1)}, f32[8,8,128]{2,1,0:T(8,128)S(1)}, f32[8,128]{1,0:T(8,128)S(1)}) custom-call(f32[9,8,128]{2,1,0:T(8,128)S(1)} %analysis.4.mine_ref, f32[9,8,128]{2,1,0:T(8,128)S(1)} %collective-permute-done.4.theirs_ref, f32[8,8,128]{2,1,0:T(8,128)S(1)} %get-tuple-element.46.rhs_ref, f32[8,128]{1,0:T(8,128)S(1)} %get-tuple-element.47.told_ref, ...), custom_call_target="tpu_custom_call" | custom-call | tf_op jit(solution)/shard_map/second/pallas_call | solution.py:69
  98.7 13.9 %all_to_all.27.recv_ref = f32[64,8,128]{2,1,0:T(8,128)S(1)} all-to-all(f32[64,8,128]{2,1,0:T(8,128)S(1)} %get-tuple-element.48), channel_id=1, replica_groups=mesh['blk'=64,'rep'=2] {'blk'}, dimensions={0} | all-to-all | bytes 524288 | tf_op jit(solution)/shard_map/all_to_all | solution.py:653
  112.6 8.1 %map_two.1 = (f32[64,8,128]{2,1,0:T(8,128)S(1)}, f32[8,8,128]{2,1,0:T(8,128)S(1)}, f32[8,128]{1,0:T(8,128)S(1)}) custom-call(f32[64,8,128]{2,1,0:T(8,128)S(1)} %all_to_all.27.recv_ref, f32[64,8,128]{2,1,0:T(8,128)S(1)} %all_to_all.25.recv_ref.before_ref, f32[8,128]{1,0:T(8,128)S(1)} %get-tuple-element.47.told_ref, ...), custom_call_target="tpu_custom_call" | custom-call | tf_op jit(solution)/shard_map/map_two/pallas_call | solution.py:620
  120.7 14.1 %all_to_all.28.recv_ref = f32[64,8,128]{2,1,0:T(8,128)S(1)} all-to-all(f32[64,8,128]{2,1,0:T(8,128)S(1)} %get-tuple-element.50), channel_id=1, replica_groups=mesh['blk'=64,'rep'=2] {'blk'}, dimensions={0} | all-to-all | bytes 524288 | tf_op jit(solution)/shard_map/all_to_all | solution.py:653
  134.8 5.6 %analysis.5.mine_ref = f32[9,8,128]{2,1,0:T(8,128)S(1)} custom-call(f32[64,8,128]{2,1,0:T(8,128)S(1)} %all_to_all.28.recv_ref, f32[2,2,8,1152]{3,2,1,0:T(8,128)S(1)} %get-tuple-element.36.keep_ref, f32[2,2,8,1152]{3,2,1,0:T(8,128)S(1)} %collective-permute-done.2.other_ref, f32[8,1024]{1,0:T(8,128)S(1)} %get-tuple-element.38.x_ref, ...), custom_call_target="tpu_custom_call" | custom-call | tf_op jit(solution)/shard_map/analysis/pallas_call | solution.py:69
  140.5 3.2 %collective-permute-start.5 = (f32[9,8,128]{2,1,0:T(8,128)S(1)}, f32[9,8,128]{2,1,0:T(8,128)S(1)}, u32[]{:S(2)}, u32[]{:S(2)}) collective-permute-start(f32[9,8,128]{2,1,0:T(8,128)S(1)} %analysis.5.mine_ref), channel_id=1, source_target_pairs={{0,1},{1,0},{2,3},{3,2},{4,5},{5,4},{6,7},{7,6},{8,9},{9,8},{10,11... | collective-permute-start | bytes 110600 | tf_op jit(solution)/shard_map/ppermute | solution.py:650
  143.7 0.9 collective-permute-done.5.theirs_ref
  144.5 0.7 last.1
Async XLA Ops:
  0.6 4.5 %copy-start.4 = (s32[512,2]{0,1:T(2,128)S(1)}, s32[512,2]{0,1:T(2,128)}, u32[]{:S(2)}) copy-start(s32[512,2]{0,1:T(2,128)} %param.12) | copy-start | bytes 12292
  3.6 4.1 %collective-permute-start = (f32[16,16384]{1,0:T(8,128)}, f32[16,16384]{1,0:T(8,128)}, u32[]{:S(2)}, u32[]{:S(2)}) collective-permute-start(f32[16,16384]{1,0:T(8,128)} %get-tuple-element.55), channel_id=1, source_target_pairs={{0,1},{1,0},{2,3},{3,2},{4,5},{5,4},{6,7},{7,6},{8,9},{9,8},{10,11... | collective-permute-start | bytes 3145736 | tf_op jit(solution)/shard_map/ppermute | solution.py:650
  7.0 7.2 %copy-start = (bf16[2,512,1024]{2,1,0:T(8,128)(2,1)}, bf16[2,512,1024]{2,1,0:T(8,128)(2,1)S(1)}, u32[]{:S(2)}) copy-start(bf16[2,512,1024]{2,1,0:T(8,128)(2,1)S(1)} %get-tuple-element.29.sin_ref.sin_hbm) | copy-start | bytes 6291460
  7.7 18.1 %copy-start.3 = (f32[8,2,2,2048]{3,2,1,0:T(2,128)S(1)}, f32[8,2,2,2048]{3,2,1,0:T(2,128)}, u32[]{:S(2)}) copy-start(f32[8,2,2,2048]{3,2,1,0:T(2,128)} %seeds_ref.1) | copy-start | bytes 786436
  7.7 18.1 %copy-start.5 = (f32[8,2,2,128]{3,2,1,0:T(2,128)S(1)}, f32[8,2,2,128]{3,2,1,0:T(2,128)}, u32[]{:S(2)}) copy-start(f32[8,2,2,128]{3,2,1,0:T(2,128)} %prior_ref.1) | copy-start | bytes 49156
  7.7 18.1 %copy-start.6 = (f32[2048]{0:T(1024)S(1)}, f32[2048]{0:T(1024)}, u32[]{:S(2)}) copy-start(f32[2048]{0:T(1024)} %param.11) | copy-start | bytes 24580
  7.7 18.1 %copy-start.7 = (s32[8]{0:T(128)S(1)}, s32[8]{0:T(128)}, u32[]{:S(2)}) copy-start(s32[8]{0:T(128)} %count_ref.1) | copy-start | bytes 100
  14.2 13.3 %collective-permute-start.1 = (f32[16,16384]{1,0:T(8,128)}, f32[16,16384]{1,0:T(8,128)}, u32[]{:S(2)}, u32[]{:S(2)}) collective-permute-start(f32[16,16384]{1,0:T(8,128)} %get-tuple-element.31), channel_id=1, source_target_pairs={{0,1},{1,0},{2,3},{3,2},{4,5},{5,4},{6,7},{7,6},{8,9},{9,8},{10,11... | collective-permute-start | bytes 3145736 | tf_op jit(solution)/shard_map/ppermute | solution.py:650
  14.5 21.1 %all-to-all-start = ((f32[64,8,128]{2,1,0:T(8,128)}), f32[64,8,128]{2,1,0:T(8,128)S(1)}, u32[]{:S(2)}, u32[]{:S(2)}) async-start(f32[64,8,128]{2,1,0:T(8,128)} %sky.1), calls=%async_computation | async-start | bytes 524288 | tf_op jit(solution)/shard_map/all_to_all | solution.py:653
  27.0 8.7 %collective-permute-start.2 = (f32[2,2,8,1152]{3,2,1,0:T(8,128)S(1)}, f32[2,2,8,1152]{3,2,1,0:T(8,128)S(1)}, u32[]{:S(2)}, u32[]{:S(2)}) collective-permute-start(f32[2,2,8,1152]{3,2,1,0:T(8,128)S(1)} %get-tuple-element.37), channel_id=1, source_target_pairs={{0,1},{1,0},{2,3},{3,2},{4,5},{5,4},{6,7},{7,6},{8,9},{9,8},{10,11... | collective-permute-start | bytes 442376 | tf_op jit(solution)/shard_map/ppermute | solution.py:650
  29.6 1.0 copy-start.1
  30.5 1.0 copy-start.2
  41.3 2.4 %collective-permute-start.3 = (f32[9,8,128]{2,1,0:T(8,128)S(1)}, f32[9,8,128]{2,1,0:T(8,128)S(1)}, u32[]{:S(2)}, u32[]{:S(2)}) collective-permute-start(f32[9,8,128]{2,1,0:T(8,128)S(1)} %analysis.3.mine_ref), channel_id=1, source_target_pairs={{0,1},{1,0},{2,3},{3,2},{4,5},{5,4},{6,7},{7,6},{8,9},{9,8},{10,11... | collective-permute-start | bytes 110600 | tf_op jit(solution)/shard_map/ppermute | solution.py:650
  90.1 4.0 %collective-permute-start.4 = (f32[9,8,128]{2,1,0:T(8,128)S(1)}, f32[9,8,128]{2,1,0:T(8,128)S(1)}, u32[]{:S(2)}, u32[]{:S(2)}) collective-permute-start(f32[9,8,128]{2,1,0:T(8,128)S(1)} %analysis.4.mine_ref), channel_id=1, source_target_pairs={{0,1},{1,0},{2,3},{3,2},{4,5},{5,4},{6,7},{7,6},{8,9},{9,8},{10,11... | collective-permute-start | bytes 110600 | tf_op jit(solution)/shard_map/ppermute | solution.py:650
  140.5 4.1 %collective-permute-start.5 = (f32[9,8,128]{2,1,0:T(8,128)S(1)}, f32[9,8,128]{2,1,0:T(8,128)S(1)}, u32[]{:S(2)}, u32[]{:S(2)}) collective-permute-start(f32[9,8,128]{2,1,0:T(8,128)S(1)} %analysis.5.mine_ref), channel_id=1, source_target_pairs={{0,1},{1,0},{2,3},{3,2},{4,5},{5,4},{6,7},{7,6},{8,9},{9,8},{10,11... | collective-permute-start | bytes 110600 | tf_op jit(solution)/shard_map/ppermute | solution.py:650

commit v3 on v2

--- a/solution.py
+++ b/solution.py
@@ -377,24 +377,29 @@
     )
 
 
-def to_columns(even, odd, cos_ref, sin_ref, phase_ref, extra, out_ref):
+def column_sums(even, odd, first, cos_ref, sin_ref, phase_ref):
     parts = [[], []]
+    count = even[0].shape[0] // RH
     for at in range(0, NCOL, CHUNK):
         spot = slice(at, at + CHUNK)
-        along = dot3(even, cos_ref, spot).reshape(OUTER, RH, CHUNK)
-        across = dot3(odd, sin_ref, spot).reshape(OUTER, RH, CHUNK)
+        along = dot3(even, cos_ref, spot).reshape(count, RH, CHUNK)
+        across = dot3(odd, sin_ref, spot).reshape(count, RH, CHUNK)
         real = jnp.zeros((RH, CHUNK), F32)
         imag = jnp.zeros((RH, CHUNK), F32)
-        for section in range(OUTER):
-            cos = phase_ref[0, section : section + 1, spot]
-            sin = phase_ref[1, section : section + 1, spot]
+        for section in range(count):
+            row = first + section
+            cos = phase_ref[0, row : row + 1, spot]
+            sin = phase_ref[1, row : row + 1, spot]
             real = real + (cos * along[section] - sin * across[section])
             imag = imag - (cos * across[section] + sin * along[section])
         parts[0].append(real)
         parts[1].append(imag)
+    return [jnp.concatenate(part, axis=1) for part in parts]
+
+
+def pack(parts, extra, out_ref):
     rows = []
-    for part in parts:
-        whole = jnp.concatenate(part, axis=1)
+    for whole in parts:
         rows += [whole[:, :NPAIRS], whole[:, NPAIRS:]]
     whole = jnp.concatenate(rows + [extra, jnp.zeros((56, NPAIRS), F32)], axis=0)
     for at in range(0, NPAIRS, 128):
@@ -415,8 +420,24 @@
     return cos, sin
 
 
-def table_kernel(place_ref, m_ref, cos_ref, sin_ref, phase_ref):
+PIECES = 4
+ANY = pl.BlockSpec(memory_space=pl.ANY)
+
+
+def table_kernel(
+    place_ref, noise_hbm, sky_hbm, m_ref, away_ref, heavy_ref, mine_ref, cos_ref, sin_ref, phase_ref, sky_ref, noise_ref, sems
+):
     rep = place_ref[1]
+    width = NPHI // 2 // PIECES
+    copies = []
+    for half, (row, noise) in enumerate(((1 - rep, away_ref), (rep, noise_ref))):
+        rows = pl.ds(pl.multiple_of(RH * row, RH), RH)
+        for piece in range(PIECES):
+            spot = pl.ds(piece * width, width)
+            for which, (source, target) in enumerate(((noise_hbm, noise), (sky_hbm, sky_ref.at[half]))):
+                sem = sems.at[half, which, piece]
+                copies.append(pltpu.make_async_copy(source.at[rows, spot], target.at[:, spot], sem))
+                copies[-1].start()
     every_m = jnp.concatenate([m_ref[0:1, :], m_ref[1:2, :]], axis=1)
 
     def angles(rows, factor):
@@ -441,10 +462,26 @@
     cos, sin = angles(OUTER, centre)
     phase_ref[0] = cos
     phase_ref[1] = sin
-
-
-def tables(*arrays):
-    return call(table_kernel, (TABLE, TABLE, PHASES), [], "tables", arrays, 1)
+    for half, (noise, out) in enumerate(((away_ref, heavy_ref), (noise_ref, mine_ref))):
+        for piece in range(PIECES):
+            at = 2 * (half * PIECES + piece)
+            copies[at].wait()
+            copies[at + 1].wait()
+            spot = slice(piece * width, (piece + 1) * width)
+            out[:, spot] = noise[:, spot] * sky_ref[half, :, spot]
+
+
+def tables(place, noise, sky, every_m):
+    pixels = pltpu.VMEM((RH, NPHI // 2), F32)
+    return pl.pallas_call(
+        table_kernel,
+        in_specs=[SMEM, ANY, ANY, VMEM],
+        out_specs=(VMEM,) * 6,
+        out_shape=(pixels, pixels, pixels, TABLE, TABLE, PHASES),
+        scratch_shapes=[pltpu.VMEM((2, RH, NPHI // 2), F32), pixels, pltpu.SemaphoreType.DMA((2, 2, PIECES))],
+        compiler_params=pltpu.CompilerParams(vmem_limit_bytes=LIMIT),
+        name="tables",
+    )(place, *far(noise, sky), *held(every_m))
 
 
 def folded(ref, offset):
@@ -463,24 +500,27 @@
     return jnp.concatenate(pieces, axis=1)
 
 
-def sky_kernel(
-    rep_ref, noise_ref, sky_ref, heavy_ref, cos_ref, sin_ref, phase_ref, out_ref, even_ref, odd_ref, mine_ref
-):
-    mine_ref[...] = noise_ref[...] * sky_ref[...]
-    for half, ref in enumerate((mine_ref, heavy_ref)):
-        spot = slice(half * ROWS // 2, (half + 1) * ROWS // 2)
-        ahead = folded(ref, HALF) * SCALE
-        back = turned(folded(ref, 0)) * SCALE
-        high, low = split(ahead + back)
-        even_ref[0, spot, :] = high
-        even_ref[1, spot, :] = low
-        high, low = split(ahead - back)
-        odd_ref[0, spot, :] = high
-        odd_ref[1, spot, :] = low
-    to_columns(
-        (even_ref[0], even_ref[1]), (odd_ref[0], odd_ref[1]), cos_ref, sin_ref, phase_ref,
-        jnp.zeros((8, NPAIRS), F32), out_ref,
-    )
+def half_sums(ref, first, cos_ref, sin_ref, phase_ref):
+    ahead = folded(ref, HALF) * SCALE
+    back = turned(folded(ref, 0)) * SCALE
+    return column_sums(split(ahead + back), split(ahead - back), first, cos_ref, sin_ref, phase_ref)
+
+
+def own_kernel(mine_ref, cos_ref, sin_ref, phase_ref, sums_ref):
+    sums_ref[0], sums_ref[1] = half_sums(mine_ref, 0, cos_ref, sin_ref, phase_ref)
+
+
+def sky_kernel(heavy_ref, sums_ref, cos_ref, sin_ref, phase_ref, out_ref):
+    parts = half_sums(heavy_ref, OUTER // 2, cos_ref, sin_ref, phase_ref)
+    pack([sums_ref[0] + parts[0], sums_ref[1] + parts[1]], jnp.zeros((8, NPAIRS), F32), out_ref)
+
+
+def own_step(*arrays):
+    return call(own_kernel, pltpu.VMEM((2, RH, NCOL), F32), [], "own", arrays)
+
+
+def sky_step(*arrays):
+    return call(sky_kernel, PAYLOAD, [], "sky", arrays)
 
 
 def noise_kernel(rep_ref, noise_ref, other_ref, plus_ref, minus_ref):
@@ -491,23 +531,6 @@
 
 
 OWN = pl.BlockSpec((RH, NPHI // 2), lambda i, rep: (rep[0], 0))
-
-
-def sky_step(rep, noise, sky, heavy, cos, sin, phases):
-    half = pltpu.VMEM((2, ROWS, HALF), BF16)
-    return pl.pallas_call(
-        sky_kernel,
-        grid_spec=pltpu.PrefetchScalarGridSpec(
-            num_scalar_prefetch=1,
-            grid=(1,),
-            in_specs=[OWN, OWN, VMEM, VMEM, VMEM, VMEM],
-            out_specs=VMEM,
-            scratch_shapes=[half, half, pltpu.VMEM((RH, NPHI // 2), F32)],
-        ),
-        out_shape=PAYLOAD,
-        compiler_params=pltpu.CompilerParams(vmem_limit_bytes=LIMIT),
-        name="sky",
-    )(rep, *far(noise, sky), *held(heavy, cos, sin, phases))
 
 
 def noise_step(rep, noise, other):
@@ -574,7 +597,8 @@
     row = lax.broadcasted_iota(jnp.int32, (8, NPAIRS), 0)
     extra = jnp.where((lane % 8 == 0) & (row == 0), pixels, 0.0)
     extra = jnp.where((lane % 8 == 0) & (row == 1), energy, extra)
-    to_columns((even_ref[0], even_ref[1]), (odd_ref[0], odd_ref[1]), cos_ref, sin_ref, phase_ref, extra, out_ref)
+    parts = column_sums((even_ref[0], even_ref[1]), (odd_ref[0], odd_ref[1]), 0, cos_ref, sin_ref, phase_ref)
+    pack(parts, extra, out_ref)
 
 
 def row_total(rows, index):
@@ -619,7 +643,7 @@
     half = pltpu.VMEM((2, ROWS, HALF), BF16)
     return pl.pallas_call(
         kernel,
-        in_specs=[VMEM] * len(arrays) + [pl.BlockSpec(memory_space=pl.ANY)] * 3,
+        in_specs=[VMEM] * len(arrays) + [ANY] * 3,
         out_specs=jax.tree.map(lambda _: VMEM, outs),
         out_shape=outs,
         scratch_shapes=[
@@ -652,13 +676,11 @@
     def transpose(payload):
         return lax.all_to_all(payload, "blk", split_axis=0, concat_axis=0, tiled=True)
 
-    away = RH * (1 - rep)
-    noise_away = lax.dynamic_slice_in_dim(noise_weight, away, RH, 0)
-    heavy = swap(noise_away * lax.dynamic_slice_in_dim(sky_map, away, RH, 0))
     every_m = jnp.transpose(pair_m)
-    cos, sin, phases = tables(place, every_m)
-    fourier = (cos, sin, phases)
-    payload = sky_step(rep_array, noise_weight, sky_map, heavy, *fourier)
+    noise_away, heavy, mine, cos, sin, phases = tables(place, noise_weight, sky_map, every_m)
+    heavy = swap(heavy)
+    sums = own_step(mine, cos, sin, phases)
+    payload = sky_step(heavy, sums, cos, sin, phases)
     recv = transpose(payload)
 
     payload, place, noise_away = lax.optimization_barrier((payload, place, noise_away))

time: 146 us -> 144 us (0.986)
  other arithmetic: 3.05 us -> 0.08 us
    pallas_call x8 -> x9, Pallas kernels: 29.9 us -> 33 us  [call(): pl.pallas_call(kernel, in_specs=[SMEM] * scalars + [VMEM] * (len(arrays)...]
    dynamic_slice x1 -> x0, other arithmetic: 2.98 us -> none  [shards(): noise_away = lax.dynamic_slice_in_dim(noise_weight, away, RH, 0)]
    pallas_call x3, Pallas kernels: 22.7 us -> 20 us  [the longest x2 16.1 us: map_call(): pl.pallas_call(kernel, in_specs=[VMEM] * len(arrays) + [ANY] * 3, out_spe...]
where the time goes in v3:
time: 144 us; the launch traced here: 143 us
  blocking collectives  56.2 us (39%)
  Pallas kernels  55 us (38%)
  starting transfers between devices  21.5 us (15%)
  waiting for transfers between devices  6.91 us (5%)
  local copies, waits for them, and re-layouts  2.66 us (2%)
    all_to_all x4, blocking collectives, transpose(): lax.all_to_all(payload, 'blk', split_axis=0, concat_axis=0, tiled=True)  56.2 us
    pallas_call x9, Pallas kernels, call(): pl.pallas_call(kernel, in_specs=[SMEM] * scalars + [VMEM] * (len(arrays)...  33 us
    pallas_call x2, Pallas kernels, map_call(): pl.pallas_call(kernel, in_specs=[VMEM] * len(arrays) + [ANY] * 3, out_spe...  16.1 us
    all_to_all x1, starting transfers between devices, transpose(): lax.all_to_all(payload, 'blk', split_axis=0, concat_axis=0, tiled=True)  11.2 us
    ppermute x6, starting transfers between devices, swap(): return lax.ppermute(value, 'rep', [(0, 1), (1, 0)])  10.3 us
    all_to_all x1, waiting for transfers between devices, transpose(): lax.all_to_all(payload, 'blk', split_axis=0, concat_axis=0, tiled=True)  4.18 us
    pallas_call x1, Pallas kernels, tables(): pl.pallas_call(table_kernel, in_specs=[SMEM, ANY, ANY, VMEM], out_specs=(...  3.82 us
  transfers between devices with their start and end apart: 7, of which 5 were waited for; matrix products, arithmetic and copies ran while one was open for 0% of the time, Pallas kernels for 4%

profile of v3, /device:TPU:1, one launch (start us, length us, event | category | flops | bytes accessed | tf_op | source)
XLA Modules:
  0.0 143.1 jit_solution(13310249407654074773)
XLA Ops:
  0.6 0.1 pad_add_fusion.place_ref
  0.7 0.0 copy-start.4
  0.7 0.7 copy-done.4
  1.4 3.8 %tables.1 = (f32[16,16384]{1,0:T(8,128)}, f32[16,16384]{1,0:T(8,128)S(1)}, f32[16,16384]{1,0:T(8,128)S(1)}, bf16[2,512,1024]{2,1,0:T(8,128)(2,1)S(1)}, bf16[2,51...) custom-call(s32[2]{0:T(128)S(1)} %pad_add_fusion.place_ref, f32[32,16384]{1,0:T(8,128)} %noise_ref.1, ...), custom_call_target="tpu_custom_call" | custom-call | tf_op jit(solution)/shard_map/tables/pallas_call | solution.py:476
  5.2 0.0 copy-start
  5.2 1.5 %collective-permute-start = (f32[16,16384]{1,0:T(8,128)S(1)}, f32[16,16384]{1,0:T(8,128)S(1)}, u32[]{:S(2)}, u32[]{:S(2)}) collective-permute-start(f32[16,16384]{1,0:T(8,128)S(1)} %get-tuple-element.31), channel_id=1, source_target_pairs={{0,1},{1,0},{2,3},{3,2},{4,5},{5,4},{6,7},{7,6},{8,9},{9,8},{10,11... | collective-permute-start | bytes 3145736 | tf_op jit(solution)/shard_map/ppermute | solution.py:674
  6.7 2.1 %own.1.sums_ref = f32[2,16,1024]{2,1,0:T(8,128)S(1)} custom-call(f32[16,16384]{1,0:T(8,128)S(1)} %get-tuple-element.32.mine_ref, bf16[2,512,1024]{2,1,0:T(8,128)(2,1)S(1)} %get-tuple-element.33.cos_ref, bf16[2,512,1024]{2,1,0:T(8,128)(2,1)S(1)} %get-tuple-element.34.sin_ref.sin_hbm, f32[2,32,1024]{2,1,0:T(8,128)S(1)} %get-tuple-element.35.phase_ref), custom_call_target="tpu_custom_call" | custom-call | tf_op jit(solution)/shard_map/own/pallas_call | solution.py:69
  8.8 0.0 copy-start.3
  8.8 0.0 copy-start.5
  8.9 0.0 copy-start.6
  8.9 0.0 copy-start.7
  8.9 0.0 copy-start.8
  8.9 0.1 collective-permute-done.heavy_ref
  9.0 0.0 copy-done
  9.0 2.9 %sky.1 = f32[64,8,128]{2,1,0:T(8,128)} custom-call(f32[16,16384]{1,0:T(8,128)S(1)} %collective-permute-done.heavy_ref, f32[2,16,1024]{2,1,0:T(8,128)S(1)} %own.1.sums_ref, bf16[2,512,1024]{2,1,0:T(8,128)(2,1)S(1)} %get-tuple-element.33.cos_ref, bf16[2,512,1024]{2,1,0:T(8,128)(2,1)S(1)} %get-tuple-element.34.sin_ref.sin_hbm, ...), custom_call_target="tpu_custom_call" | custom-call | tf_op jit(solution)/shard_map/sky/pallas_call | solution.py:69
  11.9 0.4 collective-permute-start.1
  12.3 11.2 %all-to-all-start = ((f32[64,8,128]{2,1,0:T(8,128)}), f32[64,8,128]{2,1,0:T(8,128)S(1)}, u32[]{:S(2)}, u32[]{:S(2)}) async-start(f32[64,8,128]{2,1,0:T(8,128)} %sky.1), calls=%async_computation | async-start | bytes 524288 | tf_op jit(solution)/shard_map/all_to_all | solution.py:677
  23.5 0.0 copy-done.3
  23.5 0.0 copy-done.5
  23.6 0.0 copy-done.6
  23.6 0.0 copy-done.7
  23.6 0.0 copy-done.8
  23.6 1.2 prepare.1
  24.7 0.5 collective-permute-start.2
  25.3 0.0 collective-permute-done.1.other_ref
  25.3 2.0 %noise.1 = (f32[512,512]{1,0:T(8,128)S(1)}, f32[512,512]{1,0:T(8,128)S(1)}) custom-call(s32[1]{0:T(128)} %bitcast.1.rep_ref, f32[32,16384]{1,0:T(8,128)} %noise_ref.1, f32[16,16384]{1,0:T(8,128)} %collective-permute-done.1.other_ref), custom_call_target="tpu_custom_call" | custom-call | tf_op jit(solution)/shard_map/noise/pallas_call | solution.py:537
  27.3 0.0 copy-start.1
  27.3 1.0 copy-done.1
  28.3 0.0 copy-start.2
  28.3 1.0 copy-done.2
  29.2 4.2 %all-to-all-done.recv_ref = f32[64,8,128]{2,1,0:T(8,128)S(1)} async-done(((f32[64,8,128]{2,1,0:T(8,128)}), f32[64,8,128]{2,1,0:T(8,128)S(1)}, u32[]{:S(2)}, u32[]{:S(2)}) %all-to-all-start) | async-done | bytes 262176 | tf_op jit(solution)/shard_map/all_to_all | solution.py:677
  33.4 0.0 collective-permute-done.2.other_ref
  33.4 5.6 %analysis.3.mine_ref = f32[9,8,128]{2,1,0:T(8,128)S(1)} custom-call(f32[64,8,128]{2,1,0:T(8,128)S(1)} %all-to-all-done.recv_ref, f32[2,2,8,1152]{3,2,1,0:T(8,128)S(1)} %get-tuple-element.42.keep_ref, f32[2,2,8,1152]{3,2,1,0:T(8,128)S(1)} %collective-permute-done.2.other_ref, f32[8,1024]{1,0:T(8,128)S(1)} %get-tuple-element.44.x_ref, ...), custom_call_target="tpu_custom_call" | custom-call | tf_op jit(solution)/shard_map/analysis/pallas_call | solution.py:69
  39.1 1.5 %collective-permute-start.3 = (f32[9,8,128]{2,1,0:T(8,128)S(1)}, f32[9,8,128]{2,1,0:T(8,128)S(1)}, u32[]{:S(2)}, u32[]{:S(2)}) collective-permute-start(f32[9,8,128]{2,1,0:T(8,128)S(1)} %analysis.3.mine_ref), channel_id=1, source_target_pairs={{0,1},{1,0},{2,3},{3,2},{4,5},{5,4},{6,7},{7,6},{8,9},{9,8},{10,11... | collective-permute-start | bytes 110600 | tf_op jit(solution)/shard_map/ppermute | solution.py:674
  40.6 0.9 collective-permute-done.3.theirs_ref
  41.5 4.5 %first.1 = (f32[64,8,128]{2,1,0:T(8,128)S(1)}, f32[8,8,128]{2,1,0:T(8,128)S(1)}) custom-call(f32[9,8,128]{2,1,0:T(8,128)S(1)} %analysis.3.mine_ref, f32[9,8,128]{2,1,0:T(8,128)S(1)} %collective-permute-done.3.theirs_ref, f32[2,2,8,1152]{3,2,1,0:T(8,128)S(1)} %get-tuple-element.42.keep_ref, f32[2,2,8,1152]{3,2,1,0:T(8,128)S(1)} %collective-permute-done.2.other_ref, ...), custom_call_target="tpu_custom_call" | custom-call | tf_op jit(solution)/shard_map/first/pallas_call | solution.py:69
  46.0 14.1 %all_to_all.25.recv_ref.before_ref = f32[64,8,128]{2,1,0:T(8,128)S(1)} all-to-all(f32[64,8,128]{2,1,0:T(8,128)S(1)} %get-tuple-element.48), channel_id=1, replica_groups=mesh['blk'=64,'rep'=2] {'blk'}, dimensions={0} | all-to-all | bytes 524288 | tf_op jit(solution)/shard_map/all_to_all | solution.py:677
  60.2 8.0 %map_one.1 = (f32[64,8,128]{2,1,0:T(8,128)S(1)}, f32[8,128]{1,0:T(8,128)S(1)}) custom-call(f32[64,8,128]{2,1,0:T(8,128)S(1)} %all_to_all.25.recv_ref.before_ref, f32[2,32,1024]{2,1,0:T(8,128)S(1)} %get-tuple-element.35.phase_ref, bf16[2,512,1024]{2,1,0:T(8,128)(2,1)S(1)} %get-tuple-element.33.cos_ref, bf16[2,512,1024]{2,1,0:T(8,128)(2,1)} %copy-done, ...), custom_call_target="tpu_custom_call" | custom-call | tf_op jit(solution)/shard_map/map_one/pallas_call | solution.py:644
  68.2 14.1 %all_to_all.26.recv_ref = f32[64,8,128]{2,1,0:T(8,128)S(1)} all-to-all(f32[64,8,128]{2,1,0:T(8,128)S(1)} %get-tuple-element.51), channel_id=1, replica_groups=mesh['blk'=64,'rep'=2] {'blk'}, dimensions={0} | all-to-all | bytes 524288 | tf_op jit(solution)/shard_map/all_to_all | solution.py:677
  82.3 5.6 %analysis.4.mine_ref = f32[9,8,128]{2,1,0:T(8,128)S(1)} custom-call(f32[64,8,128]{2,1,0:T(8,128)S(1)} %all_to_all.26.recv_ref, f32[2,2,8,1152]{3,2,1,0:T(8,128)S(1)} %get-tuple-element.42.keep_ref, f32[2,2,8,1152]{3,2,1,0:T(8,128)S(1)} %collective-permute-done.2.other_ref, f32[8,1024]{1,0:T(8,128)S(1)} %get-tuple-element.44.x_ref, ...), custom_call_target="tpu_custom_call" | custom-call | tf_op jit(solution)/shard_map/analysis/pallas_call | solution.py:69
  87.9 3.2 %collective-permute-start.4 = (f32[9,8,128]{2,1,0:T(8,128)S(1)}, f32[9,8,128]{2,1,0:T(8,128)S(1)}, u32[]{:S(2)}, u32[]{:S(2)}) collective-permute-start(f32[9,8,128]{2,1,0:T(8,128)S(1)} %analysis.4.mine_ref), channel_id=1, source_target_pairs={{0,1},{1,0},{2,3},{3,2},{4,5},{5,4},{6,7},{7,6},{8,9},{9,8},{10,11... | collective-permute-start | bytes 110600 | tf_op jit(solution)/shard_map/ppermute | solution.py:674
  91.1 0.9 collective-permute-done.4.theirs_ref
  91.9 4.6 %second.1 = (f32[64,8,128]{2,1,0:T(8,128)S(1)}, f32[8,8,128]{2,1,0:T(8,128)S(1)}, f32[8,128]{1,0:T(8,128)S(1)}) custom-call(f32[9,8,128]{2,1,0:T(8,128)S(1)} %analysis.4.mine_ref, f32[9,8,128]{2,1,0:T(8,128)S(1)} %collective-permute-done.4.theirs_ref, f32[8,8,128]{2,1,0:T(8,128)S(1)} %get-tuple-element.52.rhs_ref, f32[8,128]{1,0:T(8,128)S(1)} %get-tuple-element.53.told_ref, ...), custom_call_target="tpu_custom_call" | custom-call | tf_op jit(solution)/shard_map/second/pallas_call | solution.py:69
  96.6 13.9 %all_to_all.27.recv_ref = f32[64,8,128]{2,1,0:T(8,128)S(1)} all-to-all(f32[64,8,128]{2,1,0:T(8,128)S(1)} %get-tuple-element.54), channel_id=1, replica_groups=mesh['blk'=64,'rep'=2] {'blk'}, dimensions={0} | all-to-all | bytes 524288 | tf_op jit(solution)/shard_map/all_to_all | solution.py:677
  110.5 8.1 %map_two.1 = (f32[64,8,128]{2,1,0:T(8,128)S(1)}, f32[8,8,128]{2,1,0:T(8,128)S(1)}, f32[8,128]{1,0:T(8,128)S(1)}) custom-call(f32[64,8,128]{2,1,0:T(8,128)S(1)} %all_to_all.27.recv_ref, f32[64,8,128]{2,1,0:T(8,128)S(1)} %all_to_all.25.recv_ref.before_ref, f32[8,128]{1,0:T(8,128)S(1)} %get-tuple-element.53.told_ref, ...), custom_call_target="tpu_custom_call" | custom-call | tf_op jit(solution)/shard_map/map_two/pallas_call | solution.py:644
  118.6 14.1 %all_to_all.28.recv_ref = f32[64,8,128]{2,1,0:T(8,128)S(1)} all-to-all(f32[64,8,128]{2,1,0:T(8,128)S(1)} %get-tuple-element.56), channel_id=1, replica_groups=mesh['blk'=64,'rep'=2] {'blk'}, dimensions={0} | all-to-all | bytes 524288 | tf_op jit(solution)/shard_map/all_to_all | solution.py:677
  132.7 5.6 %analysis.5.mine_ref = f32[9,8,128]{2,1,0:T(8,128)S(1)} custom-call(f32[64,8,128]{2,1,0:T(8,128)S(1)} %all_to_all.28.recv_ref, f32[2,2,8,1152]{3,2,1,0:T(8,128)S(1)} %get-tuple-element.42.keep_ref, f32[2,2,8,1152]{3,2,1,0:T(8,128)S(1)} %collective-permute-done.2.other_ref, f32[8,1024]{1,0:T(8,128)S(1)} %get-tuple-element.44.x_ref, ...), custom_call_target="tpu_custom_call" | custom-call | tf_op jit(solution)/shard_map/analysis/pallas_call | solution.py:69
  138.3 3.2 %collective-permute-start.5 = (f32[9,8,128]{2,1,0:T(8,128)S(1)}, f32[9,8,128]{2,1,0:T(8,128)S(1)}, u32[]{:S(2)}, u32[]{:S(2)}) collective-permute-start(f32[9,8,128]{2,1,0:T(8,128)S(1)} %analysis.5.mine_ref), channel_id=1, source_target_pairs={{0,1},{1,0},{2,3},{3,2},{4,5},{5,4},{6,7},{7,6},{8,9},{9,8},{10,11... | collective-permute-start | bytes 110600 | tf_op jit(solution)/shard_map/ppermute | solution.py:674
  141.5 0.9 collective-permute-done.5.theirs_ref
  142.4 0.7 last.1
Async XLA Ops:
  0.7 0.7 copy-start.4
  5.2 3.8 %copy-start = (bf16[2,512,1024]{2,1,0:T(8,128)(2,1)}, bf16[2,512,1024]{2,1,0:T(8,128)(2,1)S(1)}, u32[]{:S(2)}) copy-start(bf16[2,512,1024]{2,1,0:T(8,128)(2,1)S(1)} %get-tuple-element.34.sin_ref.sin_hbm) | copy-start | bytes 6291460
  5.2 3.8 %collective-permute-start = (f32[16,16384]{1,0:T(8,128)S(1)}, f32[16,16384]{1,0:T(8,128)S(1)}, u32[]{:S(2)}, u32[]{:S(2)}) collective-permute-start(f32[16,16384]{1,0:T(8,128)S(1)} %get-tuple-element.31), channel_id=1, source_target_pairs={{0,1},{1,0},{2,3},{3,2},{4,5},{5,4},{6,7},{7,6},{8,9},{9,8},{10,11... | collective-permute-start | bytes 3145736 | tf_op jit(solution)/shard_map/ppermute | solution.py:674
  8.8 14.7 %copy-start.3 = (f32[8,2,2,2048]{3,2,1,0:T(2,128)S(1)}, f32[8,2,2,2048]{3,2,1,0:T(2,128)}, u32[]{:S(2)}) copy-start(f32[8,2,2,2048]{3,2,1,0:T(2,128)} %seeds_ref.1) | copy-start | bytes 786436
  8.8 14.7 %copy-start.5 = (s32[512,2]{0,1:T(2,128)S(1)}, s32[512,2]{0,1:T(2,128)}, u32[]{:S(2)}) copy-start(s32[512,2]{0,1:T(2,128)} %param.12) | copy-start | bytes 12292
  8.9 14.7 %copy-start.6 = (f32[8,2,2,128]{3,2,1,0:T(2,128)S(1)}, f32[8,2,2,128]{3,2,1,0:T(2,128)}, u32[]{:S(2)}) copy-start(f32[8,2,2,128]{3,2,1,0:T(2,128)} %prior_ref.1) | copy-start | bytes 49156
  8.9 14.7 %copy-start.7 = (f32[2048]{0:T(1024)S(1)}, f32[2048]{0:T(1024)}, u32[]{:S(2)}) copy-start(f32[2048]{0:T(1024)} %param.11) | copy-start | bytes 24580
  8.9 14.7 %copy-start.8 = (s32[8]{0:T(128)S(1)}, s32[8]{0:T(128)}, u32[]{:S(2)}) copy-start(s32[8]{0:T(128)} %count_ref.1) | copy-start | bytes 100
  11.9 13.3 %collective-permute-start.1 = (f32[16,16384]{1,0:T(8,128)}, f32[16,16384]{1,0:T(8,128)}, u32[]{:S(2)}, u32[]{:S(2)}) collective-permute-start(f32[16,16384]{1,0:T(8,128)} %get-tuple-element.37), channel_id=1, source_target_pairs={{0,1},{1,0},{2,3},{3,2},{4,5},{5,4},{6,7},{7,6},{8,9},{9,8},{10,11... | collective-permute-start | bytes 3145736 | tf_op jit(solution)/shard_map/ppermute | solution.py:674
  12.3 21.1 %all-to-all-start = ((f32[64,8,128]{2,1,0:T(8,128)}), f32[64,8,128]{2,1,0:T(8,128)S(1)}, u32[]{:S(2)}, u32[]{:S(2)}) async-start(f32[64,8,128]{2,1,0:T(8,128)} %sky.1), calls=%async_computation | async-start | bytes 524288 | tf_op jit(solution)/shard_map/all_to_all | solution.py:677
  24.7 8.7 %collective-permute-start.2 = (f32[2,2,8,1152]{3,2,1,0:T(8,128)S(1)}, f32[2,2,8,1152]{3,2,1,0:T(8,128)S(1)}, u32[]{:S(2)}, u32[]{:S(2)}) collective-permute-start(f32[2,2,8,1152]{3,2,1,0:T(8,128)S(1)} %get-tuple-element.43), channel_id=1, source_target_pairs={{0,1},{1,0},{2,3},{3,2},{4,5},{5,4},{6,7},{7,6},{8,9},{9,8},{10,11... | collective-permute-start | bytes 442376 | tf_op jit(solution)/shard_map/ppermute | solution.py:674
  27.3 1.0 copy-start.1
  28.3 1.0 copy-start.2
  39.1 2.4 %collective-permute-start.3 = (f32[9,8,128]{2,1,0:T(8,128)S(1)}, f32[9,8,128]{2,1,0:T(8,128)S(1)}, u32[]{:S(2)}, u32[]{:S(2)}) collective-permute-start(f32[9,8,128]{2,1,0:T(8,128)S(1)} %analysis.3.mine_ref), channel_id=1, source_target_pairs={{0,1},{1,0},{2,3},{3,2},{4,5},{5,4},{6,7},{7,6},{8,9},{9,8},{10,11... | collective-permute-start | bytes 110600 | tf_op jit(solution)/shard_map/ppermute | solution.py:674
  87.9 4.0 %collective-permute-start.4 = (f32[9,8,128]{2,1,0:T(8,128)S(1)}, f32[9,8,128]{2,1,0:T(8,128)S(1)}, u32[]{:S(2)}, u32[]{:S(2)}) collective-permute-start(f32[9,8,128]{2,1,0:T(8,128)S(1)} %analysis.4.mine_ref), channel_id=1, source_target_pairs={{0,1},{1,0},{2,3},{3,2},{4,5},{5,4},{6,7},{7,6},{8,9},{9,8},{10,11... | collective-permute-start | bytes 110600 | tf_op jit(solution)/shard_map/ppermute | solution.py:674
  138.3 4.1 %collective-permute-start.5 = (f32[9,8,128]{2,1,0:T(8,128)S(1)}, f32[9,8,128]{2,1,0:T(8,128)S(1)}, u32[]{:S(2)}, u32[]{:S(2)}) collective-permute-start(f32[9,8,128]{2,1,0:T(8,128)S(1)} %analysis.5.mine_ref), channel_id=1, source_target_pairs={{0,1},{1,0},{2,3},{3,2},{4,5},{5,4},{6,7},{7,6},{8,9},{9,8},{10,11... | collective-permute-start | bytes 110600 | tf_op jit(solution)/shard_map/ppermute | solution.py:674

commit v4 on v3

--- a/solution.py
+++ b/solution.py
@@ -360,21 +360,17 @@
 
 def dot3(left, right_ref, spot):
     high, low = left
-    return (
-        jnp.dot(high, right_ref[0, :, spot], preferred_element_type=F32)
-        + jnp.dot(low, right_ref[0, :, spot], preferred_element_type=F32)
-        + jnp.dot(high, right_ref[1, :, spot], preferred_element_type=F32)
-    )
+    rows = high.shape[0]
+    both = jnp.dot(jnp.concatenate([high, low], axis=0), right_ref[0, :, spot], preferred_element_type=F32)
+    return both[:rows] + both[rows:] + jnp.dot(high, right_ref[1, :, spot], preferred_element_type=F32)
 
 
 def dot3_turned(left, right_ref, spot):
     high, low = left
     dims = (((1,), (1,)), ((), ()))
-    return (
-        lax.dot_general(high, right_ref[0, spot, :], dims, preferred_element_type=F32)
-        + lax.dot_general(low, right_ref[0, spot, :], dims, preferred_element_type=F32)
-        + lax.dot_general(high, right_ref[1, spot, :], dims, preferred_element_type=F32)
-    )
+    rows = high.shape[0]
+    both = lax.dot_general(jnp.concatenate([high, low], axis=0), right_ref[0, spot, :], dims, preferred_element_type=F32)
+    return both[:rows] + both[rows:] + lax.dot_general(high, right_ref[1, spot, :], dims, preferred_element_type=F32)
 
 
 def column_sums(even, odd, first, cos_ref, sin_ref, phase_ref):

time: 144 us -> 142 us (0.986)
  no operation moved by 1% of the time
where the time goes in v4:
time: 142 us
  blocking collectives  56 us (39%)
  Pallas kernels  54 us (38%)
  starting transfers between devices  21.5 us (15%)
  waiting for transfers between devices  6.94 us (5%)
  local copies, waits for them, and re-layouts  2.66 us (2%)
    all_to_all x4, blocking collectives, transpose(): lax.all_to_all(payload, 'blk', split_axis=0, concat_axis=0, tiled=True)  56 us
    pallas_call x9, Pallas kernels, call(): pl.pallas_call(kernel, in_specs=[SMEM] * scalars + [VMEM] * (len(arrays)...  32.9 us
    pallas_call x2, Pallas kernels, map_call(): pl.pallas_call(kernel, in_specs=[VMEM] * len(arrays) + [ANY] * 3, out_spe...  15.2 us
    all_to_all x1, starting transfers between devices, transpose(): lax.all_to_all(payload, 'blk', split_axis=0, concat_axis=0, tiled=True)  11.2 us
    ppermute x6, starting transfers between devices, swap(): return lax.ppermute(value, 'rep', [(0, 1), (1, 0)])  10.3 us
    all_to_all x1, waiting for transfers between devices, transpose(): lax.all_to_all(payload, 'blk', split_axis=0, concat_axis=0, tiled=True)  4.18 us
    pallas_call x1, Pallas kernels, tables(): pl.pallas_call(table_kernel, in_specs=[SMEM, ANY, ANY, VMEM], out_specs=(...  3.82 us
  transfers between devices with their start and end apart: 7, of which 5 were waited for; matrix products, arithmetic and copies ran while one was open for 0% of the time, Pallas kernels for 4%

profile of v4, /device:TPU:1, one launch (start us, length us, event | category | flops | bytes accessed | tf_op | source)
XLA Modules:
  0.0 142.0 jit_solution(4477937879799867463)
XLA Ops:
  0.6 0.1 pad_add_fusion.place_ref
  0.7 0.0 copy-start.4
  0.7 0.7 copy-done.4
  1.4 3.8 %tables.1 = (f32[16,16384]{1,0:T(8,128)}, f32[16,16384]{1,0:T(8,128)S(1)}, f32[16,16384]{1,0:T(8,128)S(1)}, bf16[2,512,1024]{2,1,0:T(8,128)(2,1)S(1)}, bf16[2,51...) custom-call(s32[2]{0:T(128)S(1)} %pad_add_fusion.place_ref, f32[32,16384]{1,0:T(8,128)} %noise_ref.1, ...), custom_call_target="tpu_custom_call" | custom-call | tf_op jit(solution)/shard_map/tables/pallas_call | solution.py:472
  5.2 0.0 copy-start
  5.2 1.5 %collective-permute-start = (f32[16,16384]{1,0:T(8,128)S(1)}, f32[16,16384]{1,0:T(8,128)S(1)}, u32[]{:S(2)}, u32[]{:S(2)}) collective-permute-start(f32[16,16384]{1,0:T(8,128)S(1)} %get-tuple-element.31), channel_id=1, source_target_pairs={{0,1},{1,0},{2,3},{3,2},{4,5},{5,4},{6,7},{7,6},{8,9},{9,8},{10,11... | collective-permute-start | bytes 3145736 | tf_op jit(solution)/shard_map/ppermute | solution.py:670
  6.7 2.1 %own.1.sums_ref = f32[2,16,1024]{2,1,0:T(8,128)S(1)} custom-call(f32[16,16384]{1,0:T(8,128)S(1)} %get-tuple-element.32.mine_ref, bf16[2,512,1024]{2,1,0:T(8,128)(2,1)S(1)} %get-tuple-element.33.cos_ref, bf16[2,512,1024]{2,1,0:T(8,128)(2,1)S(1)} %get-tuple-element.34.sin_ref.sin_hbm, f32[2,32,1024]{2,1,0:T(8,128)S(1)} %get-tuple-element.35.phase_ref), custom_call_target="tpu_custom_call" | custom-call | tf_op jit(solution)/shard_map/own/pallas_call | solution.py:69
  8.8 0.0 copy-start.3
  8.8 0.0 copy-start.5
  8.8 0.0 copy-start.6
  8.8 0.0 copy-start.7
  8.9 0.0 copy-start.8
  8.9 0.2 collective-permute-done.heavy_ref
  9.0 0.0 copy-done
  9.0 2.9 %sky.1 = f32[64,8,128]{2,1,0:T(8,128)} custom-call(f32[16,16384]{1,0:T(8,128)S(1)} %collective-permute-done.heavy_ref, f32[2,16,1024]{2,1,0:T(8,128)S(1)} %own.1.sums_ref, bf16[2,512,1024]{2,1,0:T(8,128)(2,1)S(1)} %get-tuple-element.33.cos_ref, bf16[2,512,1024]{2,1,0:T(8,128)(2,1)S(1)} %get-tuple-element.34.sin_ref.sin_hbm, ...), custom_call_target="tpu_custom_call" | custom-call | tf_op jit(solution)/shard_map/sky/pallas_call | solution.py:69
  11.9 0.4 collective-permute-start.1
  12.3 11.2 %all-to-all-start = ((f32[64,8,128]{2,1,0:T(8,128)}), f32[64,8,128]{2,1,0:T(8,128)S(1)}, u32[]{:S(2)}, u32[]{:S(2)}) async-start(f32[64,8,128]{2,1,0:T(8,128)} %sky.1), calls=%async_computation | async-start | bytes 524288 | tf_op jit(solution)/shard_map/all_to_all | solution.py:673
  23.5 0.0 copy-done.3
  23.5 0.0 copy-done.5
  23.5 0.0 copy-done.6
  23.5 0.0 copy-done.7
  23.5 0.0 copy-done.8
  23.5 1.2 prepare.1
  24.7 0.5 collective-permute-start.2
  25.2 0.0 collective-permute-done.1.other_ref
  25.2 2.0 %noise.1 = (f32[512,512]{1,0:T(8,128)S(1)}, f32[512,512]{1,0:T(8,128)S(1)}) custom-call(s32[1]{0:T(128)} %bitcast.1.rep_ref, f32[32,16384]{1,0:T(8,128)} %noise_ref.1, f32[16,16384]{1,0:T(8,128)} %collective-permute-done.1.other_ref), custom_call_target="tpu_custom_call" | custom-call | tf_op jit(solution)/shard_map/noise/pallas_call | solution.py:533
  27.3 0.0 copy-start.1
  27.3 1.0 copy-done.1
  28.2 0.0 copy-start.2
  28.2 1.0 copy-done.2
  29.2 4.2 %all-to-all-done.recv_ref = f32[64,8,128]{2,1,0:T(8,128)S(1)} async-done(((f32[64,8,128]{2,1,0:T(8,128)}), f32[64,8,128]{2,1,0:T(8,128)S(1)}, u32[]{:S(2)}, u32[]{:S(2)}) %all-to-all-start) | async-done | bytes 262176 | tf_op jit(solution)/shard_map/all_to_all | solution.py:673
  33.4 0.0 collective-permute-done.2.other_ref
  33.4 5.6 %analysis.3.mine_ref = f32[9,8,128]{2,1,0:T(8,128)S(1)} custom-call(f32[64,8,128]{2,1,0:T(8,128)S(1)} %all-to-all-done.recv_ref, f32[2,2,8,1152]{3,2,1,0:T(8,128)S(1)} %get-tuple-element.42.keep_ref, f32[2,2,8,1152]{3,2,1,0:T(8,128)S(1)} %collective-permute-done.2.other_ref, f32[8,1024]{1,0:T(8,128)S(1)} %get-tuple-element.44.x_ref, ...), custom_call_target="tpu_custom_call" | custom-call | tf_op jit(solution)/shard_map/analysis/pallas_call | solution.py:69
  39.0 1.5 %collective-permute-start.3 = (f32[9,8,128]{2,1,0:T(8,128)S(1)}, f32[9,8,128]{2,1,0:T(8,128)S(1)}, u32[]{:S(2)}, u32[]{:S(2)}) collective-permute-start(f32[9,8,128]{2,1,0:T(8,128)S(1)} %analysis.3.mine_ref), channel_id=1, source_target_pairs={{0,1},{1,0},{2,3},{3,2},{4,5},{5,4},{6,7},{7,6},{8,9},{9,8},{10,11... | collective-permute-start | bytes 110600 | tf_op jit(solution)/shard_map/ppermute | solution.py:670
  40.6 0.9 collective-permute-done.3.theirs_ref
  41.4 4.5 %first.1 = (f32[64,8,128]{2,1,0:T(8,128)S(1)}, f32[8,8,128]{2,1,0:T(8,128)S(1)}) custom-call(f32[9,8,128]{2,1,0:T(8,128)S(1)} %analysis.3.mine_ref, f32[9,8,128]{2,1,0:T(8,128)S(1)} %collective-permute-done.3.theirs_ref, f32[2,2,8,1152]{3,2,1,0:T(8,128)S(1)} %get-tuple-element.42.keep_ref, f32[2,2,8,1152]{3,2,1,0:T(8,128)S(1)} %collective-permute-done.2.other_ref, ...), custom_call_target="tpu_custom_call" | custom-call | tf_op jit(solution)/shard_map/first/pallas_call | solution.py:69
  46.0 14.0 %all_to_all.25.recv_ref.before_ref = f32[64,8,128]{2,1,0:T(8,128)S(1)} all-to-all(f32[64,8,128]{2,1,0:T(8,128)S(1)} %get-tuple-element.48), channel_id=1, replica_groups=mesh['blk'=64,'rep'=2] {'blk'}, dimensions={0} | all-to-all | bytes 524288 | tf_op jit(solution)/shard_map/all_to_all | solution.py:673
  59.9 7.5 %map_one.1 = (f32[64,8,128]{2,1,0:T(8,128)S(1)}, f32[8,128]{1,0:T(8,128)S(1)}) custom-call(f32[64,8,128]{2,1,0:T(8,128)S(1)} %all_to_all.25.recv_ref.before_ref, f32[2,32,1024]{2,1,0:T(8,128)S(1)} %get-tuple-element.35.phase_ref, bf16[2,512,1024]{2,1,0:T(8,128)(2,1)S(1)} %get-tuple-element.33.cos_ref, bf16[2,512,1024]{2,1,0:T(8,128)(2,1)} %copy-done, ...), custom_call_target="tpu_custom_call" | custom-call | tf_op jit(solution)/shard_map/map_one/pallas_call | solution.py:640
  67.5 14.1 %all_to_all.26.recv_ref = f32[64,8,128]{2,1,0:T(8,128)S(1)} all-to-all(f32[64,8,128]{2,1,0:T(8,128)S(1)} %get-tuple-element.51), channel_id=1, replica_groups=mesh['blk'=64,'rep'=2] {'blk'}, dimensions={0} | all-to-all | bytes 524288 | tf_op jit(solution)/shard_map/all_to_all | solution.py:673
  81.6 5.6 %analysis.4.mine_ref = f32[9,8,128]{2,1,0:T(8,128)S(1)} custom-call(f32[64,8,128]{2,1,0:T(8,128)S(1)} %all_to_all.26.recv_ref, f32[2,2,8,1152]{3,2,1,0:T(8,128)S(1)} %get-tuple-element.42.keep_ref, f32[2,2,8,1152]{3,2,1,0:T(8,128)S(1)} %collective-permute-done.2.other_ref, f32[8,1024]{1,0:T(8,128)S(1)} %get-tuple-element.44.x_ref, ...), custom_call_target="tpu_custom_call" | custom-call | tf_op jit(solution)/shard_map/analysis/pallas_call | solution.py:69
  87.2 3.2 %collective-permute-start.4 = (f32[9,8,128]{2,1,0:T(8,128)S(1)}, f32[9,8,128]{2,1,0:T(8,128)S(1)}, u32[]{:S(2)}, u32[]{:S(2)}) collective-permute-start(f32[9,8,128]{2,1,0:T(8,128)S(1)} %analysis.4.mine_ref), channel_id=1, source_target_pairs={{0,1},{1,0},{2,3},{3,2},{4,5},{5,4},{6,7},{7,6},{8,9},{9,8},{10,11... | collective-permute-start | bytes 110600 | tf_op jit(solution)/shard_map/ppermute | solution.py:670
  90.4 0.9 collective-permute-done.4.theirs_ref
  91.3 4.6 %second.1 = (f32[64,8,128]{2,1,0:T(8,128)S(1)}, f32[8,8,128]{2,1,0:T(8,128)S(1)}, f32[8,128]{1,0:T(8,128)S(1)}) custom-call(f32[9,8,128]{2,1,0:T(8,128)S(1)} %analysis.4.mine_ref, f32[9,8,128]{2,1,0:T(8,128)S(1)} %collective-permute-done.4.theirs_ref, f32[8,8,128]{2,1,0:T(8,128)S(1)} %get-tuple-element.52.rhs_ref, f32[8,128]{1,0:T(8,128)S(1)} %get-tuple-element.53.told_ref, ...), custom_call_target="tpu_custom_call" | custom-call | tf_op jit(solution)/shard_map/second/pallas_call | solution.py:69
  95.9 13.9 %all_to_all.27.recv_ref = f32[64,8,128]{2,1,0:T(8,128)S(1)} all-to-all(f32[64,8,128]{2,1,0:T(8,128)S(1)} %get-tuple-element.54), channel_id=1, replica_groups=mesh['blk'=64,'rep'=2] {'blk'}, dimensions={0} | all-to-all | bytes 524288 | tf_op jit(solution)/shard_map/all_to_all | solution.py:673
  109.8 7.7 %map_two.1 = (f32[64,8,128]{2,1,0:T(8,128)S(1)}, f32[8,8,128]{2,1,0:T(8,128)S(1)}, f32[8,128]{1,0:T(8,128)S(1)}) custom-call(f32[64,8,128]{2,1,0:T(8,128)S(1)} %all_to_all.27.recv_ref, f32[64,8,128]{2,1,0:T(8,128)S(1)} %all_to_all.25.recv_ref.before_ref, f32[8,128]{1,0:T(8,128)S(1)} %get-tuple-element.53.told_ref, ...), custom_call_target="tpu_custom_call" | custom-call | tf_op jit(solution)/shard_map/map_two/pallas_call | solution.py:640
  117.5 14.1 %all_to_all.28.recv_ref = f32[64,8,128]{2,1,0:T(8,128)S(1)} all-to-all(f32[64,8,128]{2,1,0:T(8,128)S(1)} %get-tuple-element.56), channel_id=1, replica_groups=mesh['blk'=64,'rep'=2] {'blk'}, dimensions={0} | all-to-all | bytes 524288 | tf_op jit(solution)/shard_map/all_to_all | solution.py:673
  131.6 5.6 %analysis.5.mine_ref = f32[9,8,128]{2,1,0:T(8,128)S(1)} custom-call(f32[64,8,128]{2,1,0:T(8,128)S(1)} %all_to_all.28.recv_ref, f32[2,2,8,1152]{3,2,1,0:T(8,128)S(1)} %get-tuple-element.42.keep_ref, f32[2,2,8,1152]{3,2,1,0:T(8,128)S(1)} %collective-permute-done.2.other_ref, f32[8,1024]{1,0:T(8,128)S(1)} %get-tuple-element.44.x_ref, ...), custom_call_target="tpu_custom_call" | custom-call | tf_op jit(solution)/shard_map/analysis/pallas_call | solution.py:69
  137.2 3.2 %collective-permute-start.5 = (f32[9,8,128]{2,1,0:T(8,128)S(1)}, f32[9,8,128]{2,1,0:T(8,128)S(1)}, u32[]{:S(2)}, u32[]{:S(2)}) collective-permute-start(f32[9,8,128]{2,1,0:T(8,128)S(1)} %analysis.5.mine_ref), channel_id=1, source_target_pairs={{0,1},{1,0},{2,3},{3,2},{4,5},{5,4},{6,7},{7,6},{8,9},{9,8},{10,11... | collective-permute-start | bytes 110600 | tf_op jit(solution)/shard_map/ppermute | solution.py:670
  140.4 0.9 collective-permute-done.5.theirs_ref
  141.3 0.7 last.1
Async XLA Ops:
  0.7 0.7 copy-start.4
  5.2 3.8 %copy-start = (bf16[2,512,1024]{2,1,0:T(8,128)(2,1)}, bf16[2,512,1024]{2,1,0:T(8,128)(2,1)S(1)}, u32[]{:S(2)}) copy-start(bf16[2,512,1024]{2,1,0:T(8,128)(2,1)S(1)} %get-tuple-element.34.sin_ref.sin_hbm) | copy-start | bytes 6291460
  5.2 3.8 %collective-permute-start = (f32[16,16384]{1,0:T(8,128)S(1)}, f32[16,16384]{1,0:T(8,128)S(1)}, u32[]{:S(2)}, u32[]{:S(2)}) collective-permute-start(f32[16,16384]{1,0:T(8,128)S(1)} %get-tuple-element.31), channel_id=1, source_target_pairs={{0,1},{1,0},{2,3},{3,2},{4,5},{5,4},{6,7},{7,6},{8,9},{9,8},{10,11... | collective-permute-start | bytes 3145736 | tf_op jit(solution)/shard_map/ppermute | solution.py:670
  8.8 14.7 %copy-start.3 = (f32[8,2,2,2048]{3,2,1,0:T(2,128)S(1)}, f32[8,2,2,2048]{3,2,1,0:T(2,128)}, u32[]{:S(2)}) copy-start(f32[8,2,2,2048]{3,2,1,0:T(2,128)} %seeds_ref.1) | copy-start | bytes 786436
  8.8 14.7 %copy-start.5 = (s32[512,2]{0,1:T(2,128)S(1)}, s32[512,2]{0,1:T(2,128)}, u32[]{:S(2)}) copy-start(s32[512,2]{0,1:T(2,128)} %param.12) | copy-start | bytes 12292
  8.8 14.7 %copy-start.6 = (f32[8,2,2,128]{3,2,1,0:T(2,128)S(1)}, f32[8,2,2,128]{3,2,1,0:T(2,128)}, u32[]{:S(2)}) copy-start(f32[8,2,2,128]{3,2,1,0:T(2,128)} %prior_ref.1) | copy-start | bytes 49156
  8.8 14.7 %copy-start.7 = (f32[2048]{0:T(1024)S(1)}, f32[2048]{0:T(1024)}, u32[]{:S(2)}) copy-start(f32[2048]{0:T(1024)} %param.11) | copy-start | bytes 24580
  8.9 14.7 %copy-start.8 = (s32[8]{0:T(128)S(1)}, s32[8]{0:T(128)}, u32[]{:S(2)}) copy-start(s32[8]{0:T(128)} %count_ref.1) | copy-start | bytes 100
  11.9 13.3 %collective-permute-start.1 = (f32[16,16384]{1,0:T(8,128)}, f32[16,16384]{1,0:T(8,128)}, u32[]{:S(2)}, u32[]{:S(2)}) collective-permute-start(f32[16,16384]{1,0:T(8,128)} %get-tuple-element.37), channel_id=1, source_target_pairs={{0,1},{1,0},{2,3},{3,2},{4,5},{5,4},{6,7},{7,6},{8,9},{9,8},{10,11... | collective-permute-start | bytes 3145736 | tf_op jit(solution)/shard_map/ppermute | solution.py:670
  12.3 21.1 %all-to-all-start = ((f32[64,8,128]{2,1,0:T(8,128)}), f32[64,8,128]{2,1,0:T(8,128)S(1)}, u32[]{:S(2)}, u32[]{:S(2)}) async-start(f32[64,8,128]{2,1,0:T(8,128)} %sky.1), calls=%async_computation | async-start | bytes 524288 | tf_op jit(solution)/shard_map/all_to_all | solution.py:673
  24.7 8.7 %collective-permute-start.2 = (f32[2,2,8,1152]{3,2,1,0:T(8,128)S(1)}, f32[2,2,8,1152]{3,2,1,0:T(8,128)S(1)}, u32[]{:S(2)}, u32[]{:S(2)}) collective-permute-start(f32[2,2,8,1152]{3,2,1,0:T(8,128)S(1)} %get-tuple-element.43), channel_id=1, source_target_pairs={{0,1},{1,0},{2,3},{3,2},{4,5},{5,4},{6,7},{7,6},{8,9},{9,8},{10,11... | collective-permute-start | bytes 442376 | tf_op jit(solution)/shard_map/ppermute | solution.py:670
  27.3 1.0 copy-start.1
  28.2 1.0 copy-start.2
  39.0 2.4 %collective-permute-start.3 = (f32[9,8,128]{2,1,0:T(8,128)S(1)}, f32[9,8,128]{2,1,0:T(8,128)S(1)}, u32[]{:S(2)}, u32[]{:S(2)}) collective-permute-start(f32[9,8,128]{2,1,0:T(8,128)S(1)} %analysis.3.mine_ref), channel_id=1, source_target_pairs={{0,1},{1,0},{2,3},{3,2},{4,5},{5,4},{6,7},{7,6},{8,9},{9,8},{10,11... | collective-permute-start | bytes 110600 | tf_op jit(solution)/shard_map/ppermute | solution.py:670
  87.2 4.0 %collective-permute-start.4 = (f32[9,8,128]{2,1,0:T(8,128)S(1)}, f32[9,8,128]{2,1,0:T(8,128)S(1)}, u32[]{:S(2)}, u32[]{:S(2)}) collective-permute-start(f32[9,8,128]{2,1,0:T(8,128)S(1)} %analysis.4.mine_ref), channel_id=1, source_target_pairs={{0,1},{1,0},{2,3},{3,2},{4,5},{5,4},{6,7},{7,6},{8,9},{9,8},{10,11... | collective-permute-start | bytes 110600 | tf_op jit(solution)/shard_map/ppermute | solution.py:670
  137.2 4.1 %collective-permute-start.5 = (f32[9,8,128]{2,1,0:T(8,128)S(1)}, f32[9,8,128]{2,1,0:T(8,128)S(1)}, u32[]{:S(2)}, u32[]{:S(2)}) collective-permute-start(f32[9,8,128]{2,1,0:T(8,128)S(1)} %analysis.5.mine_ref), channel_id=1, source_target_pairs={{0,1},{1,0},{2,3},{3,2},{4,5},{5,4},{6,7},{7,6},{8,9},{9,8},{10,11... | collective-permute-start | bytes 110600 | tf_op jit(solution)/shard_map/ppermute | solution.py:670

commit v5 on v4

--- a/solution.py
+++ b/solution.py
@@ -416,7 +416,7 @@
     return cos, sin
 
 
-PIECES = 4
+PIECES = 1
 ANY = pl.BlockSpec(memory_space=pl.ANY)
 
 

time: 142 us -> 142 us (level)
  no operation moved by 1% of the time
where the time goes in v5:
time: 142 us
  blocking collectives  56 us (39%)
  Pallas kernels  53.9 us (38%)
  starting transfers between devices  21.5 us (15%)
  waiting for transfers between devices  6.96 us (5%)
  local copies, waits for them, and re-layouts  2.66 us (2%)
    all_to_all x4, blocking collectives, transpose(): lax.all_to_all(payload, 'blk', split_axis=0, concat_axis=0, tiled=True)  56 us
    pallas_call x9, Pallas kernels, call(): pl.pallas_call(kernel, in_specs=[SMEM] * scalars + [VMEM] * (len(arrays)...  32.9 us
    pallas_call x2, Pallas kernels, map_call(): pl.pallas_call(kernel, in_specs=[VMEM] * len(arrays) + [ANY] * 3, out_spe...  15.2 us
    all_to_all x1, starting transfers between devices, transpose(): lax.all_to_all(payload, 'blk', split_axis=0, concat_axis=0, tiled=True)  11.2 us
    ppermute x6, starting transfers between devices, swap(): return lax.ppermute(value, 'rep', [(0, 1), (1, 0)])  10.3 us
    all_to_all x1, waiting for transfers between devices, transpose(): lax.all_to_all(payload, 'blk', split_axis=0, concat_axis=0, tiled=True)  4.18 us
    pallas_call x1, Pallas kernels, tables(): pl.pallas_call(table_kernel, in_specs=[SMEM, ANY, ANY, VMEM], out_specs=(...  3.76 us
  transfers between devices with their start and end apart: 7, of which 5 were waited for; matrix products, arithmetic and copies ran while one was open for 0% of the time, Pallas kernels for 4%

profile of v5, /device:TPU:1, one launch (start us, length us, event | category | flops | bytes accessed | tf_op | source)
XLA Modules:
  0.0 141.9 jit_solution(9241623983141364835)
XLA Ops:
  0.6 0.1 pad_add_fusion.place_ref
  0.7 0.0 copy-start.4
  0.7 0.7 copy-done.4
  1.4 3.8 %tables.1 = (f32[16,16384]{1,0:T(8,128)}, f32[16,16384]{1,0:T(8,128)S(1)}, f32[16,16384]{1,0:T(8,128)S(1)}, bf16[2,512,1024]{2,1,0:T(8,128)(2,1)S(1)}, bf16[2,51...) custom-call(s32[2]{0:T(128)S(1)} %pad_add_fusion.place_ref, f32[32,16384]{1,0:T(8,128)} %noise_ref.1, ...), custom_call_target="tpu_custom_call" | custom-call | tf_op jit(solution)/shard_map/tables/pallas_call | solution.py:472
  5.2 0.0 copy-start
  5.2 1.5 %collective-permute-start = (f32[16,16384]{1,0:T(8,128)S(1)}, f32[16,16384]{1,0:T(8,128)S(1)}, u32[]{:S(2)}, u32[]{:S(2)}) collective-permute-start(f32[16,16384]{1,0:T(8,128)S(1)} %get-tuple-element.31), channel_id=1, source_target_pairs={{0,1},{1,0},{2,3},{3,2},{4,5},{5,4},{6,7},{7,6},{8,9},{9,8},{10,11... | collective-permute-start | bytes 3145736 | tf_op jit(solution)/shard_map/ppermute | solution.py:670
  6.7 2.0 %own.1.sums_ref = f32[2,16,1024]{2,1,0:T(8,128)S(1)} custom-call(f32[16,16384]{1,0:T(8,128)S(1)} %get-tuple-element.32.mine_ref, bf16[2,512,1024]{2,1,0:T(8,128)(2,1)S(1)} %get-tuple-element.33.cos_ref, bf16[2,512,1024]{2,1,0:T(8,128)(2,1)S(1)} %get-tuple-element.34.sin_ref.sin_hbm, f32[2,32,1024]{2,1,0:T(8,128)S(1)} %get-tuple-element.35.phase_ref), custom_call_target="tpu_custom_call" | custom-call | tf_op jit(solution)/shard_map/own/pallas_call | solution.py:69
  8.7 0.0 copy-start.3
  8.7 0.0 copy-start.5
  8.7 0.0 copy-start.6
  8.8 0.0 copy-start.7
  8.8 0.0 copy-start.8
  8.8 0.2 collective-permute-done.heavy_ref
  9.0 0.0 copy-done
  9.0 2.9 %sky.1 = f32[64,8,128]{2,1,0:T(8,128)} custom-call(f32[16,16384]{1,0:T(8,128)S(1)} %collective-permute-done.heavy_ref, f32[2,16,1024]{2,1,0:T(8,128)S(1)} %own.1.sums_ref, bf16[2,512,1024]{2,1,0:T(8,128)(2,1)S(1)} %get-tuple-element.33.cos_ref, bf16[2,512,1024]{2,1,0:T(8,128)(2,1)S(1)} %get-tuple-element.34.sin_ref.sin_hbm, ...), custom_call_target="tpu_custom_call" | custom-call | tf_op jit(solution)/shard_map/sky/pallas_call | solution.py:69
  11.8 0.4 collective-permute-start.1
  12.2 11.2 %all-to-all-start = ((f32[64,8,128]{2,1,0:T(8,128)}), f32[64,8,128]{2,1,0:T(8,128)S(1)}, u32[]{:S(2)}, u32[]{:S(2)}) async-start(f32[64,8,128]{2,1,0:T(8,128)} %sky.1), calls=%async_computation | async-start | bytes 524288 | tf_op jit(solution)/shard_map/all_to_all | solution.py:673
  23.4 0.0 copy-done.3
  23.4 0.0 copy-done.5
  23.4 0.0 copy-done.6
  23.5 0.0 copy-done.7
  23.5 0.0 copy-done.8
  23.5 1.2 prepare.1
  24.6 0.5 collective-permute-start.2
  25.1 0.0 collective-permute-done.1.other_ref
  25.1 2.0 %noise.1 = (f32[512,512]{1,0:T(8,128)S(1)}, f32[512,512]{1,0:T(8,128)S(1)}) custom-call(s32[1]{0:T(128)} %bitcast.1.rep_ref, f32[32,16384]{1,0:T(8,128)} %noise_ref.1, f32[16,16384]{1,0:T(8,128)} %collective-permute-done.1.other_ref), custom_call_target="tpu_custom_call" | custom-call | tf_op jit(solution)/shard_map/noise/pallas_call | solution.py:533
  27.2 0.0 copy-start.1
  27.2 1.0 copy-done.1
  28.2 0.0 copy-start.2
  28.2 1.0 copy-done.2
  29.1 4.2 %all-to-all-done.recv_ref = f32[64,8,128]{2,1,0:T(8,128)S(1)} async-done(((f32[64,8,128]{2,1,0:T(8,128)}), f32[64,8,128]{2,1,0:T(8,128)S(1)}, u32[]{:S(2)}, u32[]{:S(2)}) %all-to-all-start) | async-done | bytes 262176 | tf_op jit(solution)/shard_map/all_to_all | solution.py:673
  33.3 0.0 collective-permute-done.2.other_ref
  33.3 5.6 %analysis.3.mine_ref = f32[9,8,128]{2,1,0:T(8,128)S(1)} custom-call(f32[64,8,128]{2,1,0:T(8,128)S(1)} %all-to-all-done.recv_ref, f32[2,2,8,1152]{3,2,1,0:T(8,128)S(1)} %get-tuple-element.42.keep_ref, f32[2,2,8,1152]{3,2,1,0:T(8,128)S(1)} %collective-permute-done.2.other_ref, f32[8,1024]{1,0:T(8,128)S(1)} %get-tuple-element.44.x_ref, ...), custom_call_target="tpu_custom_call" | custom-call | tf_op jit(solution)/shard_map/analysis/pallas_call | solution.py:69
  39.0 1.5 %collective-permute-start.3 = (f32[9,8,128]{2,1,0:T(8,128)S(1)}, f32[9,8,128]{2,1,0:T(8,128)S(1)}, u32[]{:S(2)}, u32[]{:S(2)}) collective-permute-start(f32[9,8,128]{2,1,0:T(8,128)S(1)} %analysis.3.mine_ref), channel_id=1, source_target_pairs={{0,1},{1,0},{2,3},{3,2},{4,5},{5,4},{6,7},{7,6},{8,9},{9,8},{10,11... | collective-permute-start | bytes 110600 | tf_op jit(solution)/shard_map/ppermute | solution.py:670
  40.5 0.9 collective-permute-done.3.theirs_ref
  41.4 4.5 %first.1 = (f32[64,8,128]{2,1,0:T(8,128)S(1)}, f32[8,8,128]{2,1,0:T(8,128)S(1)}) custom-call(f32[9,8,128]{2,1,0:T(8,128)S(1)} %analysis.3.mine_ref, f32[9,8,128]{2,1,0:T(8,128)S(1)} %collective-permute-done.3.theirs_ref, f32[2,2,8,1152]{3,2,1,0:T(8,128)S(1)} %get-tuple-element.42.keep_ref, f32[2,2,8,1152]{3,2,1,0:T(8,128)S(1)} %collective-permute-done.2.other_ref, ...), custom_call_target="tpu_custom_call" | custom-call | tf_op jit(solution)/shard_map/first/pallas_call | solution.py:69
  45.9 14.0 %all_to_all.25.recv_ref.before_ref = f32[64,8,128]{2,1,0:T(8,128)S(1)} all-to-all(f32[64,8,128]{2,1,0:T(8,128)S(1)} %get-tuple-element.48), channel_id=1, replica_groups=mesh['blk'=64,'rep'=2] {'blk'}, dimensions={0} | all-to-all | bytes 524288 | tf_op jit(solution)/shard_map/all_to_all | solution.py:673
  59.9 7.5 %map_one.1 = (f32[64,8,128]{2,1,0:T(8,128)S(1)}, f32[8,128]{1,0:T(8,128)S(1)}) custom-call(f32[64,8,128]{2,1,0:T(8,128)S(1)} %all_to_all.25.recv_ref.before_ref, f32[2,32,1024]{2,1,0:T(8,128)S(1)} %get-tuple-element.35.phase_ref, bf16[2,512,1024]{2,1,0:T(8,128)(2,1)S(1)} %get-tuple-element.33.cos_ref, bf16[2,512,1024]{2,1,0:T(8,128)(2,1)} %copy-done, ...), custom_call_target="tpu_custom_call" | custom-call | tf_op jit(solution)/shard_map/map_one/pallas_call | solution.py:640
  67.4 14.1 %all_to_all.26.recv_ref = f32[64,8,128]{2,1,0:T(8,128)S(1)} all-to-all(f32[64,8,128]{2,1,0:T(8,128)S(1)} %get-tuple-element.51), channel_id=1, replica_groups=mesh['blk'=64,'rep'=2] {'blk'}, dimensions={0} | all-to-all | bytes 524288 | tf_op jit(solution)/shard_map/all_to_all | solution.py:673
  81.5 5.6 %analysis.4.mine_ref = f32[9,8,128]{2,1,0:T(8,128)S(1)} custom-call(f32[64,8,128]{2,1,0:T(8,128)S(1)} %all_to_all.26.recv_ref, f32[2,2,8,1152]{3,2,1,0:T(8,128)S(1)} %get-tuple-element.42.keep_ref, f32[2,2,8,1152]{3,2,1,0:T(8,128)S(1)} %collective-permute-done.2.other_ref, f32[8,1024]{1,0:T(8,128)S(1)} %get-tuple-element.44.x_ref, ...), custom_call_target="tpu_custom_call" | custom-call | tf_op jit(solution)/shard_map/analysis/pallas_call | solution.py:69
  87.2 3.2 %collective-permute-start.4 = (f32[9,8,128]{2,1,0:T(8,128)S(1)}, f32[9,8,128]{2,1,0:T(8,128)S(1)}, u32[]{:S(2)}, u32[]{:S(2)}) collective-permute-start(f32[9,8,128]{2,1,0:T(8,128)S(1)} %analysis.4.mine_ref), channel_id=1, source_target_pairs={{0,1},{1,0},{2,3},{3,2},{4,5},{5,4},{6,7},{7,6},{8,9},{9,8},{10,11... | collective-permute-start | bytes 110600 | tf_op jit(solution)/shard_map/ppermute | solution.py:670
  90.3 0.9 collective-permute-done.4.theirs_ref
  91.2 4.6 %second.1 = (f32[64,8,128]{2,1,0:T(8,128)S(1)}, f32[8,8,128]{2,1,0:T(8,128)S(1)}, f32[8,128]{1,0:T(8,128)S(1)}) custom-call(f32[9,8,128]{2,1,0:T(8,128)S(1)} %analysis.4.mine_ref, f32[9,8,128]{2,1,0:T(8,128)S(1)} %collective-permute-done.4.theirs_ref, f32[8,8,128]{2,1,0:T(8,128)S(1)} %get-tuple-element.52.rhs_ref, f32[8,128]{1,0:T(8,128)S(1)} %get-tuple-element.53.told_ref, ...), custom_call_target="tpu_custom_call" | custom-call | tf_op jit(solution)/shard_map/second/pallas_call | solution.py:69
  95.8 13.9 %all_to_all.27.recv_ref = f32[64,8,128]{2,1,0:T(8,128)S(1)} all-to-all(f32[64,8,128]{2,1,0:T(8,128)S(1)} %get-tuple-element.54), channel_id=1, replica_groups=mesh['blk'=64,'rep'=2] {'blk'}, dimensions={0} | all-to-all | bytes 524288 | tf_op jit(solution)/shard_map/all_to_all | solution.py:673
  109.7 7.7 %map_two.1 = (f32[64,8,128]{2,1,0:T(8,128)S(1)}, f32[8,8,128]{2,1,0:T(8,128)S(1)}, f32[8,128]{1,0:T(8,128)S(1)}) custom-call(f32[64,8,128]{2,1,0:T(8,128)S(1)} %all_to_all.27.recv_ref, f32[64,8,128]{2,1,0:T(8,128)S(1)} %all_to_all.25.recv_ref.before_ref, f32[8,128]{1,0:T(8,128)S(1)} %get-tuple-element.53.told_ref, ...), custom_call_target="tpu_custom_call" | custom-call | tf_op jit(solution)/shard_map/map_two/pallas_call | solution.py:640
  117.4 14.1 %all_to_all.28.recv_ref = f32[64,8,128]{2,1,0:T(8,128)S(1)} all-to-all(f32[64,8,128]{2,1,0:T(8,128)S(1)} %get-tuple-element.56), channel_id=1, replica_groups=mesh['blk'=64,'rep'=2] {'blk'}, dimensions={0} | all-to-all | bytes 524288 | tf_op jit(solution)/shard_map/all_to_all | solution.py:673
  131.5 5.6 %analysis.5.mine_ref = f32[9,8,128]{2,1,0:T(8,128)S(1)} custom-call(f32[64,8,128]{2,1,0:T(8,128)S(1)} %all_to_all.28.recv_ref, f32[2,2,8,1152]{3,2,1,0:T(8,128)S(1)} %get-tuple-element.42.keep_ref, f32[2,2,8,1152]{3,2,1,0:T(8,128)S(1)} %collective-permute-done.2.other_ref, f32[8,1024]{1,0:T(8,128)S(1)} %get-tuple-element.44.x_ref, ...), custom_call_target="tpu_custom_call" | custom-call | tf_op jit(solution)/shard_map/analysis/pallas_call | solution.py:69
  137.1 3.2 %collective-permute-start.5 = (f32[9,8,128]{2,1,0:T(8,128)S(1)}, f32[9,8,128]{2,1,0:T(8,128)S(1)}, u32[]{:S(2)}, u32[]{:S(2)}) collective-permute-start(f32[9,8,128]{2,1,0:T(8,128)S(1)} %analysis.5.mine_ref), channel_id=1, source_target_pairs={{0,1},{1,0},{2,3},{3,2},{4,5},{5,4},{6,7},{7,6},{8,9},{9,8},{10,11... | collective-permute-start | bytes 110600 | tf_op jit(solution)/shard_map/ppermute | solution.py:670
  140.3 0.9 collective-permute-done.5.theirs_ref
  141.2 0.7 last.1
Async XLA Ops:
  0.7 0.7 copy-start.4
  5.2 3.8 %copy-start = (bf16[2,512,1024]{2,1,0:T(8,128)(2,1)}, bf16[2,512,1024]{2,1,0:T(8,128)(2,1)S(1)}, u32[]{:S(2)}) copy-start(bf16[2,512,1024]{2,1,0:T(8,128)(2,1)S(1)} %get-tuple-element.34.sin_ref.sin_hbm) | copy-start | bytes 6291460
  5.2 3.8 %collective-permute-start = (f32[16,16384]{1,0:T(8,128)S(1)}, f32[16,16384]{1,0:T(8,128)S(1)}, u32[]{:S(2)}, u32[]{:S(2)}) collective-permute-start(f32[16,16384]{1,0:T(8,128)S(1)} %get-tuple-element.31), channel_id=1, source_target_pairs={{0,1},{1,0},{2,3},{3,2},{4,5},{5,4},{6,7},{7,6},{8,9},{9,8},{10,11... | collective-permute-start | bytes 3145736 | tf_op jit(solution)/shard_map/ppermute | solution.py:670
  8.7 14.7 %copy-start.3 = (f32[8,2,2,2048]{3,2,1,0:T(2,128)S(1)}, f32[8,2,2,2048]{3,2,1,0:T(2,128)}, u32[]{:S(2)}) copy-start(f32[8,2,2,2048]{3,2,1,0:T(2,128)} %seeds_ref.1) | copy-start | bytes 786436
  8.7 14.7 %copy-start.5 = (s32[512,2]{0,1:T(2,128)S(1)}, s32[512,2]{0,1:T(2,128)}, u32[]{:S(2)}) copy-start(s32[512,2]{0,1:T(2,128)} %param.12) | copy-start | bytes 12292
  8.7 14.7 %copy-start.6 = (f32[8,2,2,128]{3,2,1,0:T(2,128)S(1)}, f32[8,2,2,128]{3,2,1,0:T(2,128)}, u32[]{:S(2)}) copy-start(f32[8,2,2,128]{3,2,1,0:T(2,128)} %prior_ref.1) | copy-start | bytes 49156
  8.8 14.7 %copy-start.7 = (f32[2048]{0:T(1024)S(1)}, f32[2048]{0:T(1024)}, u32[]{:S(2)}) copy-start(f32[2048]{0:T(1024)} %param.11) | copy-start | bytes 24580
  8.8 14.7 %copy-start.8 = (s32[8]{0:T(128)S(1)}, s32[8]{0:T(128)}, u32[]{:S(2)}) copy-start(s32[8]{0:T(128)} %count_ref.1) | copy-start | bytes 100
  11.8 13.3 %collective-permute-start.1 = (f32[16,16384]{1,0:T(8,128)}, f32[16,16384]{1,0:T(8,128)}, u32[]{:S(2)}, u32[]{:S(2)}) collective-permute-start(f32[16,16384]{1,0:T(8,128)} %get-tuple-element.37), channel_id=1, source_target_pairs={{0,1},{1,0},{2,3},{3,2},{4,5},{5,4},{6,7},{7,6},{8,9},{9,8},{10,11... | collective-permute-start | bytes 3145736 | tf_op jit(solution)/shard_map/ppermute | solution.py:670
  12.2 21.1 %all-to-all-start = ((f32[64,8,128]{2,1,0:T(8,128)}), f32[64,8,128]{2,1,0:T(8,128)S(1)}, u32[]{:S(2)}, u32[]{:S(2)}) async-start(f32[64,8,128]{2,1,0:T(8,128)} %sky.1), calls=%async_computation | async-start | bytes 524288 | tf_op jit(solution)/shard_map/all_to_all | solution.py:673
  24.6 8.7 %collective-permute-start.2 = (f32[2,2,8,1152]{3,2,1,0:T(8,128)S(1)}, f32[2,2,8,1152]{3,2,1,0:T(8,128)S(1)}, u32[]{:S(2)}, u32[]{:S(2)}) collective-permute-start(f32[2,2,8,1152]{3,2,1,0:T(8,128)S(1)} %get-tuple-element.43), channel_id=1, source_target_pairs={{0,1},{1,0},{2,3},{3,2},{4,5},{5,4},{6,7},{7,6},{8,9},{9,8},{10,11... | collective-permute-start | bytes 442376 | tf_op jit(solution)/shard_map/ppermute | solution.py:670
  27.2 1.0 copy-start.1
  28.2 1.0 copy-start.2
  39.0 2.4 %collective-permute-start.3 = (f32[9,8,128]{2,1,0:T(8,128)S(1)}, f32[9,8,128]{2,1,0:T(8,128)S(1)}, u32[]{:S(2)}, u32[]{:S(2)}) collective-permute-start(f32[9,8,128]{2,1,0:T(8,128)S(1)} %analysis.3.mine_ref), channel_id=1, source_target_pairs={{0,1},{1,0},{2,3},{3,2},{4,5},{5,4},{6,7},{7,6},{8,9},{9,8},{10,11... | collective-permute-start | bytes 110600 | tf_op jit(solution)/shard_map/ppermute | solution.py:670
  87.2 4.0 %collective-permute-start.4 = (f32[9,8,128]{2,1,0:T(8,128)S(1)}, f32[9,8,128]{2,1,0:T(8,128)S(1)}, u32[]{:S(2)}, u32[]{:S(2)}) collective-permute-start(f32[9,8,128]{2,1,0:T(8,128)S(1)} %analysis.4.mine_ref), channel_id=1, source_target_pairs={{0,1},{1,0},{2,3},{3,2},{4,5},{5,4},{6,7},{7,6},{8,9},{9,8},{10,11... | collective-permute-start | bytes 110600 | tf_op jit(solution)/shard_map/ppermute | solution.py:670
  137.1 4.1 %collective-permute-start.5 = (f32[9,8,128]{2,1,0:T(8,128)S(1)}, f32[9,8,128]{2,1,0:T(8,128)S(1)}, u32[]{:S(2)}, u32[]{:S(2)}) collective-permute-start(f32[9,8,128]{2,1,0:T(8,128)S(1)} %analysis.5.mine_ref), channel_id=1, source_target_pairs={{0,1},{1,0},{2,3},{3,2},{4,5},{5,4},{6,7},{7,6},{8,9},{9,8},{10,11... | collective-permute-start | bytes 110600 | tf_op jit(solution)/shard_map/ppermute | solution.py:670
